TPU v7x, 32 devices: a whole 2x2x4 slice. The times are simulated.
32 devices in a mesh: grp: 2 (over x), blk: 16 (over z, y, core).
Axes of the slice: x: 2, y: 2, z: 4, core: 2. Of those that a mesh axis runs over, the one named last changes fastest.
Arguments:
- integrals: bfloat16 [32, 16, 3, 4096], P(('grp', 'blk')), parts along dimension 0, may hold values from -6 to 6
- occupied: bfloat16 [32, 3, 4096], P(('grp', 'blk')), parts along dimension 0, may hold values from -0.5 to 0.5
- virtual: bfloat16 [32, 3, 4096], P(('grp', 'blk')), parts along dimension 0, may hold values from -0.5 to 0.5
- integral_block_mask: int32 [16, 3], replicated, may hold values 0 or 1
- occupied_block_mask: int32 [16, 3], replicated, may hold values 0 or 1
- virtual_block_mask: int32 [16, 3], replicated, may hold values 0 or 1
- block_orbital_count: int32 [16], replicated, may hold values from 32 to 64
Outputs:
- polarizability: float32 [32, 16], P(('grp', 'blk')), parts along dimension 0
There are 2 independent parts, one for each index of `grp`. A program takes and returns all parts, laid end to end along the dimension named above; an argument that names none is the same for every part. Nothing has to cross between parts.
All inputs are finite; a program needn't handle non-finite values.
Results may differ from a plain program's by a relative error of at most 0.0037.
Values may be sent and summed in bfloat16 or wider, within the bound.
No kernel may reach another device: no remote copies, remote signals or barrier semaphores. Data moves between devices by JAX's collectives and lax.ppermute only.
A program may use at most 64 MiB of HBM per device.

v0:
```python
import math

import jax
import jax.numpy as jnp
from jax import lax
from jax.sharding import PartitionSpec as P

PADDED_ORBITALS = 64


def cyclic_boundary(array, margin, axis_pos):
    length = array.shape[axis_pos]
    front = lax.slice_in_dim(array, length - margin, length, axis=axis_pos)
    back = lax.slice_in_dim(array, 0, margin, axis=axis_pos)
    return jnp.concatenate([front, array, back], axis_pos)


def block_windows(
    integral_block_mask, occupied_block_mask, virtual_block_mask, block_orbital_count
):
    integral_mask_input = cyclic_boundary(integral_block_mask, 1, 0)
    occupied_mask_input = cyclic_boundary(occupied_block_mask, 1, 0)
    virtual_mask_input = cyclic_boundary(virtual_block_mask, 1, 0)
    block_count_input = cyclic_boundary(block_orbital_count, 2, 0)
    return (integral_mask_input, occupied_mask_input, virtual_mask_input, block_count_input)


def pairwise_terms(
    screening_input,
    occupied_input,
    virtual_input,
    integral_mask_input,
    occupied_mask_input,
    virtual_mask_input,
    block_count_input,
    target_blocks,
    window_border,
):
    aux_rows = screening_input.shape[0]
    window_extent = target_blocks + 2
    lane_index = jnp.arange(window_border, dtype=jnp.int32)
    usable = (lane_index[None, :] < block_count_input[:, None]).astype(jnp.bfloat16)
    row_part = usable[1 : window_extent + 1]
    col_part = jnp.stack(
        [usable[shift_val : shift_val + window_extent] for shift_val in range(3)], 1
    )
    factor = (
        integral_mask_input.astype(jnp.bfloat16)[:, :, None, None]
        * row_part[:, None, :, None]
        * col_part[:, :, None, :]
    )
    screened = (
        screening_input.reshape(aux_rows, window_extent, 3, window_border, window_border)
        * factor[None]
    )
    occ_blocks = (
        occupied_input.reshape(window_extent, 3, window_border, window_border)
        * occupied_mask_input.astype(jnp.bfloat16)[:, :, None, None]
    )
    virtual_block_list = (
        virtual_input.reshape(window_extent, 3, window_border, window_border)
        * virtual_mask_input.astype(jnp.bfloat16)[:, :, None, None]
    )
    forward_list = []
    backward_list = []
    for offset in range(5):
        forward_terms = []
        backward_terms = []
        for source in range(3):
            first_idx = 2 - source
            second_idx = first_idx + offset - 2
            if 0 <= second_idx <= 2:
                forward_terms.append(
                    jnp.einsum(
                        "stml,tmn->stln",
                        screened[:, source : source + target_blocks, first_idx],
                        occ_blocks[source : source + target_blocks, second_idx],
                        preferred_element_type=jnp.float32,
                    )
                )
                backward_terms.append(
                    jnp.einsum(
                        "tml,stmn->stln",
                        virtual_block_list[source : source + target_blocks, first_idx],
                        screened[:, source : source + target_blocks, second_idx],
                        preferred_element_type=jnp.float32,
                    )
                )
        forward_window = forward_terms[0]
        backward_window = backward_terms[0]
        for extra in range(1, len(forward_terms)):
            forward_window = forward_window + forward_terms[extra]
            backward_window = backward_window + backward_terms[extra]
        forward_list.append(
            forward_window.astype(jnp.bfloat16).reshape(
                aux_rows, target_blocks, window_border * window_border
            )
        )
        backward_list.append(
            backward_window.astype(jnp.bfloat16).reshape(
                aux_rows, target_blocks, window_border * window_border
            )
        )
    return (jnp.stack(forward_list, 2), jnp.stack(backward_list, 2))


def body(
    integrals,
    occupied,
    virtual,
    integral_block_mask,
    occupied_block_mask,
    virtual_block_mask,
    block_orbital_count,
):
    total_blocks = integrals.shape[1]
    aux_local = integrals.shape[0]
    greens = jnp.stack([occupied, virtual], 0)
    everyone = lax.all_gather(greens, "blk", axis=1, tiled=True)
    wrapped = cyclic_boundary(everyone, 1, 1)
    integral_mask_input, occupied_mask_input, virtual_mask_input, block_count_input = block_windows(
        integral_block_mask, occupied_block_mask, virtual_block_mask, block_orbital_count
    )
    forward_aux, backward_aux = pairwise_terms(
        cyclic_boundary(integrals, 1, 1),
        wrapped[0],
        wrapped[1],
        integral_mask_input,
        occupied_mask_input,
        virtual_mask_input,
        block_count_input,
        total_blocks,
        PADDED_ORBITALS,
    )
    forward_window, backward_window = (
        lax.all_to_all(forward_aux, "blk", split_axis=1, concat_axis=0, tiled=True),
        lax.all_to_all(backward_aux, "blk", split_axis=1, concat_axis=0, tiled=True),
    )
    flat_fwd = forward_window.reshape(forward_window.shape[0], -1)
    flat_bwd = backward_window.reshape(backward_window.shape[0], -1)
    partial_sum = lax.dot_general(
        flat_fwd, flat_bwd, (((1,), (1,)), ((), ())), preferred_element_type=jnp.float32
    )
    summed = lax.psum(partial_sum, "blk")
    my_rows = lax.dynamic_slice_in_dim(summed, lax.axis_index("blk") * aux_local, aux_local, 0)
    return my_rows * jnp.float32(
        1.0 / math.sqrt(5 * PADDED_ORBITALS * PADDED_ORBITALS * total_blocks)
    )


def solution(mesh):
    return jax.shard_map(
        body,
        mesh=mesh,
        in_specs=(
            P(("grp", "blk"), None, None, None),
            P(("grp", "blk"), None, None),
            P(("grp", "blk"), None, None),
            P(),
            P(),
            P(),
            P(),
        ),
        out_specs=P(("grp", "blk"), None),
        check_vma=False,
    )
```

profile of v0, /device:TPU:0, one launch (start us, length us, event | category | flops | bytes accessed | tf_op | source)
XLA Modules:
  0.0 145.2 jit_solution(15581446147846247371)
XLA Ops:
  0.0 1.1 fusion.29
  1.2 1.2 pad_maximum_fusion.1
  2.4 0.9 reshape.199
  3.8 26.2 %all_gather.3 = bf16[2,16,3,4096]{3,2,1,0:T(4,128)(2,1)S(1)} all-gather(bf16[2,1,3,4096]{3,2,1,0:T(4,128)(2,1)S(1)} %pad_maximum_fusion.2), channel_id=1, replica_groups=mesh['grp'=2,'blk'=16] {'blk'}, dimensions={1}, use_global_device_ids=true | all-gather | bytes 835584 | tf_op jit(solution)/shard_map/all_gather | solution.py:119
  30.0 0.9 pad_maximum_fusion
  31.7 0.9 reshape_squeeze.7
  33.9 1.1 fusion.21
  35.3 1.1 fusion.20
  36.7 0.8 copy.51
  37.5 1.2 stack_reshape.35
  38.7 0.7 constant_dynamic-update-slice_fusion.9
  39.4 1.3 fusion.8
  40.7 0.9 copy.54
  41.6 1.9 %stack_reshape.36 = bf16[1,16,1,4096]{3,1,2,0:T(8,128)(2,1)} reshape(bf16[1,16,64,64]{3,2,1,0:T(8,128)(2,1)} %copy.54) | data formatting | bytes 262144 | tf_op jit(solution)/shard_map/stack;reshape | solution.py:104
  44.0 0.9 copy.58
  44.9 1.9 %stack_reshape.37 = bf16[1,16,1,4096]{3,1,2,0:T(8,128)(2,1)} reshape(bf16[1,16,64,64]{3,2,1,0:T(8,128)(2,1)} %copy.58) | data formatting | bytes 262144 | tf_op jit(solution)/shard_map/stack;reshape | solution.py:104
  48.2 1.3 copy.64
  49.6 4.5 %all-to-all-start.1 = ((bf16[1,16,5,4096]{3,2,0,1:T(8,128)(2,1)}), bf16[1,16,5,4096]{3,2,0,1:T(8,128)(2,1)}, u32[]{:S(2)}, u32[]{:S(2)}) async-start(bf16[1,16,5,4096]{3,2,0,1:T(8,128)(2,1)} %copy.64), calls=%async_computation.1 | async-start | bytes 2097152 | tf_op jit(solution)/shard_map/all_to_all | solution.py:137
  54.1 0.7 reshape.212
  55.8 0.9 fusion.12
  57.4 0.9 fusion.13
  58.3 1.8 %copy.42 = bf16[1,16,64,64]{3,2,1,0:T(8,128)(2,1)} copy(bf16[1,16,64,64]{2,3,1,0:T(8,128)(2,1)} %fusion.12) | data formatting | bytes 262144 | tf_op jit(solution)/shard_map/convert_element_type | solution.py:95
  60.1 1.2 stack_reshape.30
  61.3 0.7 constant_dynamic-update-slice_fusion.4
  62.0 0.9 fusion.11
  62.9 1.1 copy.43
  66.7 1.4 copy.47
  68.1 8.8 %all-to-all-done.1 = bf16[1,16,5,4096]{3,2,0,1:T(8,128)(2,1)} async-done(((bf16[1,16,5,4096]{3,2,0,1:T(8,128)(2,1)}), bf16[1,16,5,4096]{3,2,0,1:T(8,128)(2,1)}, u32[]{:S(2)}, u32[]{:S(2)}) %all-to-all-start.1) | async-done | bytes 655392 | tf_op jit(solution)/shard_map/all_to_all | solution.py:137
  76.9 6.8 %all-to-all-start = ((bf16[1,16,5,4096]{3,2,0,1:T(8,128)(2,1)}), bf16[1,16,5,4096]{3,2,0,1:T(8,128)(2,1)S(1)}, u32[]{:S(2)}, u32[]{:S(2)}) async-start(bf16[1,16,5,4096]{3,2,0,1:T(8,128)(2,1)} %copy.47), calls=%async_computation | async-start | bytes 2097152 | tf_op jit(solution)/shard_map/all_to_all | solution.py:136
  83.7 22.9 %all-to-all-done = bf16[1,16,5,4096]{3,2,0,1:T(8,128)(2,1)S(1)} async-done(((bf16[1,16,5,4096]{3,2,0,1:T(8,128)(2,1)}), bf16[1,16,5,4096]{3,2,0,1:T(8,128)(2,1)S(1)}, u32[]{:S(2)}, u32[]{:S(2)}) %all-to-all-start) | async-done | bytes 655392 | tf_op jit(solution)/shard_map/all_to_all | solution.py:136
  106.6 2.7 %convolution_bitcast_fusion = f32[16,16]{1,0:T(8,128)S(1)} fusion(bf16[1,16,5,4096]{3,2,0,1:T(8,128)(2,1)} %all-to-all-done.1, bf16[1,16,5,4096]{3,2,0,1:T(8,128)(2,1)S(1)} %all-to-all-done), kind=kOutput, calls=%fused_computation.29 | convolution fusion | flops 10485760 | bytes 1311744 | tf_op jit(solution)/shard_map/dot_general | solution.py:141
  109.3 35.4 %psum.7 = f32[16,16]{1,0:T(8,128)S(1)} all-reduce(f32[16,16]{1,0:T(8,128)S(1)} %convolution_bitcast_fusion), channel_id=1, replica_groups=mesh['grp'=2,'blk'=16] {'blk'}, use_global_device_ids=true, to_apply=%region_0.0 | all-reduce | flops 256 | bytes 2048 | tf_op jit(solution)/shard_map/psum | solution.py:144
  (78 shorter events, 9.6 us)
Async XLA Ops:
  1.1 2.2 %copy-start.8 = (s32[16]{0:T(128)S(1)}, s32[16]{0:T(128)}, u32[]{:S(2)}) copy-start(s32[16]{0:T(128)} %param.13) | copy-start | bytes 196
  1.1 2.5 %copy-start.9 = (s32[16,3]{0,1:T(4,128)S(1)}, s32[16,3]{0,1:T(4,128)}, u32[]{:S(2)}) copy-start(s32[16,3]{0,1:T(4,128)} %param.10) | copy-start | bytes 580
  1.1 2.6 %copy-start.6 = (bf16[1,3,4096]{2,1,0:T(4,128)(2,1)S(1)}, bf16[1,3,4096]{2,1,0:T(4,128)(2,1)}, u32[]{:S(2)}) copy-start(bf16[1,3,4096]{2,1,0:T(4,128)(2,1)} %param.9) | copy-start | bytes 73732
  1.1 2.6 %copy-start.7 = (bf16[1,3,4096]{2,1,0:T(4,128)(2,1)S(1)}, bf16[1,3,4096]{2,1,0:T(4,128)(2,1)}, u32[]{:S(2)}) copy-start(bf16[1,3,4096]{2,1,0:T(4,128)(2,1)} %param.8) | copy-start | bytes 73732
  31.4 1.3 copy-start.10
  43.7 3.0 %copy-start = (f32[16,64,64]{2,1,0:T(8,128)S(1)}, f32[16,64,64]{2,1,0:T(8,128)}, u32[]{:S(2)}) copy-start(f32[16,64,64]{2,1,0:T(8,128)} %fusion.20) | copy-start | bytes 786436
  47.0 1.1 copy-start.3
  47.1 1.1 copy-start.4
  47.1 1.1 copy-start.5
  49.6 27.3 %all-to-all-start.1 = ((bf16[1,16,5,4096]{3,2,0,1:T(8,128)(2,1)}), bf16[1,16,5,4096]{3,2,0,1:T(8,128)(2,1)}, u32[]{:S(2)}, u32[]{:S(2)}) async-start(bf16[1,16,5,4096]{3,2,0,1:T(8,128)(2,1)} %copy.64), calls=%async_computation.1 | async-start | bytes 2097152 | tf_op jit(solution)/shard_map/all_to_all | solution.py:137
  54.8 0.7 copy-start.11
  65.2 1.0 copy-start.1
  65.4 1.2 copy-start.2
  76.9 29.8 %all-to-all-start = ((bf16[1,16,5,4096]{3,2,0,1:T(8,128)(2,1)}), bf16[1,16,5,4096]{3,2,0,1:T(8,128)(2,1)S(1)}, u32[]{:S(2)}, u32[]{:S(2)}) async-start(bf16[1,16,5,4096]{3,2,0,1:T(8,128)(2,1)} %copy.47), calls=%async_computation | async-start | bytes 2097152 | tf_op jit(solution)/shard_map/all_to_all | solution.py:136
where the time goes:
time: 146 us; the launch traced here: 145 us
  blocking collectives  61.6 us (42%)
  waiting for transfers between devices  31.8 us (22%)
  local copies, waits for them, and re-layouts  24.3 us (17%)
  matrix products  11.8 us (8%)
  starting transfers between devices  11.3 us (8%)
  other arithmetic  3.95 us (3%)
    psum x1, blocking collectives, body(): summed = lax.psum(partial_sum, 'blk')  35.4 us
    all_gather x1, blocking collectives, body(): everyone = lax.all_gather(greens, 'blk', axis=1, tiled=True)  26.2 us
    all_to_all x1, waiting for transfers between devices, body(): lax.all_to_all(forward_aux, 'blk', split_axis=1, concat_axis=0, tiled=True)  22.9 us
    another operation x14, local copies, waits for them, and re-layouts, pairwise_terms(): return (jnp.stack(forward_list, 2), jnp.stack(backward_list, 2))  10.6 us
    all_to_all x1, waiting for transfers between devices, body(): lax.all_to_all(backward_aux, 'blk', split_axis=1, concat_axis=0, tiled=True)  8.81 us
    all_to_all x1, starting transfers between devices, body(): lax.all_to_all(forward_aux, 'blk', split_axis=1, concat_axis=0, tiled=True)  6.81 us
    dot_general x9, matrix products, pairwise_terms(): jnp.einsum('tml,stmn->stln', virtual_block_list[source:source + target_bl...  5.1 us
    all_to_all x1, starting transfers between devices, body(): lax.all_to_all(backward_aux, 'blk', split_axis=1, concat_axis=0, tiled=True)  4.52 us
  transfers between devices with their start and end apart: 2, of which 2 were waited for; matrix products, arithmetic and copies ran while one was open for 9% of the time, Pallas kernels for 0%

commit v1 on v0

v1 whole, which is shorter than its diff:
```python
import functools
import math

import jax
import jax.numpy as jnp
from jax import lax
from jax.experimental import pallas as pl
from jax.experimental.pallas import tpu as pltpu
from jax.sharding import PartitionSpec as P

EDGE = 64
HALF = 32
LANES = 128
VMEM = pl.BlockSpec(memory_space=pltpu.VMEM)
SMEM = pl.BlockSpec(memory_space=pltpu.SMEM)


def block_order(count):
    if count == 16:
        chips = [0, 2, 4, 6, 7, 5, 3, 1]
        return [2 * chip + core for chip in chips for core in (0, 1)]
    return list(range(count))


def block_of(device, count):
    order = block_order(count)
    if order == list(range(count)):
        return device
    block = jnp.int32(0)
    for j, d in enumerate(order):
        block = jnp.where(device == d, j, block)
    return block


def pack_kernel(works_on, x_ref, out_ref, rows_ref):
    blocks = x_ref.shape[1]
    for a in range(3):
        for c in range(HALF):
            rows_ref[a, pl.ds(c, blocks, stride=HALF), :] = x_ref[
                a, :, c * LANES : (c + 1) * LANES
            ].astype(jnp.float32)
        for d, b in enumerate(works_on):
            out_ref[d, pl.ds(a * HALF, HALF), :] = rows_ref[a, pl.ds(b * HALF, HALF), :].astype(
                jnp.bfloat16
            )


def prep_kernel(
    total, members, imask, omask, vmask, count, gprev, gown, gnext, vir_ref, occ_ref
):
    own = block_of(lax.axis_index("blk"), members)
    greens = (gprev, gown, gnext)
    lane = lax.broadcasted_iota(jnp.int32, (HALF, LANES), 1)
    row = lax.broadcasted_iota(jnp.int32, (HALF, LANES), 0)
    left = lane < EDGE
    col = jnp.where(left, lane, lane - EDGE)
    block = [lax.rem(own + (total + k - 2), total) for k in range(5)]
    held = [count[b] for b in block]
    cols = [(col < held[k]).astype(jnp.float32) for k in range(5)]
    rows = [[(2 * row + par < held[s + 1]).astype(jnp.float32) for par in range(2)] for s in range(3)]
    vir = []
    for s in range(3):
        v = greens[s][pl.ds((5 - s) * HALF, HALF), :].astype(jnp.float32) * cols[2]
        vir.append((v * rows[s][0], pltpu.roll(v, EDGE, 1) * rows[s][1]))
    for t in range(5):
        parts = []
        for par in range(2):
            for s in range(3):
                if 0 <= t - s <= 2:
                    m = block[s + 1]
                    factor = (vmask[2 - s, m] * imask[t - s, m]).astype(jnp.float32)
                    parts.append(vir[s][par] * factor)
        while len(parts) < 8:
            parts.append(jnp.zeros((HALF, LANES), jnp.float32))
        vir_ref[t] = jnp.concatenate(parts, 0).T[:EDGE].astype(jnp.bfloat16)
    for s in range(3):
        m = block[s + 1]
        for t in range(5):
            to = pl.ds(t * LANES, LANES)
            if 0 <= t - s <= 2:
                factor = (omask[t - s, m] * imask[2 - s, m]).astype(jnp.float32)
                o = greens[s][pl.ds((t - s) * HALF, HALF), :].astype(jnp.float32) * (cols[t] * factor)
                turned = pltpu.roll(o, EDGE, 1)
            for half in range(2):
                for par in range(2):
                    at = pl.ds((half * 6 + s * 2 + par) * HALF, HALF)
                    if 0 <= t - s <= 2:
                        value = (o if half == par else turned) * rows[s][par]
                        kept = jnp.where(left == (half == 0), value, 0.0).astype(jnp.bfloat16)
                    else:
                        kept = jnp.zeros((HALF, LANES), jnp.bfloat16)
                    occ_ref[at, to] = kept


def main_kernel(scale, vir_ref, occ_ref, sprev, sown, snext, out_ref, half_ref, full_ref):
    rows = sown.shape[0]
    slabs = (sprev, sown, snext)
    left = lax.broadcasted_iota(jnp.int32, (HALF, LANES), 1) < EDGE
    for j in range(rows // 2):
        sides = []
        for s in range(3):
            one, two = slabs[s][2 * j], slabs[s][2 * j + 1]
            sides.append(
                (
                    jnp.concatenate([one[:, :EDGE], two[:, :EDGE]], 1),
                    jnp.concatenate([one[:, EDGE:], two[:, EDGE:]], 1),
                )
            )
        for t in range(5):
            parts = [
                sides[s][par][(t - s) * HALF : (t - s + 1) * HALF]
                for par in range(2)
                for s in range(3)
                if 0 <= t - s <= 2
            ]
            both = jnp.dot(
                vir_ref[t][:, : HALF * len(parts)],
                jnp.concatenate(parts, 0),
                preferred_element_type=jnp.float32,
            )
            half_ref[pl.ds(j * EDGE, EDGE), pl.ds(t * LANES, LANES)] = both.astype(jnp.bfloat16)
    for j in range(0, rows // 2, 4):
        full = lax.dot_general(
            occ_ref[...],
            half_ref[pl.ds(j * EDGE, 4 * EDGE), :],
            (((1,), (1,)), ((), ())),
            preferred_element_type=jnp.float32,
        )
        for half in range(2):
            for s in range(3):
                at = (half * 6 + s * 2) * HALF
                for pair in range(2):
                    to = slice(pair * LANES, (pair + 1) * LANES)
                    even = full[at : at + HALF, to]
                    odd = full[at + HALF : at + 2 * HALF, to]
                    first = 2 * (j + 2 * pair) + half
                    place = pl.ds(s * HALF, HALF)
                    full_ref[first, place, :] = jnp.where(
                        left, even, pltpu.roll(odd, EDGE, 1)
                    ).astype(jnp.bfloat16)
                    full_ref[first + 2, place, :] = jnp.where(
                        left, pltpu.roll(even, EDGE, 1), odd
                    ).astype(jnp.bfloat16)
    group = 16
    span = group * 16
    ri = lax.broadcasted_iota(jnp.int32, (span, span), 0)
    ci = lax.broadcasted_iota(jnp.int32, (span, span), 1)
    same = lax.rem(ri, 16) == lax.rem(ci, 16)
    pick = (
        lax.broadcasted_iota(jnp.int32, (span, group), 0) // 16
        == lax.broadcasted_iota(jnp.int32, (span, group), 1)
    ).astype(jnp.float32)
    for p in range(0, rows, group):
        for q in range(0, rows, group):
            acc = None
            for s in range(3):
                for c in range(2):
                    lhs = slabs[s][pl.ds(p, group), pl.ds((2 - s) * HALF + c * 16, 16), :]
                    rhs = full_ref[pl.ds(q, group), pl.ds(s * HALF + c * 16, 16), :]
                    one = lax.dot_general(
                        lhs.reshape(span, LANES),
                        rhs.reshape(span, LANES),
                        (((1,), (1,)), ((), ())),
                        preferred_element_type=jnp.float32,
                    )
                    acc = one if acc is None else acc + one
            kept = jnp.where(same, acc, 0.0).reshape(group, 16, span)
            summed = jnp.sum(kept, axis=1)
            out_ref[pl.ds(p, group), pl.ds(q, group)] = scale * jnp.dot(
                summed, pick, preferred_element_type=jnp.float32, precision=lax.Precision.HIGHEST
            )


def body(integrals, occupied, virtual, imask, omask, vmask, count):
    total = integrals.shape[1]
    members = lax.axis_size("blk")
    order = block_order(members)
    works_on = [order.index(d) for d in range(members)]

    greens = jnp.concatenate([occupied[0], virtual[0]], 0).reshape(6 * HALF, LANES)

    def from_block(shift):
        return [(b, order[(b - shift) % members]) for b in range(members)]

    greens = tuple(lax.ppermute(greens, "blk", from_block(k)) for k in (-1, 0, 1))
    rows = pl.pallas_call(
        functools.partial(pack_kernel, works_on),
        out_shape=jax.ShapeDtypeStruct((members, 3 * HALF, LANES), jnp.bfloat16),
        in_specs=[VMEM],
        out_specs=VMEM,
        scratch_shapes=[pltpu.VMEM((3, total * HALF, LANES), jnp.float32)],
        compiler_params=pltpu.CompilerParams(vmem_limit_bytes=32 * 1024 * 1024),
        name="pack",
    )(jnp.transpose(integrals[0], (1, 0, 2)))
    rows, *greens = lax.optimization_barrier((rows, *greens))
    own = lax.all_to_all(rows, "blk", split_axis=0, concat_axis=0, tiled=True)
    own, *greens = lax.optimization_barrier((own, *greens))
    vir, occ = pl.pallas_call(
        functools.partial(prep_kernel, total, members),
        out_shape=(
            jax.ShapeDtypeStruct((5, EDGE, 2 * LANES), jnp.bfloat16),
            jax.ShapeDtypeStruct((12 * HALF, 5 * LANES), jnp.bfloat16),
        ),
        in_specs=[SMEM] * 4 + [VMEM] * 3,
        out_specs=(VMEM, VMEM),
        name="prep",
    )(imask.T, omask.T, vmask.T, count, *greens)

    forth = [(order[j], order[(j + 1) % members]) for j in range(members)]
    back = [(order[(j + 1) % members], order[j]) for j in range(members)]
    sprev = lax.ppermute(own, "blk", forth)
    snext = lax.ppermute(own, "blk", back)
    part = pl.pallas_call(
        functools.partial(main_kernel, 1.0 / math.sqrt(5 * EDGE * EDGE * total)),
        out_shape=jax.ShapeDtypeStruct((members, members), jnp.float32),
        in_specs=[VMEM] * 5,
        out_specs=VMEM,
        scratch_shapes=[
            pltpu.VMEM((members // 2 * EDGE, 5 * LANES), jnp.bfloat16),
            pltpu.VMEM((members, 3 * HALF, LANES), jnp.bfloat16),
        ],
        compiler_params=pltpu.CompilerParams(vmem_limit_bytes=48 * 1024 * 1024),
        name="products",
    )(vir, occ, sprev, own, snext)
    mine = lax.all_to_all(part, "blk", split_axis=0, concat_axis=0, tiled=True)
    return jnp.sum(mine, axis=0, keepdims=True)


def solution(mesh):
    return jax.shard_map(
        body,
        mesh=mesh,
        in_specs=(
            P(("grp", "blk"), None, None, None),
            P(("grp", "blk"), None, None),
            P(("grp", "blk"), None, None),
            P(),
            P(),
            P(),
            P(),
        ),
        out_specs=P(("grp", "blk"), None),
        check_vma=False,
    )
```

time: 146 us -> 52 us (0.36)
  blocking collectives: 61.6 us -> 28.7 us
  waiting for transfers between devices: 31.8 us -> 3.55 us
  local copies, waits for them, and re-layouts: 24.3 us -> 3.04 us
  matrix products: 11.8 us -> 0 us
  Pallas kernels: 0 us -> 4.45 us
  other arithmetic: 3.95 us -> 1.35 us
    psum x1 -> x0, blocking collectives: 35.4 us -> none  [body(): summed = lax.psum(partial_sum, 'blk')]
    all_to_all x2 -> x0, waiting for transfers between devices: 31.8 us -> none  [the longest x1 22.9 us: body(): lax.all_to_all(forward_aux, 'blk', split_axis=1, concat_axis=0, tiled=True)]
    all_to_all x0 -> x2, blocking collectives: none -> 28.7 us  [the longest x1 18.7 us: body(): own = lax.all_to_all(rows, 'blk', split_axis=0, concat_axis=0, tiled=True)]
    all_gather x1 -> x0, blocking collectives: 26.2 us -> none  [body(): everyone = lax.all_gather(greens, 'blk', axis=1, tiled=True)]
    another operation x17 -> x0, local copies, waits for them, and re-layouts: 12.8 us -> none  [the longest x14 10.6 us: pairwise_terms(): return (jnp.stack(forward_list, 2), jnp.stack(backward_list, 2))]
    dot_general x19 -> x0, matrix products: 11.8 us -> none  [the longest x9 5.1 us: pairwise_terms(): jnp.einsum('tml,stmn->stln', virtual_block_list[source:source + target_bl...]
    all_to_all x2 -> x0, starting transfers between devices: 11.3 us -> none  [the longest x1 6.81 us: body(): lax.all_to_all(forward_aux, 'blk', split_axis=1, concat_axis=0, tiled=True)]
    ppermute x0 -> x5, starting transfers between devices: none -> 10.3 us  [the longest x3 8.52 us: body(): lax.ppermute(greens, 'blk', from_block(k))]
  transfers between devices with their start and end apart: 2 -> 5, of which waited for: 2 -> 1; matrix products, arithmetic and copies ran while one was open for 9% -> 0% of each run, Pallas kernels for 0% -> 5%
where the time goes in v1:
time: 52 us; the launch traced here: 51.5 us
  blocking collectives  28.7 us (55%)
  starting transfers between devices  10.3 us (20%)
  Pallas kernels  4.45 us (9%)
  waiting for transfers between devices  3.55 us (7%)
  local copies, waits for them, and re-layouts  3.04 us (6%)
  other arithmetic  1.35 us (3%)
    all_to_all x1, blocking collectives, body(): own = lax.all_to_all(rows, 'blk', split_axis=0, concat_axis=0, tiled=True)  18.7 us
    all_to_all x1, blocking collectives, body(): mine = lax.all_to_all(part, 'blk', split_axis=0, concat_axis=0, tiled=True)  10 us
    ppermute x3, starting transfers between devices, body(): lax.ppermute(greens, 'blk', from_block(k))  8.52 us
    ppermute x1, waiting for transfers between devices, body(): sprev = lax.ppermute(own, 'blk', forth)  3.52 us
    unnamed x12, local copies, waits for them, and re-layouts  2.95 us
    pallas_call x1, Pallas kernels, body(): pl.pallas_call(functools.partial(prep_kernel, total, members), out_shape=...  1.94 us
    pallas_call x1, Pallas kernels, body(): pl.pallas_call(functools.partial(main_kernel, 1.0 / math.sqrt(5 * EDGE *...  1.84 us
    ppermute x1, starting transfers between devices, body(): snext = lax.ppermute(own, 'blk', back)  1.63 us
  transfers between devices with their start and end apart: 5, of which 1 were waited for; matrix products, arithmetic and copies ran while one was open for 0% of the time, Pallas kernels for 5%

profile of v1, /device:TPU:0, one launch (start us, length us, event | category | flops | bytes accessed | tf_op | source)
XLA Modules:
  0.0 51.5 jit_solution(16684666094703328944)
XLA Ops:
  0.0 0.8 %pad_maximum_fusion = bf16[6,4096]{1,0:T(8,128)(2,1)S(1)} fusion(bf16[3,4096]{1,0:T(4,128)(2,1)} %bitcast.14, bf16[3,4096]{1,0:T(4,128)(2,1)} %bitcast.15), kind=kLoop, calls=%fused_computation | loop fusion | flops 98304 | bytes 98304 | tf_op jit(solution)/shard_map/concatenate | solution.py:180
  0.8 0.1 reshape.5
  0.9 0.5 collective-permute-start
  1.4 0.7 %collective-permute-start.1 = (bf16[192,128]{1,0:T(8,128)(2,1)S(1)}, bf16[192,128]{1,0:T(8,128)(2,1)S(1)}, u32[]{:S(2)}, u32[]{:S(2)}) collective-permute-start(bf16[192,128]{1,0:T(8,128)(2,1)S(1)} %reshape.5), channel_id=1, source_target_pairs={{0,0},{1,1},{2,4},{3,5},{4,8},{5,9},{6,12},{7,13},{8,14},{9,15},{1... | collective-permute-start | bytes 147464 | tf_op jit(solution)/shard_map/ppermute | solution.py:185
  2.1 7.4 %collective-permute-start.2 = (bf16[192,128]{1,0:T(8,128)(2,1)S(1)}, bf16[192,128]{1,0:T(8,128)(2,1)S(1)}, u32[]{:S(2)}, u32[]{:S(2)}) collective-permute-start(bf16[192,128]{1,0:T(8,128)(2,1)S(1)} %reshape.5), channel_id=1, source_target_pairs={{0,3},{1,0},{2,1},{3,4},{4,5},{5,8},{6,9},{7,12},{8,13},{9,14},{10... | collective-permute-start | bytes 147464 | tf_op jit(solution)/shard_map/ppermute | solution.py:185
  9.4 0.0 copy-start.1
  9.4 1.0 %copy-done.1 = bf16[1,16,3,4096]{3,1,2,0:T(8,128)(2,1)S(1)} copy-done((bf16[1,16,3,4096]{3,1,2,0:T(8,128)(2,1)S(1)}, bf16[1,16,3,4096]{3,1,2,0:T(8,128)(2,1)}, u32[]{:S(2)}) %copy-start.1) | copy-done | bytes 393240
  10.4 0.7 %pack.1 = bf16[16,96,128]{2,1,0:T(8,128)(2,1)S(1)} custom-call(bf16[3,16,4096]{2,1,0:T(8,128)(2,1)S(1)} %bitcast.12), custom_call_target="tpu_custom_call" | custom-call | tf_op jit(solution)/shard_map/pack/pallas_call | solution.py:186
  11.1 0.0 collective-permute-done.gprev
  11.1 0.0 copy-start.3
  11.1 0.0 collective-permute-done.1.gown
  11.1 0.0 copy-start.4
  11.2 0.0 collective-permute-done.2.gnext
  11.2 0.0 copy-start.5
  11.2 18.7 %all_to_all.14.sown = bf16[16,96,128]{2,1,0:T(8,128)(2,1)S(1)} all-to-all(bf16[16,96,128]{2,1,0:T(8,128)(2,1)S(1)} %pack.1), channel_id=1, replica_groups=mesh['grp'=2,'blk'=16] {'blk'}, dimensions={0} | all-to-all | bytes 786432 | tf_op jit(solution)/shard_map/all_to_all | solution.py:196
  29.9 0.0 copy-done.3
  29.9 0.0 copy-done.4
  29.9 0.0 copy-done.5
  29.9 0.2 collective-permute-start.3
  30.1 1.6 %collective-permute-start.4 = (bf16[16,96,128]{2,1,0:T(8,128)(2,1)S(1)}, bf16[16,96,128]{2,1,0:T(8,128)(2,1)S(1)}, u32[]{:S(2)}, u32[]{:S(2)}) collective-permute-start(bf16[16,96,128]{2,1,0:T(8,128)(2,1)S(1)} %all_to_all.14.sown), channel_id=1, source_target_pairs={{1,0},{4,1},{5,4},{8,5},{9,8},{12,9},{13,12},{14,13},{15,14},{10,1... | collective-permute-start | bytes 1179656 | tf_op jit(solution)/shard_map/ppermute | solution.py:212
  31.7 1.9 %prep.1 = (bf16[5,64,256]{2,1,0:T(8,128)(2,1)}, bf16[384,640]{1,0:T(8,128)(2,1)}) custom-call(s32[3,16]{1,0:T(4,128)} %bitcast.16, s32[3,16]{1,0:T(4,128)} %bitcast.17, s32[3,16]{1,0:T(4,128)} %bitcast.18, s32[16]{0:T(128)} %count.1, bf16[192,128]{1,0:T(8,128)(2,1)} %copy-done.3, bf16[192,128]{1,0:T(8,128)(2,1)} %copy-done.4, bf16[192,128]{1,0:T(8,128)(2,1)} %copy-done.5), custom_call_target="tpu_custom_call" | custom-call | tf_op jit(solution)/shard_map/prep/pallas_call | solution.py:198
  33.7 3.5 %collective-permute-done.3.sprev = bf16[16,96,128]{2,1,0:T(8,128)(2,1)S(1)} collective-permute-done((bf16[16,96,128]{2,1,0:T(8,128)(2,1)S(1)}, bf16[16,96,128]{2,1,0:T(8,128)(2,1)S(1)}, u32[]{:S(2)}, u32[]{:S(2)}) %collective-permute-start.3) | collective-permute-done | bytes 393248 | tf_op jit(solution)/shard_map/ppermute | solution.py:211
  37.2 0.0 collective-permute-done.4.snext
  37.2 0.0 copy-start
  37.2 1.0 %copy-done = bf16[384,640]{1,0:T(8,128)(2,1)S(1)} copy-done((bf16[384,640]{1,0:T(8,128)(2,1)S(1)}, bf16[384,640]{1,0:T(8,128)(2,1)}, u32[]{:S(2)}) %copy-start) | copy-done | bytes 491544
  38.2 0.0 copy-start.2
  38.2 0.9 %copy-done.2 = bf16[5,64,256]{2,1,0:T(8,128)(2,1)S(1)} copy-done((bf16[5,64,256]{2,1,0:T(8,128)(2,1)S(1)}, bf16[5,64,256]{2,1,0:T(8,128)(2,1)}, u32[]{:S(2)}) %copy-start.2) | copy-done | bytes 163864
  39.1 1.8 %products.1 = f32[16,16]{1,0:T(8,128)S(1)} custom-call(bf16[5,64,256]{2,1,0:T(8,128)(2,1)S(1)} %copy-done.2, bf16[384,640]{1,0:T(8,128)(2,1)S(1)} %copy-done, bf16[16,96,128]{2,1,0:T(8,128)(2,1)S(1)} %collective-permute-done.3.sprev, bf16[16,96,128]{2,1,0:T(8,128)(2,1)S(1)} %all_to_all.14.sown, bf16[16,96,128]{2,1,0:T(8,128)(2,1)S(1)} %collective-permute-done.4.snext), custom_call_target="tpu_custom_call" | custom-call | tf_op jit(solution)/shard_map/products/pallas_call | solution.py:213
  41.0 10.0 %all_to_all.15 = f32[16,1,16]{2,1,0:T(1,128)S(1)} all-to-all(f32[16,1,16]{2,1,0:T(1,128)S(1)} %bitcast.13), channel_id=1, replica_groups=mesh['grp'=2,'blk'=16] {'blk'}, dimensions={0} | all-to-all | bytes 2048 | tf_op jit(solution)/shard_map/all_to_all | solution.py:225
  51.0 0.5 %reduce_sum.9 = f32[16]{0:T(128)} reduce(f32[16,1,16]{2,1,0:T(1,128)S(1)} %all_to_all.15, f32[]{:T(128)} %constant.0.clone.1), dimensions={0,1}, to_apply=%region_0.0 | reduce | flops 240 | bytes 1092 | tf_op jit(solution)/shard_map/reduce_sum | solution.py:226
Async XLA Ops:
  0.9 10.2 %collective-permute-start = (bf16[192,128]{1,0:T(8,128)(2,1)S(1)}, bf16[192,128]{1,0:T(8,128)(2,1)S(1)}, u32[]{:S(2)}, u32[]{:S(2)}) collective-permute-start(bf16[192,128]{1,0:T(8,128)(2,1)S(1)} %reshape.5), channel_id=1, source_target_pairs={{0,1},{1,4},{2,5},{3,8},{4,9},{5,12},{6,13},{7,14},{8,15},{9,10},{... | collective-permute-start | bytes 147464 | tf_op jit(solution)/shard_map/ppermute | solution.py:185
  1.4 9.7 %collective-permute-start.1 = (bf16[192,128]{1,0:T(8,128)(2,1)S(1)}, bf16[192,128]{1,0:T(8,128)(2,1)S(1)}, u32[]{:S(2)}, u32[]{:S(2)}) collective-permute-start(bf16[192,128]{1,0:T(8,128)(2,1)S(1)} %reshape.5), channel_id=1, source_target_pairs={{0,0},{1,1},{2,4},{3,5},{4,8},{5,9},{6,12},{7,13},{8,14},{9,15},{1... | collective-permute-start | bytes 147464 | tf_op jit(solution)/shard_map/ppermute | solution.py:185
  2.1 9.1 %collective-permute-start.2 = (bf16[192,128]{1,0:T(8,128)(2,1)S(1)}, bf16[192,128]{1,0:T(8,128)(2,1)S(1)}, u32[]{:S(2)}, u32[]{:S(2)}) collective-permute-start(bf16[192,128]{1,0:T(8,128)(2,1)S(1)} %reshape.5), channel_id=1, source_target_pairs={{0,3},{1,0},{2,1},{3,4},{4,5},{5,8},{6,9},{7,12},{8,13},{9,14},{10... | collective-permute-start | bytes 147464 | tf_op jit(solution)/shard_map/ppermute | solution.py:185
  9.4 1.0 %copy-start.1 = (bf16[1,16,3,4096]{3,1,2,0:T(8,128)(2,1)S(1)}, bf16[1,16,3,4096]{3,1,2,0:T(8,128)(2,1)}, u32[]{:S(2)}) copy-start(bf16[1,16,3,4096]{3,1,2,0:T(8,128)(2,1)} %param.7) | copy-start | bytes 1179652
  11.1 18.8 %copy-start.3 = (bf16[192,128]{1,0:T(8,128)(2,1)}, bf16[192,128]{1,0:T(8,128)(2,1)S(1)}, u32[]{:S(2)}) copy-start(bf16[192,128]{1,0:T(8,128)(2,1)S(1)} %collective-permute-done.gprev) | copy-start | bytes 147460
  11.1 18.8 %copy-start.4 = (bf16[192,128]{1,0:T(8,128)(2,1)}, bf16[192,128]{1,0:T(8,128)(2,1)S(1)}, u32[]{:S(2)}) copy-start(bf16[192,128]{1,0:T(8,128)(2,1)S(1)} %collective-permute-done.1.gown) | copy-start | bytes 147460
  11.2 18.7 %copy-start.5 = (bf16[192,128]{1,0:T(8,128)(2,1)}, bf16[192,128]{1,0:T(8,128)(2,1)S(1)}, u32[]{:S(2)}) copy-start(bf16[192,128]{1,0:T(8,128)(2,1)S(1)} %collective-permute-done.2.gnext) | copy-start | bytes 147460
  29.9 7.3 %collective-permute-start.3 = (bf16[16,96,128]{2,1,0:T(8,128)(2,1)S(1)}, bf16[16,96,128]{2,1,0:T(8,128)(2,1)S(1)}, u32[]{:S(2)}, u32[]{:S(2)}) collective-permute-start(bf16[16,96,128]{2,1,0:T(8,128)(2,1)S(1)} %all_to_all.14.sown), channel_id=1, source_target_pairs={{0,1},{1,4},{4,5},{5,8},{8,9},{9,12},{12,13},{13,14},{14,15},{15,1... | collective-permute-start | bytes 1179656 | tf_op jit(solution)/shard_map/ppermute | solution.py:211
  30.1 7.1 %collective-permute-start.4 = (bf16[16,96,128]{2,1,0:T(8,128)(2,1)S(1)}, bf16[16,96,128]{2,1,0:T(8,128)(2,1)S(1)}, u32[]{:S(2)}, u32[]{:S(2)}) collective-permute-start(bf16[16,96,128]{2,1,0:T(8,128)(2,1)S(1)} %all_to_all.14.sown), channel_id=1, source_target_pairs={{1,0},{4,1},{5,4},{8,5},{9,8},{12,9},{13,12},{14,13},{15,14},{10,1... | collective-permute-start | bytes 1179656 | tf_op jit(solution)/shard_map/ppermute | solution.py:212
  37.2 1.0 %copy-start = (bf16[384,640]{1,0:T(8,128)(2,1)S(1)}, bf16[384,640]{1,0:T(8,128)(2,1)}, u32[]{:S(2)}) copy-start(bf16[384,640]{1,0:T(8,128)(2,1)} %get-tuple-element.23.occ_ref) | copy-start | bytes 1474564
  38.2 0.9 %copy-start.2 = (bf16[5,64,256]{2,1,0:T(8,128)(2,1)S(1)}, bf16[5,64,256]{2,1,0:T(8,128)(2,1)}, u32[]{:S(2)}) copy-start(bf16[5,64,256]{2,1,0:T(8,128)(2,1)} %get-tuple-element.22.vir_ref) | copy-start | bytes 491524

commit v2 on v1

v2 whole, which is shorter than its diff:
```python
import functools
import math

import jax
import jax.numpy as jnp
from jax import lax
from jax.experimental import pallas as pl
from jax.experimental.pallas import tpu as pltpu
from jax.sharding import PartitionSpec as P

EDGE = 64
HALF = 32
LANES = 128
VMEM = pl.BlockSpec(memory_space=pltpu.VMEM)
SMEM = pl.BlockSpec(memory_space=pltpu.SMEM)


def block_order(count):
    if count == 16:
        chips = [0, 2, 4, 6, 7, 5, 3, 1]
        return [2 * chip + core for chip in chips for core in (0, 1)]
    return list(range(count))


def block_of(device, count):
    order = block_order(count)
    if order == list(range(count)):
        return device
    block = jnp.int32(0)
    for j, d in enumerate(order):
        block = jnp.where(device == d, j, block)
    return block


def pack_kernel(works_on, x_ref, occ_ref, vir_ref, out_ref, greens_ref, rows_ref):
    blocks = x_ref.shape[1]
    for k, ref in enumerate((occ_ref, vir_ref)):
        for c in range(HALF):
            rows_ref[3, pl.ds(3 * HALF * k + c, 3, stride=HALF), :] = ref[
                :, c * LANES : (c + 1) * LANES
            ].astype(jnp.float32)
    greens_ref[...] = rows_ref[3, pl.ds(0, 6 * HALF), :].astype(jnp.bfloat16)
    for a in range(3):
        for c in range(HALF):
            rows_ref[a, pl.ds(c, blocks, stride=HALF), :] = x_ref[
                a, :, c * LANES : (c + 1) * LANES
            ].astype(jnp.float32)
        for d, b in enumerate(works_on):
            out_ref[d, pl.ds(a * HALF, HALF), :] = rows_ref[a, pl.ds(b * HALF, HALF), :].astype(
                jnp.bfloat16
            )


def main_kernel(scale, total, rows, table, sprev, sown, snext, out_ref, vir_ref, occ_ref, half_ref, full_ref):
    slabs = (sprev, sown, snext)
    block_rows = 3 * HALF
    greens = rows * block_rows
    left = lax.broadcasted_iota(jnp.int32, (HALF, LANES), 1) < EDGE

    own = block_of(lax.axis_index("blk"), rows)
    lane = lax.broadcasted_iota(jnp.int32, (HALF, LANES), 1)
    row = lax.broadcasted_iota(jnp.int32, (HALF, LANES), 0)
    col = jnp.where(left, lane, lane - EDGE)
    block = [lax.rem(own + (total + k - 2), total) for k in range(5)]
    held = [table[9, b] for b in block]
    cols = [(col < held[k]).astype(jnp.float32) for k in range(5)]
    keep = [[(2 * row + par < held[s + 1]).astype(jnp.float32) for par in range(2)] for s in range(3)]
    vir = [[], []]
    for s in range(3):
        v = slabs[s][pl.ds(greens + (5 - s) * HALF, HALF), :].astype(jnp.float32)
        v = v * (cols[2] * table[8 - s, block[s + 1]].astype(jnp.float32))
        vir[0].append(v * keep[s][0])
        vir[1].append(pltpu.roll(v, EDGE, 1) * keep[s][1])
    for par in range(2):
        vir[par].append(jnp.zeros((HALF, LANES), jnp.float32))
    turned = jnp.concatenate([jnp.concatenate(vir[par], 0).T[:EDGE] for par in range(2)], 1)
    which = lax.rem(lax.broadcasted_iota(jnp.int32, (EDGE, 2 * LANES), 1), LANES) // HALF
    for t in range(5):
        factor = jnp.zeros((EDGE, 2 * LANES), jnp.float32)
        for s in range(3):
            if 0 <= t - s <= 2:
                factor = jnp.where(which == s, table[t - s, block[s + 1]].astype(jnp.float32), factor)
        vir_ref[t] = (turned * factor).astype(jnp.bfloat16)
    for s in range(3):
        m = block[s + 1]
        for t in range(5):
            to = pl.ds(t * LANES, LANES)
            if 0 <= t - s <= 2:
                factor = (table[3 + t - s, m] * table[2 - s, m]).astype(jnp.float32)
                o = slabs[s][pl.ds(greens + (t - s) * HALF, HALF), :].astype(jnp.float32)
                o = o * (cols[t] * factor)
                swapped = pltpu.roll(o, EDGE, 1)
            for half in range(2):
                for par in range(2):
                    at = pl.ds((half * 6 + s * 2 + par) * HALF, HALF)
                    if 0 <= t - s <= 2:
                        value = (o if half == par else swapped) * keep[s][par]
                        occ_ref[at, to] = jnp.where(left == (half == 0), value, 0.0).astype(
                            jnp.bfloat16
                        )
                    else:
                        occ_ref[at, to] = jnp.zeros((HALF, LANES), jnp.bfloat16)

    blank = jnp.zeros((HALF, LANES), jnp.bfloat16)
    for j in range(rows // 2):
        sides = []
        for s in range(3):
            one = slabs[s][pl.ds(2 * j * block_rows, block_rows), :]
            two = slabs[s][pl.ds((2 * j + 1) * block_rows, block_rows), :]
            sides.append(
                (
                    jnp.concatenate([one[:, :EDGE], two[:, :EDGE]], 1),
                    jnp.concatenate([one[:, EDGE:], two[:, EDGE:]], 1),
                )
            )
        for t in range(5):
            parts = []
            for par in range(2):
                for s in range(3):
                    if 0 <= t - s <= 2:
                        parts.append(sides[s][par][(t - s) * HALF : (t - s + 1) * HALF])
                    else:
                        parts.append(blank)
                parts.append(blank)
            both = jnp.dot(
                vir_ref[t], jnp.concatenate(parts, 0), preferred_element_type=jnp.float32
            )
            half_ref[pl.ds(j * EDGE, EDGE), pl.ds(t * LANES, LANES)] = both.astype(jnp.bfloat16)
    for j in range(0, rows // 2, 4):
        full = lax.dot_general(
            occ_ref[...],
            half_ref[pl.ds(j * EDGE, 4 * EDGE), :],
            (((1,), (1,)), ((), ())),
            preferred_element_type=jnp.float32,
        )
        for half in range(2):
            for s in range(3):
                at = (half * 6 + s * 2) * HALF
                for pair in range(2):
                    to = slice(pair * LANES, (pair + 1) * LANES)
                    even = full[at : at + HALF, to]
                    odd = full[at + HALF : at + 2 * HALF, to]
                    first = 2 * (j + 2 * pair) + half
                    place = pl.ds(s * HALF, HALF)
                    full_ref[first, place, :] = jnp.where(
                        left, even, pltpu.roll(odd, EDGE, 1)
                    ).astype(jnp.bfloat16)
                    full_ref[first + 2, place, :] = jnp.where(
                        left, pltpu.roll(even, EDGE, 1), odd
                    ).astype(jnp.bfloat16)
    group = 16
    span = group * 16
    ri = lax.broadcasted_iota(jnp.int32, (span, span), 0)
    ci = lax.broadcasted_iota(jnp.int32, (span, span), 1)
    same = lax.rem(ri, 16) == lax.rem(ci, 16)
    pick = (
        lax.broadcasted_iota(jnp.int32, (span, group), 0) // 16
        == lax.broadcasted_iota(jnp.int32, (span, group), 1)
    ).astype(jnp.float32)
    for p in range(0, rows, group):
        for q in range(0, rows, group):
            acc = None
            for s in range(3):
                for c in range(2):
                    lhs = jnp.concatenate(
                        [
                            slabs[s][pl.ds(k * block_rows + (2 - s) * HALF + c * 16, 16), :]
                            for k in range(p, p + group)
                        ],
                        0,
                    )
                    rhs = full_ref[pl.ds(q, group), pl.ds(s * HALF + c * 16, 16), :]
                    one = lax.dot_general(
                        lhs,
                        rhs.reshape(span, LANES),
                        (((1,), (1,)), ((), ())),
                        preferred_element_type=jnp.float32,
                    )
                    acc = one if acc is None else acc + one
            kept = jnp.where(same, acc, 0.0).reshape(group, 16, span)
            summed = jnp.sum(kept, axis=1)
            out_ref[pl.ds(p, group), pl.ds(q, group)] = scale * jnp.dot(
                summed, pick, preferred_element_type=jnp.float32, precision=lax.Precision.HIGHEST
            )


def body(integrals, occupied, virtual, imask, omask, vmask, count):
    total = integrals.shape[1]
    members = lax.axis_size("blk")
    order = block_order(members)
    works_on = [order.index(d) for d in range(members)]

    rows, greens = pl.pallas_call(
        functools.partial(pack_kernel, works_on),
        out_shape=(
            jax.ShapeDtypeStruct((members, 3 * HALF, LANES), jnp.bfloat16),
            jax.ShapeDtypeStruct((6 * HALF, LANES), jnp.bfloat16),
        ),
        in_specs=[VMEM] * 3,
        out_specs=(VMEM, VMEM),
        scratch_shapes=[pltpu.VMEM((4, total * HALF, LANES), jnp.float32)],
        compiler_params=pltpu.CompilerParams(vmem_limit_bytes=32 * 1024 * 1024),
        name="pack",
    )(jnp.transpose(integrals[0], (1, 0, 2)), occupied[0], virtual[0])
    greens = lax.ppermute(greens, "blk", list(enumerate(order)))
    own = lax.all_to_all(rows, "blk", split_axis=0, concat_axis=0, tiled=True)
    slab = jnp.concatenate([own.reshape(members * 3 * HALF, LANES), greens], 0)
    forth = [(order[j], order[(j + 1) % members]) for j in range(members)]
    back = [(order[(j + 1) % members], order[j]) for j in range(members)]
    sprev = lax.ppermute(slab, "blk", forth)
    snext = lax.ppermute(slab, "blk", back)
    table = jnp.concatenate([imask.T, omask.T, vmask.T, count[None]], 0)
    part = pl.pallas_call(
        functools.partial(main_kernel, 1.0 / math.sqrt(5 * EDGE * EDGE * total), total, members),
        out_shape=jax.ShapeDtypeStruct((members, members), jnp.float32),
        in_specs=[SMEM] + [VMEM] * 3,
        out_specs=VMEM,
        scratch_shapes=[
            pltpu.VMEM((5, EDGE, 2 * LANES), jnp.bfloat16),
            pltpu.VMEM((12 * HALF, 5 * LANES), jnp.bfloat16),
            pltpu.VMEM((members // 2 * EDGE, 5 * LANES), jnp.bfloat16),
            pltpu.VMEM((members, 3 * HALF, LANES), jnp.bfloat16),
        ],
        compiler_params=pltpu.CompilerParams(vmem_limit_bytes=48 * 1024 * 1024),
        name="products",
    )(table, sprev, slab, snext)
    mine = lax.all_to_all(part, "blk", split_axis=0, concat_axis=0, tiled=True)
    return jnp.sum(mine, axis=0, keepdims=True)


def solution(mesh):
    return jax.shard_map(
        body,
        mesh=mesh,
        in_specs=(
            P(("grp", "blk"), None, None, None),
            P(("grp", "blk"), None, None),
            P(("grp", "blk"), None, None),
            P(),
            P(),
            P(),
            P(),
        ),
        out_specs=P(("grp", "blk"), None),
        check_vma=False,
    )
```

time: 52 us -> 46.7 us (0.90)
  blocking collectives: 28.7 us -> 11.1 us
  waiting for transfers between devices: 3.55 us -> 17.3 us
  other arithmetic: 1.35 us -> 0.58 us
    all_to_all x1 -> x0, blocking collectives: 18.7 us -> none  [body(): own = lax.all_to_all(rows, 'blk', split_axis=0, concat_axis=0, tiled=True)]
    all_to_all x0 -> x1, waiting for transfers between devices: none -> 12 us  [body(): own = lax.all_to_all(rows, 'blk', split_axis=0, concat_axis=0, tiled=True)]
    ppermute x5 -> x3, starting transfers between devices: 10.3 us -> 2.46 us  [the longest x1 1.29 us: body(): snext = lax.ppermute(slab, 'blk', back)]
    all_to_all x0 -> x1, starting transfers between devices: none -> 7.39 us  [body(): own = lax.all_to_all(rows, 'blk', split_axis=0, concat_axis=0, tiled=True)]
    ppermute x5 -> x3, waiting for transfers between devices: 3.55 us -> 5.27 us  [the longest x1 5.27 us: body(): sprev = lax.ppermute(slab, 'blk', forth)]
    pallas_call x2 -> x1, Pallas kernels: 2.62 us -> 1.5 us  [body(): pl.pallas_call(functools.partial(pack_kernel, works_on), out_shape=(jax.S...]
    all_to_all x1, blocking collectives: 10 us -> 11.1 us  [body(): mine = lax.all_to_all(part, 'blk', split_axis=0, concat_axis=0, tiled=True)]
    pallas_call x1, Pallas kernels: 1.84 us -> 2.76 us  [body(): pl.pallas_call(functools.partial(main_kernel, 1.0 / math.sqrt(5 * EDGE *...]
  transfers between devices with their start and end apart: 5 -> 4, of which waited for: 1 -> 2; matrix products, arithmetic and copies ran while one was open for 0% -> 0% of each run, Pallas kernels for 5% -> 0%
where the time goes in v2:
time: 46.7 us; the launch traced here: 46.3 us
  waiting for transfers between devices  17.3 us (37%)
  blocking collectives  11.1 us (24%)
  starting transfers between devices  9.85 us (21%)
  Pallas kernels  4.25 us (9%)
  local copies, waits for them, and re-layouts  3.21 us (7%)
  other arithmetic  0.58 us (1%)
    all_to_all x1, waiting for transfers between devices, body(): own = lax.all_to_all(rows, 'blk', split_axis=0, concat_axis=0, tiled=True)  12 us
    all_to_all x1, blocking collectives, body(): mine = lax.all_to_all(part, 'blk', split_axis=0, concat_axis=0, tiled=True)  11.1 us
    all_to_all x1, starting transfers between devices, body(): own = lax.all_to_all(rows, 'blk', split_axis=0, concat_axis=0, tiled=True)  7.39 us
    ppermute x1, waiting for transfers between devices, body(): sprev = lax.ppermute(slab, 'blk', forth)  5.27 us
    unnamed x14, local copies, waits for them, and re-layouts  3.21 us
    pallas_call x1, Pallas kernels, body(): pl.pallas_call(functools.partial(main_kernel, 1.0 / math.sqrt(5 * EDGE *...  2.76 us
    pallas_call x1, Pallas kernels, body(): pl.pallas_call(functools.partial(pack_kernel, works_on), out_shape=(jax.S...  1.5 us
    ppermute x1, starting transfers between devices, body(): snext = lax.ppermute(slab, 'blk', back)  1.29 us
  transfers between devices with their start and end apart: 4, of which 2 were waited for; matrix products, arithmetic and copies ran while one was open for 0% of the time, Pallas kernels for 0%

profile of v2, /device:TPU:0, one launch (start us, length us, event | category | flops | bytes accessed | tf_op | source)
XLA Modules:
  0.0 46.3 jit_solution(9611556872495448446)
XLA Ops:
  0.0 0.0 copy-start
  0.0 1.0 %copy-done = bf16[1,16,3,4096]{3,1,2,0:T(8,128)(2,1)S(1)} copy-done((bf16[1,16,3,4096]{3,1,2,0:T(8,128)(2,1)S(1)}, bf16[1,16,3,4096]{3,1,2,0:T(8,128)(2,1)}, u32[]{:S(2)}) %copy-start) | copy-done | bytes 393240
  1.0 0.0 copy-start.1
  1.0 0.8 %copy-done.1 = bf16[1,3,4096]{2,1,0:T(4,128)(2,1)S(1)} copy-done((bf16[1,3,4096]{2,1,0:T(4,128)(2,1)S(1)}, bf16[1,3,4096]{2,1,0:T(4,128)(2,1)}, u32[]{:S(2)}) %copy-start.1) | copy-done | bytes 24600
  1.8 0.0 copy-start.2
  1.8 0.8 %copy-done.2 = bf16[1,3,4096]{2,1,0:T(4,128)(2,1)S(1)} copy-done((bf16[1,3,4096]{2,1,0:T(4,128)(2,1)S(1)}, bf16[1,3,4096]{2,1,0:T(4,128)(2,1)}, u32[]{:S(2)}) %copy-start.2) | copy-done | bytes 24600
  2.5 1.5 %pack.1 = (bf16[16,96,128]{2,1,0:T(8,128)(2,1)}, bf16[192,128]{1,0:T(8,128)(2,1)S(1)}) custom-call(bf16[3,16,4096]{2,1,0:T(8,128)(2,1)S(1)} %bitcast.14, bf16[3,4096]{1,0:T(4,128)(2,1)S(1)} %bitcast.16, bf16[3,4096]{1,0:T(4,128)(2,1)S(1)} %bitcast.17), custom_call_target="tpu_custom_call" | custom-call | tf_op jit(solution)/shard_map/pack/pallas_call | solution.py:193
  4.0 7.4 %all-to-all-start = ((bf16[16,96,128]{2,1,0:T(8,128)(2,1)}), bf16[16,96,128]{2,1,0:T(8,128)(2,1)S(1)}, u32[]{:S(2)}, u32[]{:S(2)}) async-start(bf16[16,96,128]{2,1,0:T(8,128)(2,1)} %get-tuple-element.7), calls=%async_computation | async-start | bytes 786432 | tf_op jit(solution)/shard_map/all_to_all | solution.py:206
  11.4 0.7 %collective-permute-start = (bf16[192,128]{1,0:T(8,128)(2,1)S(1)}, bf16[192,128]{1,0:T(8,128)(2,1)S(1)}, u32[]{:S(2)}, u32[]{:S(2)}) collective-permute-start(bf16[192,128]{1,0:T(8,128)(2,1)S(1)} %get-tuple-element.8), channel_id=1, source_target_pairs={{0,0},{1,1},{2,4},{3,5},{4,8},{5,9},{6,12},{7,13},{8,14},{9,15},{1... | collective-permute-start | bytes 147464 | tf_op jit(solution)/shard_map/ppermute | solution.py:205
  12.1 0.0 collective-permute-done
  12.1 12.0 %all-to-all-done = bf16[16,96,128]{2,1,0:T(8,128)(2,1)S(1)} async-done(((bf16[16,96,128]{2,1,0:T(8,128)(2,1)}), bf16[16,96,128]{2,1,0:T(8,128)(2,1)S(1)}, u32[]{:S(2)}, u32[]{:S(2)}) %all-to-all-start) | async-done | bytes 393248 | tf_op jit(solution)/shard_map/all_to_all | solution.py:206
  24.1 0.0 copy-start.5
  24.1 0.5 %collective-permute-start.1 = (bf16[1728,128]{1,0:T(8,128)(2,1)S(1)}, bf16[1728,128]{1,0:T(8,128)(2,1)S(1)}, u32[]{:S(2)}, u32[]{:S(2)}) collective-permute-start(bf16[1728,128]{1,0:T(8,128)(2,1)S(1)} %pad_maximum_fusion.sown), channel_id=1, source_target_pairs={{0,1},{1,4},{4,5},{5,8},{8,9},{9,12},{12,13},{13,14},{14,15},{15,1... | collective-permute-start | bytes 1327112 | tf_op jit(solution)/shard_map/ppermute | solution.py:210
  24.6 1.3 %collective-permute-start.2 = (bf16[1728,128]{1,0:T(8,128)(2,1)S(1)}, bf16[1728,128]{1,0:T(8,128)(2,1)S(1)}, u32[]{:S(2)}, u32[]{:S(2)}) collective-permute-start(bf16[1728,128]{1,0:T(8,128)(2,1)S(1)} %pad_maximum_fusion.sown), channel_id=1, source_target_pairs={{1,0},{4,1},{5,4},{8,5},{9,8},{12,9},{13,12},{14,13},{15,14},{10,1... | collective-permute-start | bytes 1327112 | tf_op jit(solution)/shard_map/ppermute | solution.py:211
  25.9 0.0 copy-start.4
  25.9 0.0 copy-start.3
  25.9 0.0 copy-start.6
  25.9 0.0 copy-done.5
  25.9 0.7 %copy-done.4 = s32[16,3]{0,1:T(4,128)S(1)} copy-done((s32[16,3]{0,1:T(4,128)S(1)}, s32[16,3]{0,1:T(4,128)}, u32[]{:S(2)}) %copy-start.4) | copy-done | bytes 216
  26.6 0.0 copy-done.3
  26.6 0.0 copy-done.6
  26.6 5.3 %collective-permute-done.1.sprev = bf16[1728,128]{1,0:T(8,128)(2,1)S(1)} collective-permute-done((bf16[1728,128]{1,0:T(8,128)(2,1)S(1)}, bf16[1728,128]{1,0:T(8,128)(2,1)S(1)}, u32[]{:S(2)}, u32[]{:S(2)}) %collective-permute-start.1) | collective-permute-done | bytes 442400 | tf_op jit(solution)/shard_map/ppermute | solution.py:210
  31.9 0.0 collective-permute-done.2.snext
  31.9 2.8 %products.1 = f32[16,16]{1,0:T(8,128)S(1)} custom-call(s32[10,16]{1,0:T(8,128)S(1)} %pad_add_fusion.table, bf16[1728,128]{1,0:T(8,128)(2,1)S(1)} %collective-permute-done.1.sprev, bf16[1728,128]{1,0:T(8,128)(2,1)S(1)} %pad_maximum_fusion.sown, bf16[1728,128]{1,0:T(8,128)(2,1)S(1)} %collective-permute-done.2.snext), custom_call_target="tpu_custom_call" | custom-call | tf_op jit(solution)/shard_map/products/pallas_call | solution.py:213
  34.6 11.1 %all_to_all.14 = f32[16,1,16]{2,1,0:T(1,128)S(1)} all-to-all(f32[16,1,16]{2,1,0:T(1,128)S(1)} %bitcast.15), channel_id=1, replica_groups=mesh['grp'=2,'blk'=16] {'blk'}, dimensions={0} | all-to-all | bytes 2048 | tf_op jit(solution)/shard_map/all_to_all | solution.py:227
  45.7 0.5 %reduce_sum.9 = f32[16]{0:T(128)} reduce(f32[16,1,16]{2,1,0:T(1,128)S(1)} %all_to_all.14, f32[]{:T(128)} %constant.0.clone.1), dimensions={0,1}, to_apply=%region_0.0 | reduce | flops 240 | bytes 1092 | tf_op jit(solution)/shard_map/reduce_sum | solution.py:228
  (2 shorter events, 0.0 us)
Async XLA Ops:
  0.0 1.0 %copy-start = (bf16[1,16,3,4096]{3,1,2,0:T(8,128)(2,1)S(1)}, bf16[1,16,3,4096]{3,1,2,0:T(8,128)(2,1)}, u32[]{:S(2)}) copy-start(bf16[1,16,3,4096]{3,1,2,0:T(8,128)(2,1)} %param.7) | copy-start | bytes 1179652
  1.0 0.8 %copy-start.1 = (bf16[1,3,4096]{2,1,0:T(4,128)(2,1)S(1)}, bf16[1,3,4096]{2,1,0:T(4,128)(2,1)}, u32[]{:S(2)}) copy-start(bf16[1,3,4096]{2,1,0:T(4,128)(2,1)} %param.8) | copy-start | bytes 73732
  1.8 0.8 %copy-start.2 = (bf16[1,3,4096]{2,1,0:T(4,128)(2,1)S(1)}, bf16[1,3,4096]{2,1,0:T(4,128)(2,1)}, u32[]{:S(2)}) copy-start(bf16[1,3,4096]{2,1,0:T(4,128)(2,1)} %param.9) | copy-start | bytes 73732
  4.0 20.1 %all-to-all-start = ((bf16[16,96,128]{2,1,0:T(8,128)(2,1)}), bf16[16,96,128]{2,1,0:T(8,128)(2,1)S(1)}, u32[]{:S(2)}, u32[]{:S(2)}) async-start(bf16[16,96,128]{2,1,0:T(8,128)(2,1)} %get-tuple-element.7), calls=%async_computation | async-start | bytes 786432 | tf_op jit(solution)/shard_map/all_to_all | solution.py:206
  11.4 0.7 %collective-permute-start = (bf16[192,128]{1,0:T(8,128)(2,1)S(1)}, bf16[192,128]{1,0:T(8,128)(2,1)S(1)}, u32[]{:S(2)}, u32[]{:S(2)}) collective-permute-start(bf16[192,128]{1,0:T(8,128)(2,1)S(1)} %get-tuple-element.8), channel_id=1, source_target_pairs={{0,0},{1,1},{2,4},{3,5},{4,8},{5,9},{6,12},{7,13},{8,14},{9,15},{1... | collective-permute-start | bytes 147464 | tf_op jit(solution)/shard_map/ppermute | solution.py:205
  24.1 1.8 %copy-start.5 = (s32[16,3]{0,1:T(4,128)S(1)}, s32[16,3]{0,1:T(4,128)}, u32[]{:S(2)}) copy-start(s32[16,3]{0,1:T(4,128)} %param.10) | copy-start | bytes 580
  24.1 7.8 %collective-permute-start.1 = (bf16[1728,128]{1,0:T(8,128)(2,1)S(1)}, bf16[1728,128]{1,0:T(8,128)(2,1)S(1)}, u32[]{:S(2)}, u32[]{:S(2)}) collective-permute-start(bf16[1728,128]{1,0:T(8,128)(2,1)S(1)} %pad_maximum_fusion.sown), channel_id=1, source_target_pairs={{0,1},{1,4},{4,5},{5,8},{8,9},{9,12},{12,13},{13,14},{14,15},{15,1... | collective-permute-start | bytes 1327112 | tf_op jit(solution)/shard_map/ppermute | solution.py:210
  24.6 7.3 %collective-permute-start.2 = (bf16[1728,128]{1,0:T(8,128)(2,1)S(1)}, bf16[1728,128]{1,0:T(8,128)(2,1)S(1)}, u32[]{:S(2)}, u32[]{:S(2)}) collective-permute-start(bf16[1728,128]{1,0:T(8,128)(2,1)S(1)} %pad_maximum_fusion.sown), channel_id=1, source_target_pairs={{1,0},{4,1},{5,4},{8,5},{9,8},{12,9},{13,12},{14,13},{15,14},{10,1... | collective-permute-start | bytes 1327112 | tf_op jit(solution)/shard_map/ppermute | solution.py:211
  25.9 0.7 %copy-start.4 = (s32[16,3]{0,1:T(4,128)S(1)}, s32[16,3]{0,1:T(4,128)}, u32[]{:S(2)}) copy-start(s32[16,3]{0,1:T(4,128)} %param.11) | copy-start | bytes 580
  25.9 0.7 %copy-start.3 = (s32[16,3]{0,1:T(4,128)S(1)}, s32[16,3]{0,1:T(4,128)}, u32[]{:S(2)}) copy-start(s32[16,3]{0,1:T(4,128)} %param.12) | copy-start | bytes 580
  25.9 0.7 %copy-start.6 = (s32[16]{0:T(128)S(1)}, s32[16]{0:T(128)}, u32[]{:S(2)}) copy-start(s32[16]{0:T(128)} %param.13) | copy-start | bytes 196

commit v3 on v2

v3 whole, which is shorter than its diff:
```python
import functools
import math

import jax
import jax.numpy as jnp
from jax import lax
from jax.experimental import pallas as pl
from jax.experimental.pallas import tpu as pltpu
from jax.sharding import PartitionSpec as P

EDGE = 64
HALF = 32
LANES = 128
VMEM = pl.BlockSpec(memory_space=pltpu.VMEM)
SMEM = pl.BlockSpec(memory_space=pltpu.SMEM)


def block_order(count):
    if count == 16:
        chips = [0, 2, 4, 6, 7, 5, 3, 1]
        return [2 * chip + core for chip in chips for core in (0, 1)]
    return list(range(count))


def pack_kernel(works_on, x_hbm, imask_hbm, out_hbm, x_ref, imask_ref, rows_ref, out_ref, sems):
    blocks = x_ref.shape[1]
    copies = [pltpu.make_async_copy(x_hbm.at[a], x_ref.at[a], sems.at[a]) for a in range(3)]
    masks = pltpu.make_async_copy(imask_hbm, imask_ref, sems.at[3])
    masks.start()
    for copy in copies:
        copy.start()
    diagonal = lax.broadcasted_iota(jnp.int32, (blocks, blocks), 0) == lax.broadcasted_iota(
        jnp.int32, (blocks, blocks), 1
    )
    masks.wait()
    sent = []
    for a in range(3):
        mask = jnp.where(diagonal, imask_ref[pl.ds(a, 1), :].astype(jnp.float32), 0.0)
        mask = jnp.broadcast_to(jnp.sum(mask, axis=1, keepdims=True), (blocks, LANES))
        copies[a].wait()
        for c in range(HALF):
            rows_ref[a, pl.ds(c, blocks, stride=HALF), :] = (
                x_ref[a, :, c * LANES : (c + 1) * LANES].astype(jnp.float32) * mask
            )
        part = pl.ds(a * HALF, HALF)
        for d, b in enumerate(works_on):
            out_ref[d, part, :] = rows_ref[a, pl.ds(b * HALF, HALF), :].astype(jnp.bfloat16)
        sent.append(
            pltpu.make_async_copy(out_ref.at[:, part, :], out_hbm.at[:, part, :], sems.at[4 + a])
        )
        sent[a].start()
    for copy in sent:
        copy.wait()


def prep_kernel(total, omask, vmask, count, occ_ref, vir_ref, out_ref, rows_ref):
    own = lax.axis_index("blk")
    for k, ref in enumerate((occ_ref, vir_ref)):
        for c in range(HALF):
            rows_ref[k, pl.ds(c, 3, stride=HALF), :] = ref[
                :, c * LANES : (c + 1) * LANES
            ].astype(jnp.float32)
    lane = lax.broadcasted_iota(jnp.int32, (HALF, LANES), 1)
    row = lax.broadcasted_iota(jnp.int32, (HALF, LANES), 0)
    left = lane < EDGE
    col = jnp.where(left, lane, lane - EDGE)
    keep = [(2 * row + par < count[own]).astype(jnp.float32) for par in range(2)]
    vir, occ = [], []
    for a in range(3):
        used = (col < count[lax.rem(own + (total + a - 1), total)]).astype(jnp.float32)
        v = rows_ref[1, pl.ds(a * HALF, HALF), :] * (used * vmask[a, own].astype(jnp.float32))
        vir += [v * keep[0], pltpu.roll(v, EDGE, 1) * keep[1]]
        o = rows_ref[0, pl.ds(a * HALF, HALF), :] * (used * omask[a, own].astype(jnp.float32))
        occ.append((pltpu.roll(o, EDGE, 1) * keep[0], o * keep[1]))
    vir += [jnp.zeros((HALF, LANES), jnp.float32)] * 2
    first = jnp.concatenate(vir[:4], 0).T[:EDGE]
    second = jnp.concatenate(vir[4:], 0).T[:EDGE]
    for a, turned in enumerate((first, pltpu.roll(first, EDGE, 1), second)):
        for par in range(2):
            out_ref[pl.ds((2 * a + par) * HALF, HALF), :] = jnp.where(
                left, turned[par * HALF : (par + 1) * HALF], occ[a][par]
            ).astype(jnp.bfloat16)


def main_kernel(scale, rows, sprev, sown, snext, out_ref, occ_ref, half_ref, full_ref):
    slabs = (sprev, sown, snext)
    block_rows = 3 * HALF
    greens = rows * block_rows
    left = lax.broadcasted_iota(jnp.int32, (HALF, LANES), 1) < EDGE

    def green(s, a):
        return slabs[s][pl.ds(greens + a * EDGE, EDGE), :]

    vir = jnp.concatenate([green(s, 2 - s)[:, :EDGE] for s in range(3)], 1)
    none = jnp.zeros((EDGE, EDGE), jnp.bfloat16)
    for s in range(3):
        for t in range(5):
            for half in range(2):
                at = pl.ds((half * 3 + s) * EDGE, EDGE)
                to = pl.ds(t * LANES, LANES)
                if 0 <= t - s <= 2:
                    o = green(s, t - s)[:, EDGE:]
                    occ_ref[at, to] = jnp.concatenate([none, o] if half else [o, none], 1)
                else:
                    occ_ref[at, to] = jnp.zeros((EDGE, LANES), jnp.bfloat16)

    blank = jnp.zeros((EDGE, LANES), jnp.bfloat16)
    for j in range(rows // 2):
        sides = []
        for s in range(3):
            one = slabs[s][pl.ds(2 * j * block_rows, block_rows), :]
            two = slabs[s][pl.ds((2 * j + 1) * block_rows, block_rows), :]
            sides.append(
                (
                    jnp.concatenate([one[:, :EDGE], two[:, :EDGE]], 1),
                    jnp.concatenate([one[:, EDGE:], two[:, EDGE:]], 1),
                )
            )
        for t in range(5):
            parts = []
            for s in range(3):
                if 0 <= t - s <= 2:
                    parts += [sides[s][par][(t - s) * HALF : (t - s + 1) * HALF] for par in range(2)]
                else:
                    parts.append(blank)
            both = jnp.dot(vir, jnp.concatenate(parts, 0), preferred_element_type=jnp.float32)
            half_ref[pl.ds(j * EDGE, EDGE), pl.ds(t * LANES, LANES)] = both.astype(jnp.bfloat16)
    for j in range(0, rows // 2, 4):
        full = lax.dot_general(
            occ_ref[...],
            half_ref[pl.ds(j * EDGE, 4 * EDGE), :],
            (((1,), (1,)), ((), ())),
            preferred_element_type=jnp.float32,
        )
        for half in range(2):
            for s in range(3):
                at = (half * 6 + s * 2) * HALF
                for pair in range(2):
                    to = slice(pair * LANES, (pair + 1) * LANES)
                    even = full[at : at + HALF, to]
                    odd = full[at + HALF : at + 2 * HALF, to]
                    first = 2 * (j + 2 * pair) + half
                    place = pl.ds(s * HALF, HALF)
                    full_ref[first, place, :] = jnp.where(
                        left, even, pltpu.roll(odd, EDGE, 1)
                    ).astype(jnp.bfloat16)
                    full_ref[first + 2, place, :] = jnp.where(
                        left, pltpu.roll(even, EDGE, 1), odd
                    ).astype(jnp.bfloat16)
    group = 16
    span = group * 16
    ri = lax.broadcasted_iota(jnp.int32, (span, span), 0)
    ci = lax.broadcasted_iota(jnp.int32, (span, span), 1)
    same = lax.rem(ri, 16) == lax.rem(ci, 16)
    pick = (
        lax.broadcasted_iota(jnp.int32, (span, group), 0) // 16
        == lax.broadcasted_iota(jnp.int32, (span, group), 1)
    ).astype(jnp.float32)
    for p in range(0, rows, group):
        for q in range(0, rows, group):
            acc = None
            for s in range(3):
                for c in range(2):
                    lhs = jnp.concatenate(
                        [
                            slabs[s][pl.ds(k * block_rows + (2 - s) * HALF + c * 16, 16), :]
                            for k in range(p, p + group)
                        ],
                        0,
                    )
                    rhs = full_ref[pl.ds(q, group), pl.ds(s * HALF + c * 16, 16), :]
                    one = lax.dot_general(
                        lhs,
                        rhs.reshape(span, LANES),
                        (((1,), (1,)), ((), ())),
                        preferred_element_type=jnp.float32,
                    )
                    acc = one if acc is None else acc + one
            kept = jnp.where(same, acc, 0.0).reshape(group, 16, span)
            summed = jnp.sum(kept, axis=1)
            out_ref[pl.ds(p, group), pl.ds(q, group)] = scale * jnp.dot(
                summed, pick, preferred_element_type=jnp.float32, precision=lax.Precision.HIGHEST
            )


def body(integrals, occupied, virtual, imask, omask, vmask, count):
    total = integrals.shape[1]
    members = lax.axis_size("blk")
    order = block_order(members)
    works_on = [order.index(d) for d in range(members)]

    rows = pl.pallas_call(
        functools.partial(pack_kernel, works_on),
        out_shape=jax.ShapeDtypeStruct((members, 3 * HALF, LANES), jnp.bfloat16),
        in_specs=[pl.BlockSpec(memory_space=pl.ANY)] * 2,
        out_specs=pl.BlockSpec(memory_space=pl.ANY),
        scratch_shapes=[
            pltpu.VMEM((3, total, EDGE * EDGE), jnp.bfloat16),
            pltpu.VMEM((3, total), jnp.int32),
            pltpu.VMEM((3, total * HALF, LANES), jnp.float32),
            pltpu.VMEM((members, 3 * HALF, LANES), jnp.bfloat16),
            pltpu.SemaphoreType.DMA((7,)),
        ],
        compiler_params=pltpu.CompilerParams(vmem_limit_bytes=63 * 1024 * 1024),
        name="pack",
    )(jnp.transpose(integrals[0], (1, 0, 2)), imask.T)
    greens = pl.pallas_call(
        functools.partial(prep_kernel, total),
        out_shape=jax.ShapeDtypeStruct((6 * HALF, LANES), jnp.bfloat16),
        in_specs=[SMEM] * 3 + [VMEM] * 2,
        out_specs=VMEM,
        scratch_shapes=[pltpu.VMEM((2, 3 * HALF, LANES), jnp.float32)],
        name="prep",
    )(omask.T, vmask.T, count, occupied[0], virtual[0])
    greens = lax.ppermute(greens, "blk", list(enumerate(order)))
    own = lax.all_to_all(rows, "blk", split_axis=0, concat_axis=0, tiled=True)
    slab = jnp.concatenate([own.reshape(members * 3 * HALF, LANES), greens], 0)
    forth = [(order[j], order[(j + 1) % members]) for j in range(members)]
    back = [(order[(j + 1) % members], order[j]) for j in range(members)]
    sprev = lax.ppermute(slab, "blk", forth)
    snext = lax.ppermute(slab, "blk", back)
    part = pl.pallas_call(
        functools.partial(main_kernel, 1.0 / math.sqrt(5 * EDGE * EDGE * total), members),
        out_shape=jax.ShapeDtypeStruct((members, members), jnp.float32),
        in_specs=[VMEM] * 3,
        out_specs=VMEM,
        scratch_shapes=[
            pltpu.VMEM((12 * HALF, 5 * LANES), jnp.bfloat16),
            pltpu.VMEM((members // 2 * EDGE, 5 * LANES), jnp.bfloat16),
            pltpu.VMEM((members, 3 * HALF, LANES), jnp.bfloat16),
        ],
        compiler_params=pltpu.CompilerParams(vmem_limit_bytes=48 * 1024 * 1024),
        name="products",
    )(sprev, slab, snext)
    mine = lax.all_to_all(part, "blk", split_axis=0, concat_axis=0, tiled=True)
    return jnp.sum(mine, axis=0, keepdims=True)


def solution(mesh):
    return jax.shard_map(
        body,
        mesh=mesh,
        in_specs=(
            P(("grp", "blk"), None, None, None),
            P(("grp", "blk"), None, None),
            P(("grp", "blk"), None, None),
            P(),
            P(),
            P(),
            P(),
        ),
        out_specs=P(("grp", "blk"), None),
        check_vma=False,
    )
```

time: 46.7 us -> 44.8 us (0.959)
  local copies, waits for them, and re-layouts: 3.21 us -> 0 us
  Pallas kernels: 4.25 us -> 5.97 us
  blocking collectives: 11.1 us -> 10.5 us
    ppermute x1, waiting for transfers between devices: 0.01 us -> 5.82 us  [body(): snext = lax.ppermute(slab, 'blk', back)]
    ppermute x1, waiting for transfers between devices: 5.27 us -> 1.91 us  [body(): sprev = lax.ppermute(slab, 'blk', forth)]
    unnamed x14 -> x0, local copies, waits for them, and re-layouts: 3.21 us -> none
    pallas_call x1 -> x2, Pallas kernels: 1.5 us -> 4.05 us  [the longest x1 2.35 us: body(): pl.pallas_call(functools.partial(pack_kernel, works_on), out_shape=jax.Sh...]
    all_to_all x1, waiting for transfers between devices: 12 us -> 9.52 us  [body(): own = lax.all_to_all(rows, 'blk', split_axis=0, concat_axis=0, tiled=True)]
    pallas_call x1, Pallas kernels: 2.76 us -> 1.92 us  [body(): pl.pallas_call(functools.partial(main_kernel, 1.0 / math.sqrt(5 * EDGE *...]
    ppermute x1, starting transfers between devices: 0.66 us -> 1.44 us  [body(): greens = lax.ppermute(greens, 'blk', list(enumerate(order)))]
    all_to_all x1, blocking collectives: 11.1 us -> 10.5 us  [body(): mine = lax.all_to_all(part, 'blk', split_axis=0, concat_axis=0, tiled=True)]
  transfers between devices with their start and end apart: 4 -> 4, of which waited for: 2 -> 3; matrix products, arithmetic and copies ran while one was open for 0% -> 0% of each run, Pallas kernels for 0% -> 4%
where the time goes in v3:
time: 44.8 us; the launch traced here: 44.4 us
  waiting for transfers between devices  17.2 us (38%)
  blocking collectives  10.5 us (23%)
  starting transfers between devices  10 us (22%)
  Pallas kernels  5.97 us (13%)
  other arithmetic  0.57 us (1%)
    all_to_all x1, blocking collectives, body(): mine = lax.all_to_all(part, 'blk', split_axis=0, concat_axis=0, tiled=True)  10.5 us
    all_to_all x1, waiting for transfers between devices, body(): own = lax.all_to_all(rows, 'blk', split_axis=0, concat_axis=0, tiled=True)  9.52 us
    all_to_all x1, starting transfers between devices, body(): own = lax.all_to_all(rows, 'blk', split_axis=0, concat_axis=0, tiled=True)  7.4 us
    ppermute x1, waiting for transfers between devices, body(): snext = lax.ppermute(slab, 'blk', back)  5.82 us
    pallas_call x1, Pallas kernels, body(): pl.pallas_call(functools.partial(pack_kernel, works_on), out_shape=jax.Sh...  2.35 us
    pallas_call x1, Pallas kernels, body(): pl.pallas_call(functools.partial(main_kernel, 1.0 / math.sqrt(5 * EDGE *...  1.92 us
    ppermute x1, waiting for transfers between devices, body(): sprev = lax.ppermute(slab, 'blk', forth)  1.91 us
    pallas_call x1, Pallas kernels, body(): pl.pallas_call(functools.partial(prep_kernel, total), out_shape=jax.Shape...  1.7 us
  transfers between devices with their start and end apart: 4, of which 3 were waited for; matrix products, arithmetic and copies ran while one was open for 0% of the time, Pallas kernels for 4%

profile of v3, /device:TPU:0, one launch (start us, length us, event | category | flops | bytes accessed | tf_op | source)
XLA Modules:
  0.0 44.4 jit_solution(15789115924969327974)
XLA Ops:
  0.0 2.3 %pack.1 = bf16[16,96,128]{2,1,0:T(8,128)(2,1)} custom-call(bf16[3,16,4096]{2,1,0:T(8,128)(2,1)} %bitcast.15, s32[3,16]{1,0:T(4,128)} %bitcast.18), custom_call_target="tpu_custom_call" | custom-call | tf_op jit(solution)/shard_map/pack/pallas_call | solution.py:192
  2.4 7.4 %all-to-all-start = ((bf16[16,96,128]{2,1,0:T(8,128)(2,1)}), bf16[16,96,128]{2,1,0:T(8,128)(2,1)S(1)}, u32[]{:S(2)}, u32[]{:S(2)}) async-start(bf16[16,96,128]{2,1,0:T(8,128)(2,1)} %pack.1), calls=%async_computation | async-start | bytes 786432 | tf_op jit(solution)/shard_map/all_to_all | solution.py:216
  9.8 1.7 %prep.1 = bf16[192,128]{1,0:T(8,128)(2,1)} custom-call(s32[3,16]{1,0:T(4,128)} %bitcast.19, s32[3,16]{1,0:T(4,128)} %bitcast.20, s32[16]{0:T(128)} %count.1, bf16[3,4096]{1,0:T(4,128)(2,1)} %bitcast.16, bf16[3,4096]{1,0:T(4,128)(2,1)} %bitcast.17), custom_call_target="tpu_custom_call" | custom-call | tf_op jit(solution)/shard_map/prep/pallas_call | solution.py:207
  11.5 1.4 %collective-permute-start = (bf16[192,128]{1,0:T(8,128)(2,1)}, bf16[192,128]{1,0:T(8,128)(2,1)S(1)}, u32[]{:S(2)}, u32[]{:S(2)}) collective-permute-start(bf16[192,128]{1,0:T(8,128)(2,1)} %prep.1), channel_id=1, source_target_pairs={{0,0},{1,1},{2,4},{3,5},{4,8},{5,9},{6,12},{7,13},{8,14},{9,15},{1... | collective-permute-start | bytes 147464 | tf_op jit(solution)/shard_map/ppermute | solution.py:215
  12.9 0.0 collective-permute-done
  12.9 9.5 %all-to-all-done = bf16[16,96,128]{2,1,0:T(8,128)(2,1)S(1)} async-done(((bf16[16,96,128]{2,1,0:T(8,128)(2,1)}), bf16[16,96,128]{2,1,0:T(8,128)(2,1)S(1)}, u32[]{:S(2)}, u32[]{:S(2)}) %all-to-all-start) | async-done | bytes 393248 | tf_op jit(solution)/shard_map/all_to_all | solution.py:216
  22.5 1.2 %collective-permute-start.2 = (bf16[1728,128]{1,0:T(8,128)(2,1)S(1)}, bf16[1728,128]{1,0:T(8,128)(2,1)S(1)}, u32[]{:S(2)}, u32[]{:S(2)}) collective-permute-start(bf16[1728,128]{1,0:T(8,128)(2,1)S(1)} %pad_maximum_fusion.sown), channel_id=1, source_target_pairs={{1,0},{4,1},{5,4},{8,5},{9,8},{12,9},{13,12},{14,13},{15,14},{10,1... | collective-permute-start | bytes 1327112 | tf_op jit(solution)/shard_map/ppermute | solution.py:221
  23.7 0.0 collective-permute-start.1
  23.7 5.8 %collective-permute-done.2.snext = bf16[1728,128]{1,0:T(8,128)(2,1)S(1)} collective-permute-done((bf16[1728,128]{1,0:T(8,128)(2,1)S(1)}, bf16[1728,128]{1,0:T(8,128)(2,1)S(1)}, u32[]{:S(2)}, u32[]{:S(2)}) %collective-permute-start.2) | collective-permute-done | bytes 442400 | tf_op jit(solution)/shard_map/ppermute | solution.py:221
  29.5 1.9 %collective-permute-done.1.sprev = bf16[1728,128]{1,0:T(8,128)(2,1)S(1)} collective-permute-done((bf16[1728,128]{1,0:T(8,128)(2,1)S(1)}, bf16[1728,128]{1,0:T(8,128)(2,1)S(1)}, u32[]{:S(2)}, u32[]{:S(2)}) %collective-permute-start.1) | collective-permute-done | bytes 442400 | tf_op jit(solution)/shard_map/ppermute | solution.py:220
  31.4 1.9 %products.1 = f32[16,16]{1,0:T(8,128)S(1)} custom-call(bf16[1728,128]{1,0:T(8,128)(2,1)S(1)} %collective-permute-done.1.sprev, bf16[1728,128]{1,0:T(8,128)(2,1)S(1)} %pad_maximum_fusion.sown, bf16[1728,128]{1,0:T(8,128)(2,1)S(1)} %collective-permute-done.2.snext), custom_call_target="tpu_custom_call" | custom-call | tf_op jit(solution)/shard_map/products/pallas_call | solution.py:222
  33.3 10.5 %all_to_all.14 = f32[16,1,16]{2,1,0:T(1,128)S(1)} all-to-all(f32[16,1,16]{2,1,0:T(1,128)S(1)} %bitcast.13), channel_id=1, replica_groups=mesh['grp'=2,'blk'=16] {'blk'}, dimensions={0} | all-to-all | bytes 2048 | tf_op jit(solution)/shard_map/all_to_all | solution.py:235
  43.8 0.5 %reduce_sum.9 = f32[16]{0:T(128)} reduce(f32[16,1,16]{2,1,0:T(1,128)S(1)} %all_to_all.14, f32[]{:T(128)} %constant.0.clone.1), dimensions={0,1}, to_apply=%region_0.0 | reduce | flops 240 | bytes 1092 | tf_op jit(solution)/shard_map/reduce_sum | solution.py:236
  (1 shorter events, 0.0 us)
Async XLA Ops:
  2.4 20.1 %all-to-all-start = ((bf16[16,96,128]{2,1,0:T(8,128)(2,1)}), bf16[16,96,128]{2,1,0:T(8,128)(2,1)S(1)}, u32[]{:S(2)}, u32[]{:S(2)}) async-start(bf16[16,96,128]{2,1,0:T(8,128)(2,1)} %pack.1), calls=%async_computation | async-start | bytes 786432 | tf_op jit(solution)/shard_map/all_to_all | solution.py:216
  11.5 1.4 %collective-permute-start = (bf16[192,128]{1,0:T(8,128)(2,1)}, bf16[192,128]{1,0:T(8,128)(2,1)S(1)}, u32[]{:S(2)}, u32[]{:S(2)}) collective-permute-start(bf16[192,128]{1,0:T(8,128)(2,1)} %prep.1), channel_id=1, source_target_pairs={{0,0},{1,1},{2,4},{3,5},{4,8},{5,9},{6,12},{7,13},{8,14},{9,15},{1... | collective-permute-start | bytes 147464 | tf_op jit(solution)/shard_map/ppermute | solution.py:215
  22.5 7.0 %collective-permute-start.2 = (bf16[1728,128]{1,0:T(8,128)(2,1)S(1)}, bf16[1728,128]{1,0:T(8,128)(2,1)S(1)}, u32[]{:S(2)}, u32[]{:S(2)}) collective-permute-start(bf16[1728,128]{1,0:T(8,128)(2,1)S(1)} %pad_maximum_fusion.sown), channel_id=1, source_target_pairs={{1,0},{4,1},{5,4},{8,5},{9,8},{12,9},{13,12},{14,13},{15,14},{10,1... | collective-permute-start | bytes 1327112 | tf_op jit(solution)/shard_map/ppermute | solution.py:221
  23.7 7.7 %collective-permute-start.1 = (bf16[1728,128]{1,0:T(8,128)(2,1)S(1)}, bf16[1728,128]{1,0:T(8,128)(2,1)S(1)}, u32[]{:S(2)}, u32[]{:S(2)}) collective-permute-start(bf16[1728,128]{1,0:T(8,128)(2,1)S(1)} %pad_maximum_fusion.sown), channel_id=1, source_target_pairs={{0,1},{1,4},{4,5},{5,8},{8,9},{9,12},{12,13},{13,14},{14,15},{15,1... | collective-permute-start | bytes 1327112 | tf_op jit(solution)/shard_map/ppermute | solution.py:220

commit v4 on v3

--- a/solution.py
+++ b/solution.py
@@ -82,71 +82,119 @@
             ).astype(jnp.bfloat16)
 
 
-def main_kernel(scale, rows, sprev, sown, snext, out_ref, occ_ref, half_ref, full_ref):
-    slabs = (sprev, sown, snext)
-    block_rows = 3 * HALF
-    greens = rows * block_rows
-    left = lax.broadcasted_iota(jnp.int32, (HALF, LANES), 1) < EDGE
+def main_kernel(
+    scale, rows, sprev, sown, gown, snext, out_ref, occ_ref, far_ref, half_ref, full_ref
+):
+    pair = 2 * HALF
+
+    def slab(s, q, a):
+        if s == 0:
+            return sprev[pl.ds(q * pair + (a - 1) * HALF, HALF), :]
+        if s == 2:
+            return snext[pl.ds(q * pair + a * HALF, HALF), :]
+        return sown[q, pl.ds(a * HALF, HALF), :]
 
     def green(s, a):
-        return slabs[s][pl.ds(greens + a * EDGE, EDGE), :]
-
-    vir = jnp.concatenate([green(s, 2 - s)[:, :EDGE] for s in range(3)], 1)
+        if s == 0:
+            return sprev[pl.ds(rows * pair + (a - 1) * EDGE, EDGE), :]
+        if s == 2:
+            return snext[pl.ds(rows * pair + a * EDGE, EDGE), :]
+        return gown[pl.ds(a * EDGE, EDGE), :]
+
     none = jnp.zeros((EDGE, EDGE), jnp.bfloat16)
+    near = [green(0, 2)[:, :EDGE], green(1, 1)[:, :EDGE], green(2, 0)[:, :EDGE]]
+    vir = [
+        jnp.concatenate(
+            [
+                jnp.concatenate(near[:2], 1),
+                jnp.concatenate([none, green(1, 2)[:, :EDGE]], 1),
+            ],
+            0,
+        ),
+        jnp.concatenate(near, 1),
+        jnp.concatenate(
+            [
+                jnp.concatenate(near[1:], 1),
+                jnp.concatenate([green(1, 0)[:, :EDGE], none], 1),
+            ],
+            0,
+        ),
+    ]
+    used = ({0: 1, 1: 2}, {0: 0, 1: 1, 2: 2}, {1: 0, 2: 1})
     for s in range(3):
-        for t in range(5):
+        for t in range(3):
             for half in range(2):
                 at = pl.ds((half * 3 + s) * EDGE, EDGE)
                 to = pl.ds(t * LANES, LANES)
-                if 0 <= t - s <= 2:
-                    o = green(s, t - s)[:, EDGE:]
+                if t in used[s]:
+                    o = green(s, used[s][t])[:, EDGE:]
                     occ_ref[at, to] = jnp.concatenate([none, o] if half else [o, none], 1)
                 else:
                     occ_ref[at, to] = jnp.zeros((EDGE, LANES), jnp.bfloat16)
-
-    blank = jnp.zeros((EDGE, LANES), jnp.bfloat16)
-    for j in range(rows // 2):
-        sides = []
-        for s in range(3):
-            one = slabs[s][pl.ds(2 * j * block_rows, block_rows), :]
-            two = slabs[s][pl.ds((2 * j + 1) * block_rows, block_rows), :]
-            sides.append(
-                (
-                    jnp.concatenate([one[:, :EDGE], two[:, :EDGE]], 1),
-                    jnp.concatenate([one[:, EDGE:], two[:, EDGE:]], 1),
-                )
+    for k in range(2):
+        o = green(1, 2 * k)[:, EDGE:]
+        far_ref[k] = jnp.concatenate(
+            [jnp.concatenate([o, none], 1), jnp.concatenate([none, o], 1)], 0
+        )
+
+    members = (((0, 1), (1, 0)), ((0, 2), (1, 1), (2, 0)), ((1, 2), (2, 1)))
+    for j in range(0, rows // 2, 2):
+
+        def side(s, a):
+            even, odd = [], []
+            for k in range(j, j + 2):
+                one, two = slab(s, 2 * k, a), slab(s, 2 * k + 1, a)
+                even.append(jnp.concatenate([one[:, :EDGE], two[:, :EDGE]], 1))
+                odd.append(jnp.concatenate([one[:, EDGE:], two[:, EDGE:]], 1))
+            return [jnp.concatenate(even, 1), jnp.concatenate(odd, 1)]
+
+        for t in range(3):
+            parts = []
+            for s, a in members[t]:
+                parts += side(s, a)
+            both = jnp.dot(vir[t], jnp.concatenate(parts, 0), preferred_element_type=jnp.float32)
+            both = both.astype(jnp.bfloat16)
+            for k in range(2):
+                at = pl.ds((j + k) * EDGE, EDGE)
+                piece = both[:, k * LANES : (k + 1) * LANES]
+                half_ref[at, pl.ds(t * LANES, LANES)] = piece[:EDGE]
+                if t != 1:
+                    half_ref[at, pl.ds((3 + t // 2) * LANES, LANES)] = piece[EDGE:]
+
+    left = lax.broadcasted_iota(jnp.int32, (HALF, LANES), 1) < EDGE
+    for j in range(0, rows // 2, 4):
+        at = pl.ds(j * EDGE, 4 * EDGE)
+        nt = (((1,), (1,)), ((), ()))
+        full = lax.dot_general(
+            occ_ref[...], half_ref[at, pl.ds(0, 3 * LANES)], nt, preferred_element_type=jnp.float32
+        )
+        far = [
+            lax.dot_general(
+                far_ref[k],
+                half_ref[at, pl.ds((3 + k) * LANES, LANES)],
+                nt,
+                preferred_element_type=jnp.float32,
             )
-        for t in range(5):
-            parts = []
-            for s in range(3):
-                if 0 <= t - s <= 2:
-                    parts += [sides[s][par][(t - s) * HALF : (t - s + 1) * HALF] for par in range(2)]
+            for k in range(2)
+        ]
+        for half in range(2):
+            for g in range(5):
+                if g < 3:
+                    block = full[(half * 3 + g) * EDGE : (half * 3 + g + 1) * EDGE]
                 else:
-                    parts.append(blank)
-            both = jnp.dot(vir, jnp.concatenate(parts, 0), preferred_element_type=jnp.float32)
-            half_ref[pl.ds(j * EDGE, EDGE), pl.ds(t * LANES, LANES)] = both.astype(jnp.bfloat16)
-    for j in range(0, rows // 2, 4):
-        full = lax.dot_general(
-            occ_ref[...],
-            half_ref[pl.ds(j * EDGE, 4 * EDGE), :],
-            (((1,), (1,)), ((), ())),
-            preferred_element_type=jnp.float32,
-        )
-        for half in range(2):
-            for s in range(3):
-                at = (half * 6 + s * 2) * HALF
-                for pair in range(2):
-                    to = slice(pair * LANES, (pair + 1) * LANES)
-                    even = full[at : at + HALF, to]
-                    odd = full[at + HALF : at + 2 * HALF, to]
-                    first = 2 * (j + 2 * pair) + half
-                    place = pl.ds(s * HALF, HALF)
+                    block = far[g - 3][half * EDGE : (half + 1) * EDGE]
+                for k in range(2):
+                    even = block[:HALF, k * LANES : (k + 1) * LANES]
+                    odd = block[HALF:, k * LANES : (k + 1) * LANES]
+                    first = 2 * (j + 2 * k) + half
+                    place = pl.ds(g * HALF, HALF)
                     full_ref[first, place, :] = jnp.where(
                         left, even, pltpu.roll(odd, EDGE, 1)
                     ).astype(jnp.bfloat16)
                     full_ref[first + 2, place, :] = jnp.where(
                         left, pltpu.roll(even, EDGE, 1), odd
                     ).astype(jnp.bfloat16)
+
     group = 16
     span = group * 16
     ri = lax.broadcasted_iota(jnp.int32, (span, span), 0)
@@ -159,23 +207,20 @@
     for p in range(0, rows, group):
         for q in range(0, rows, group):
             acc = None
-            for s in range(3):
-                for c in range(2):
-                    lhs = jnp.concatenate(
-                        [
-                            slabs[s][pl.ds(k * block_rows + (2 - s) * HALF + c * 16, 16), :]
-                            for k in range(p, p + group)
-                        ],
-                        0,
-                    )
-                    rhs = full_ref[pl.ds(q, group), pl.ds(s * HALF + c * 16, 16), :]
-                    one = lax.dot_general(
-                        lhs,
-                        rhs.reshape(span, LANES),
-                        (((1,), (1,)), ((), ())),
-                        preferred_element_type=jnp.float32,
-                    )
-                    acc = one if acc is None else acc + one
+            for g, (s, a) in enumerate(((0, 2), (1, 1), (2, 0), (1, 2), (1, 0))):
+                lhs = [slab(s, k, a) for k in range(p, p + group)]
+                lhs = [jnp.concatenate([x[:16], x[16:]], 1) for x in lhs]
+                rhs = [
+                    full_ref[pl.ds(q, group), pl.ds(g * HALF + c * 16, 16), :].reshape(span, LANES)
+                    for c in range(2)
+                ]
+                one = lax.dot_general(
+                    jnp.concatenate(lhs, 0),
+                    jnp.concatenate(rhs, 1),
+                    (((1,), (1,)), ((), ())),
+                    preferred_element_type=jnp.float32,
+                )
+                acc = one if acc is None else acc + one
             kept = jnp.where(same, acc, 0.0).reshape(group, 16, span)
             summed = jnp.sum(kept, axis=1)
             out_ref[pl.ds(p, group), pl.ds(q, group)] = scale * jnp.dot(
@@ -214,24 +259,26 @@
     )(omask.T, vmask.T, count, occupied[0], virtual[0])
     greens = lax.ppermute(greens, "blk", list(enumerate(order)))
     own = lax.all_to_all(rows, "blk", split_axis=0, concat_axis=0, tiled=True)
-    slab = jnp.concatenate([own.reshape(members * 3 * HALF, LANES), greens], 0)
     forth = [(order[j], order[(j + 1) % members]) for j in range(members)]
     back = [(order[(j + 1) % members], order[j]) for j in range(members)]
-    sprev = lax.ppermute(slab, "blk", forth)
-    snext = lax.ppermute(slab, "blk", back)
+    later = jnp.concatenate([own[:, HALF:].reshape(-1, LANES), greens[EDGE:]], 0)
+    early = jnp.concatenate([own[:, : 2 * HALF].reshape(-1, LANES), greens[: 2 * EDGE]], 0)
+    sprev = lax.ppermute(later, "blk", forth)
+    snext = lax.ppermute(early, "blk", back)
     part = pl.pallas_call(
         functools.partial(main_kernel, 1.0 / math.sqrt(5 * EDGE * EDGE * total), members),
         out_shape=jax.ShapeDtypeStruct((members, members), jnp.float32),
-        in_specs=[VMEM] * 3,
+        in_specs=[VMEM] * 4,
         out_specs=VMEM,
         scratch_shapes=[
-            pltpu.VMEM((12 * HALF, 5 * LANES), jnp.bfloat16),
+            pltpu.VMEM((6 * EDGE, 3 * LANES), jnp.bfloat16),
+            pltpu.VMEM((2, 2 * EDGE, LANES), jnp.bfloat16),
             pltpu.VMEM((members // 2 * EDGE, 5 * LANES), jnp.bfloat16),
-            pltpu.VMEM((members, 3 * HALF, LANES), jnp.bfloat16),
+            pltpu.VMEM((members, 5 * HALF, LANES), jnp.bfloat16),
         ],
         compiler_params=pltpu.CompilerParams(vmem_limit_bytes=48 * 1024 * 1024),
         name="products",
-    )(sprev, slab, snext)
+    )(sprev, own, greens, snext)
     mine = lax.all_to_all(part, "blk", split_axis=0, concat_axis=0, tiled=True)
     return jnp.sum(mine, axis=0, keepdims=True)
 

time: 44.8 us -> 42.4 us (0.946)
  waiting for transfers between devices: 17.2 us -> 13.8 us
  blocking collectives: 10.5 us -> 11.2 us
  starting transfers between devices: 10 us -> 10.7 us
    ppermute x2, waiting for transfers between devices: 7.72 us -> 4.33 us  [the longest x1 4.33 us: body(): sprev = lax.ppermute(later, 'blk', forth)]
    ppermute x2, starting transfers between devices: 1.2 us -> 1.85 us  [the longest x1 1.35 us: body(): snext = lax.ppermute(early, 'blk', back)]
    all_to_all x1, blocking collectives: 10.5 us -> 11.2 us  [body(): mine = lax.all_to_all(part, 'blk', split_axis=0, concat_axis=0, tiled=True)]
  transfers between devices with their start and end apart: 4 -> 4, of which waited for: 3 -> 2; matrix products, arithmetic and copies ran while one was open for 0% -> 0% of each run, Pallas kernels for 4% -> 4%
where the time goes in v4:
time: 42.4 us; the launch traced here: 42 us
  waiting for transfers between devices  13.8 us (33%)
  blocking collectives  11.2 us (26%)
  starting transfers between devices  10.7 us (25%)
  Pallas kernels  5.58 us (13%)
  other arithmetic  0.59 us (1%)
    all_to_all x1, blocking collectives, body(): mine = lax.all_to_all(part, 'blk', split_axis=0, concat_axis=0, tiled=True)  11.2 us
    all_to_all x1, waiting for transfers between devices, body(): own = lax.all_to_all(rows, 'blk', split_axis=0, concat_axis=0, tiled=True)  9.51 us
    all_to_all x1, starting transfers between devices, body(): own = lax.all_to_all(rows, 'blk', split_axis=0, concat_axis=0, tiled=True)  7.4 us
    ppermute x1, waiting for transfers between devices, body(): sprev = lax.ppermute(later, 'blk', forth)  4.33 us
    pallas_call x1, Pallas kernels, body(): pl.pallas_call(functools.partial(pack_kernel, works_on), out_shape=jax.Sh...  2.35 us
    pallas_call x1, Pallas kernels, body(): pl.pallas_call(functools.partial(prep_kernel, total), out_shape=jax.Shape...  1.7 us
    pallas_call x1, Pallas kernels, body(): pl.pallas_call(functools.partial(main_kernel, 1.0 / math.sqrt(5 * EDGE *...  1.53 us
    ppermute x1, starting transfers between devices, body(): greens = lax.ppermute(greens, 'blk', list(enumerate(order)))  1.44 us
  transfers between devices with their start and end apart: 4, of which 2 were waited for; matrix products, arithmetic and copies ran while one was open for 0% of the time, Pallas kernels for 4%

profile of v4, /device:TPU:0, one launch (start us, length us, event | category | flops | bytes accessed | tf_op | source)
XLA Modules:
  0.0 42.0 jit_solution(8675037313061216679)
XLA Ops:
  0.0 2.4 %pack.1 = bf16[16,96,128]{2,1,0:T(8,128)(2,1)} custom-call(bf16[3,16,4096]{2,1,0:T(8,128)(2,1)} %bitcast.17, s32[3,16]{1,0:T(4,128)} %bitcast.20), custom_call_target="tpu_custom_call" | custom-call | tf_op jit(solution)/shard_map/pack/pallas_call | solution.py:237
  2.4 7.4 %all-to-all-start = ((bf16[16,96,128]{2,1,0:T(8,128)(2,1)}), bf16[16,96,128]{2,1,0:T(8,128)(2,1)S(1)}, u32[]{:S(2)}, u32[]{:S(2)}) async-start(bf16[16,96,128]{2,1,0:T(8,128)(2,1)} %pack.1), calls=%async_computation | async-start | bytes 786432 | tf_op jit(solution)/shard_map/all_to_all | solution.py:261
  9.8 1.7 %prep.1 = bf16[192,128]{1,0:T(8,128)(2,1)} custom-call(s32[3,16]{1,0:T(4,128)} %bitcast.21, s32[3,16]{1,0:T(4,128)} %bitcast.22, s32[16]{0:T(128)} %count.1, bf16[3,4096]{1,0:T(4,128)(2,1)} %bitcast.18, bf16[3,4096]{1,0:T(4,128)(2,1)} %bitcast.19), custom_call_target="tpu_custom_call" | custom-call | tf_op jit(solution)/shard_map/prep/pallas_call | solution.py:252
  11.5 1.4 %collective-permute-start = (bf16[192,128]{1,0:T(8,128)(2,1)}, bf16[192,128]{1,0:T(8,128)(2,1)S(1)}, u32[]{:S(2)}, u32[]{:S(2)}) collective-permute-start(bf16[192,128]{1,0:T(8,128)(2,1)} %prep.1), channel_id=1, source_target_pairs={{0,0},{1,1},{2,4},{3,5},{4,8},{5,9},{6,12},{7,13},{8,14},{9,15},{1... | collective-permute-start | bytes 147464 | tf_op jit(solution)/shard_map/ppermute | solution.py:260
  12.9 0.0 collective-permute-done.gown
  12.9 9.5 %all-to-all-done.sown = bf16[16,96,128]{2,1,0:T(8,128)(2,1)S(1)} async-done(((bf16[16,96,128]{2,1,0:T(8,128)(2,1)}), bf16[16,96,128]{2,1,0:T(8,128)(2,1)S(1)}, u32[]{:S(2)}, u32[]{:S(2)}) %all-to-all-start) | async-done | bytes 393248 | tf_op jit(solution)/shard_map/all_to_all | solution.py:261
  22.4 0.1 fusion
  22.5 0.5 %collective-permute-start.1 = (bf16[1152,128]{1,0:T(8,128)(2,1)S(1)}, bf16[1152,128]{1,0:T(8,128)(2,1)S(1)}, u32[]{:S(2)}, u32[]{:S(2)}) collective-permute-start(bf16[1152,128]{1,0:T(8,128)(2,1)S(1)} %pad_maximum_fusion), channel_id=1, source_target_pairs={{0,1},{1,4},{4,5},{5,8},{8,9},{9,12},{12,13},{13,14},{14,15},{15,1... | collective-permute-start | bytes 884744 | tf_op jit(solution)/shard_map/ppermute | solution.py:266
  23.0 1.3 %collective-permute-start.2 = (bf16[1152,128]{1,0:T(8,128)(2,1)S(1)}, bf16[1152,128]{1,0:T(8,128)(2,1)S(1)}, u32[]{:S(2)}, u32[]{:S(2)}) collective-permute-start(bf16[1152,128]{1,0:T(8,128)(2,1)S(1)} %pad_maximum_fusion.1), channel_id=1, source_target_pairs={{1,0},{4,1},{5,4},{8,5},{9,8},{12,9},{13,12},{14,13},{15,14},{10,1... | collective-permute-start | bytes 884744 | tf_op jit(solution)/shard_map/ppermute | solution.py:267
  24.4 4.3 %collective-permute-done.1.sprev = bf16[1152,128]{1,0:T(8,128)(2,1)S(1)} collective-permute-done((bf16[1152,128]{1,0:T(8,128)(2,1)S(1)}, bf16[1152,128]{1,0:T(8,128)(2,1)S(1)}, u32[]{:S(2)}, u32[]{:S(2)}) %collective-permute-start.1) | collective-permute-done | bytes 294944 | tf_op jit(solution)/shard_map/ppermute | solution.py:266
  28.7 0.0 collective-permute-done.2.snext
  28.7 1.5 %products.1 = f32[16,16]{1,0:T(8,128)S(1)} custom-call(bf16[1152,128]{1,0:T(8,128)(2,1)S(1)} %collective-permute-done.1.sprev, bf16[16,96,128]{2,1,0:T(8,128)(2,1)S(1)} %all-to-all-done.sown, bf16[192,128]{1,0:T(8,128)(2,1)S(1)} %collective-permute-done.gown, bf16[1152,128]{1,0:T(8,128)(2,1)S(1)} %collective-permute-done.2.snext), custom_call_target="tpu_custom_call" | custom-call | tf_op jit(solution)/shard_map/products/pallas_call | solution.py:268
  30.3 11.2 %all_to_all.14 = f32[16,1,16]{2,1,0:T(1,128)S(1)} all-to-all(f32[16,1,16]{2,1,0:T(1,128)S(1)} %bitcast.14), channel_id=1, replica_groups=mesh['grp'=2,'blk'=16] {'blk'}, dimensions={0} | all-to-all | bytes 2048 | tf_op jit(solution)/shard_map/all_to_all | solution.py:282
  41.4 0.5 %reduce_sum.9 = f32[16]{0:T(128)} reduce(f32[16,1,16]{2,1,0:T(1,128)S(1)} %all_to_all.14, f32[]{:T(128)} %constant.0.clone.1), dimensions={0,1}, to_apply=%region_0.0 | reduce | flops 240 | bytes 1092 | tf_op jit(solution)/shard_map/reduce_sum | solution.py:283
  (3 shorter events, 0.0 us)
Async XLA Ops:
  2.4 20.1 %all-to-all-start = ((bf16[16,96,128]{2,1,0:T(8,128)(2,1)}), bf16[16,96,128]{2,1,0:T(8,128)(2,1)S(1)}, u32[]{:S(2)}, u32[]{:S(2)}) async-start(bf16[16,96,128]{2,1,0:T(8,128)(2,1)} %pack.1), calls=%async_computation | async-start | bytes 786432 | tf_op jit(solution)/shard_map/all_to_all | solution.py:261
  11.5 1.4 %collective-permute-start = (bf16[192,128]{1,0:T(8,128)(2,1)}, bf16[192,128]{1,0:T(8,128)(2,1)S(1)}, u32[]{:S(2)}, u32[]{:S(2)}) collective-permute-start(bf16[192,128]{1,0:T(8,128)(2,1)} %prep.1), channel_id=1, source_target_pairs={{0,0},{1,1},{2,4},{3,5},{4,8},{5,9},{6,12},{7,13},{8,14},{9,15},{1... | collective-permute-start | bytes 147464 | tf_op jit(solution)/shard_map/ppermute | solution.py:260
  22.5 6.2 %collective-permute-start.1 = (bf16[1152,128]{1,0:T(8,128)(2,1)S(1)}, bf16[1152,128]{1,0:T(8,128)(2,1)S(1)}, u32[]{:S(2)}, u32[]{:S(2)}) collective-permute-start(bf16[1152,128]{1,0:T(8,128)(2,1)S(1)} %pad_maximum_fusion), channel_id=1, source_target_pairs={{0,1},{1,4},{4,5},{5,8},{8,9},{9,12},{12,13},{13,14},{14,15},{15,1... | collective-permute-start | bytes 884744 | tf_op jit(solution)/shard_map/ppermute | solution.py:266
  23.0 5.7 %collective-permute-start.2 = (bf16[1152,128]{1,0:T(8,128)(2,1)S(1)}, bf16[1152,128]{1,0:T(8,128)(2,1)S(1)}, u32[]{:S(2)}, u32[]{:S(2)}) collective-permute-start(bf16[1152,128]{1,0:T(8,128)(2,1)S(1)} %pad_maximum_fusion.1), channel_id=1, source_target_pairs={{1,0},{4,1},{5,4},{8,5},{9,8},{12,9},{13,12},{14,13},{15,14},{10,1... | collective-permute-start | bytes 884744 | tf_op jit(solution)/shard_map/ppermute | solution.py:267

commit v5 on v4

--- a/solution.py
+++ b/solution.py
@@ -22,35 +22,27 @@
     return list(range(count))
 
 
-def pack_kernel(works_on, x_hbm, imask_hbm, out_hbm, x_ref, imask_ref, rows_ref, out_ref, sems):
+def block_of(device, count):
+    order = block_order(count)
+    if order == list(range(count)):
+        return device
+    block = jnp.int32(0)
+    for j, d in enumerate(order):
+        block = jnp.where(device == d, j, block)
+    return block
+
+
+def pack_kernel(works_on, x_ref, out_ref, rows_ref):
     blocks = x_ref.shape[1]
-    copies = [pltpu.make_async_copy(x_hbm.at[a], x_ref.at[a], sems.at[a]) for a in range(3)]
-    masks = pltpu.make_async_copy(imask_hbm, imask_ref, sems.at[3])
-    masks.start()
-    for copy in copies:
-        copy.start()
-    diagonal = lax.broadcasted_iota(jnp.int32, (blocks, blocks), 0) == lax.broadcasted_iota(
-        jnp.int32, (blocks, blocks), 1
-    )
-    masks.wait()
-    sent = []
     for a in range(3):
-        mask = jnp.where(diagonal, imask_ref[pl.ds(a, 1), :].astype(jnp.float32), 0.0)
-        mask = jnp.broadcast_to(jnp.sum(mask, axis=1, keepdims=True), (blocks, LANES))
-        copies[a].wait()
         for c in range(HALF):
-            rows_ref[a, pl.ds(c, blocks, stride=HALF), :] = (
-                x_ref[a, :, c * LANES : (c + 1) * LANES].astype(jnp.float32) * mask
+            rows_ref[a, pl.ds(c, blocks, stride=HALF), :] = x_ref[
+                a, :, c * LANES : (c + 1) * LANES
+            ].astype(jnp.float32)
+        for d, b in enumerate(works_on):
+            out_ref[d, pl.ds(a * HALF, HALF), :] = rows_ref[a, pl.ds(b * HALF, HALF), :].astype(
+                jnp.bfloat16
             )
-        part = pl.ds(a * HALF, HALF)
-        for d, b in enumerate(works_on):
-            out_ref[d, part, :] = rows_ref[a, pl.ds(b * HALF, HALF), :].astype(jnp.bfloat16)
-        sent.append(
-            pltpu.make_async_copy(out_ref.at[:, part, :], out_hbm.at[:, part, :], sems.at[4 + a])
-        )
-        sent[a].start()
-    for copy in sent:
-        copy.wait()
 
 
 def prep_kernel(total, omask, vmask, count, occ_ref, vir_ref, out_ref, rows_ref):
@@ -83,7 +75,7 @@
 
 
 def main_kernel(
-    scale, rows, sprev, sown, gown, snext, out_ref, occ_ref, far_ref, half_ref, full_ref
+    scale, rows, imask, sprev, sown, gown, snext, out_ref, occ_ref, far_ref, half_ref, full_ref
 ):
     pair = 2 * HALF
 
@@ -101,25 +93,24 @@
             return snext[pl.ds(rows * pair + a * EDGE, EDGE), :]
         return gown[pl.ds(a * EDGE, EDGE), :]
 
+    own = block_of(lax.axis_index("blk"), rows)
+    block = [lax.rem(own + (rows + s - 1), rows) for s in range(3)]
+
+    def screened(x, *at):
+        x = x.astype(jnp.float32)
+        for s, a in at:
+            x = x * imask[a, block[s]].astype(jnp.float32)
+        return x.astype(jnp.bfloat16)
+
     none = jnp.zeros((EDGE, EDGE), jnp.bfloat16)
-    near = [green(0, 2)[:, :EDGE], green(1, 1)[:, :EDGE], green(2, 0)[:, :EDGE]]
-    vir = [
-        jnp.concatenate(
-            [
-                jnp.concatenate(near[:2], 1),
-                jnp.concatenate([none, green(1, 2)[:, :EDGE]], 1),
-            ],
-            0,
-        ),
-        jnp.concatenate(near, 1),
-        jnp.concatenate(
-            [
-                jnp.concatenate(near[1:], 1),
-                jnp.concatenate([green(1, 0)[:, :EDGE], none], 1),
-            ],
-            0,
-        ),
-    ]
+
+    def vir_part(s, to, a):
+        return screened(green(s, to)[:, :EDGE], (s, a))
+
+    members = (((0, 1), (1, 0)), ((0, 2), (1, 1), (2, 0)), ((1, 2), (2, 1)))
+    vir = [jnp.concatenate([vir_part(s, 2 - s, a) for s, a in members[t]], 1) for t in range(3)]
+    vir[0] = jnp.concatenate([vir[0], jnp.concatenate([none, vir_part(1, 2, 0)], 1)], 0)
+    vir[2] = jnp.concatenate([vir[2], jnp.concatenate([vir_part(1, 0, 2), none], 1)], 0)
     used = ({0: 1, 1: 2}, {0: 0, 1: 1, 2: 2}, {1: 0, 2: 1})
     for s in range(3):
         for t in range(3):
@@ -127,17 +118,16 @@
                 at = pl.ds((half * 3 + s) * EDGE, EDGE)
                 to = pl.ds(t * LANES, LANES)
                 if t in used[s]:
-                    o = green(s, used[s][t])[:, EDGE:]
+                    o = screened(green(s, used[s][t])[:, EDGE:], (s, 2 - s))
                     occ_ref[at, to] = jnp.concatenate([none, o] if half else [o, none], 1)
                 else:
                     occ_ref[at, to] = jnp.zeros((EDGE, LANES), jnp.bfloat16)
     for k in range(2):
-        o = green(1, 2 * k)[:, EDGE:]
+        o = screened(green(1, 2 * k)[:, EDGE:], (1, 2 - 2 * k))
         far_ref[k] = jnp.concatenate(
             [jnp.concatenate([o, none], 1), jnp.concatenate([none, o], 1)], 0
         )
 
-    members = (((0, 1), (1, 0)), ((0, 2), (1, 1), (2, 0)), ((1, 2), (2, 1)))
     for j in range(0, rows // 2, 2):
 
         def side(s, a):
@@ -237,18 +227,12 @@
     rows = pl.pallas_call(
         functools.partial(pack_kernel, works_on),
         out_shape=jax.ShapeDtypeStruct((members, 3 * HALF, LANES), jnp.bfloat16),
-        in_specs=[pl.BlockSpec(memory_space=pl.ANY)] * 2,
-        out_specs=pl.BlockSpec(memory_space=pl.ANY),
-        scratch_shapes=[
-            pltpu.VMEM((3, total, EDGE * EDGE), jnp.bfloat16),
-            pltpu.VMEM((3, total), jnp.int32),
-            pltpu.VMEM((3, total * HALF, LANES), jnp.float32),
-            pltpu.VMEM((members, 3 * HALF, LANES), jnp.bfloat16),
-            pltpu.SemaphoreType.DMA((7,)),
-        ],
-        compiler_params=pltpu.CompilerParams(vmem_limit_bytes=63 * 1024 * 1024),
+        in_specs=[VMEM],
+        out_specs=VMEM,
+        scratch_shapes=[pltpu.VMEM((3, total * HALF, LANES), jnp.float32)],
+        compiler_params=pltpu.CompilerParams(vmem_limit_bytes=max(8, total // 4) * 1024 * 1024),
         name="pack",
-    )(jnp.transpose(integrals[0], (1, 0, 2)), imask.T)
+    )(jnp.transpose(integrals[0], (1, 0, 2)))
     greens = pl.pallas_call(
         functools.partial(prep_kernel, total),
         out_shape=jax.ShapeDtypeStruct((6 * HALF, LANES), jnp.bfloat16),
@@ -268,7 +252,7 @@
     part = pl.pallas_call(
         functools.partial(main_kernel, 1.0 / math.sqrt(5 * EDGE * EDGE * total), members),
         out_shape=jax.ShapeDtypeStruct((members, members), jnp.float32),
-        in_specs=[VMEM] * 4,
+        in_specs=[SMEM] + [VMEM] * 4,
         out_specs=VMEM,
         scratch_shapes=[
             pltpu.VMEM((6 * EDGE, 3 * LANES), jnp.bfloat16),
@@ -278,7 +262,7 @@
         ],
         compiler_params=pltpu.CompilerParams(vmem_limit_bytes=48 * 1024 * 1024),
         name="products",
-    )(sprev, own, greens, snext)
+    )(imask.T, sprev, own, greens, snext)
     mine = lax.all_to_all(part, "blk", split_axis=0, concat_axis=0, tiled=True)
     return jnp.sum(mine, axis=0, keepdims=True)
 

time: 42.4 us -> 43.1 us (1.017)
  local copies, waits for them, and re-layouts: 0.06 us -> 1.07 us
    unnamed x0 -> x4, local copies, waits for them, and re-layouts: none -> 1 us
    pallas_call x1, Pallas kernels: 2.35 us -> 1.45 us  [body(): pl.pallas_call(functools.partial(pack_kernel, works_on), out_shape=jax.Sh...]
    pallas_call x1, Pallas kernels: 1.53 us -> 2.14 us  [body(): pl.pallas_call(functools.partial(main_kernel, 1.0 / math.sqrt(5 * EDGE *...]
where the time goes in v5:
time: 43.1 us; the launch traced here: 42.7 us
  waiting for transfers between devices  13.8 us (32%)
  blocking collectives  11.2 us (26%)
  starting transfers between devices  10.7 us (25%)
  Pallas kernels  5.29 us (12%)
  local copies, waits for them, and re-layouts  1.07 us (2%)
  other arithmetic  0.59 us (1%)
    all_to_all x1, blocking collectives, body(): mine = lax.all_to_all(part, 'blk', split_axis=0, concat_axis=0, tiled=True)  11.2 us
    all_to_all x1, waiting for transfers between devices, body(): own = lax.all_to_all(rows, 'blk', split_axis=0, concat_axis=0, tiled=True)  9.51 us
    all_to_all x1, starting transfers between devices, body(): own = lax.all_to_all(rows, 'blk', split_axis=0, concat_axis=0, tiled=True)  7.39 us
    ppermute x1, waiting for transfers between devices, body(): sprev = lax.ppermute(later, 'blk', forth)  4.32 us
    pallas_call x1, Pallas kernels, body(): pl.pallas_call(functools.partial(main_kernel, 1.0 / math.sqrt(5 * EDGE *...  2.14 us
    pallas_call x1, Pallas kernels, body(): pl.pallas_call(functools.partial(prep_kernel, total), out_shape=jax.Shape...  1.7 us
    pallas_call x1, Pallas kernels, body(): pl.pallas_call(functools.partial(pack_kernel, works_on), out_shape=jax.Sh...  1.45 us
    ppermute x1, starting transfers between devices, body(): greens = lax.ppermute(greens, 'blk', list(enumerate(order)))  1.44 us
  transfers between devices with their start and end apart: 4, of which 2 were waited for; matrix products, arithmetic and copies ran while one was open for 0% of the time, Pallas kernels for 4%

profile of v5, /device:TPU:0, one launch (start us, length us, event | category | flops | bytes accessed | tf_op | source)
XLA Modules:
  0.0 42.7 jit_solution(13213707067312987457)
XLA Ops:
  0.0 0.0 copy-start
  0.0 1.0 %copy-done = bf16[1,16,3,4096]{3,1,2,0:T(8,128)(2,1)S(1)} copy-done((bf16[1,16,3,4096]{3,1,2,0:T(8,128)(2,1)S(1)}, bf16[1,16,3,4096]{3,1,2,0:T(8,128)(2,1)}, u32[]{:S(2)}) %copy-start) | copy-done | bytes 393240
  1.0 1.4 %pack.1 = bf16[16,96,128]{2,1,0:T(8,128)(2,1)} custom-call(bf16[3,16,4096]{2,1,0:T(8,128)(2,1)S(1)} %bitcast.14), custom_call_target="tpu_custom_call" | custom-call | tf_op jit(solution)/shard_map/pack/pallas_call | solution.py:227
  2.4 7.4 %all-to-all-start = ((bf16[16,96,128]{2,1,0:T(8,128)(2,1)}), bf16[16,96,128]{2,1,0:T(8,128)(2,1)S(1)}, u32[]{:S(2)}, u32[]{:S(2)}) async-start(bf16[16,96,128]{2,1,0:T(8,128)(2,1)} %pack.1), calls=%async_computation | async-start | bytes 786432 | tf_op jit(solution)/shard_map/all_to_all | solution.py:245
  9.8 1.7 %prep.1 = bf16[192,128]{1,0:T(8,128)(2,1)} custom-call(s32[3,16]{1,0:T(4,128)} %bitcast.21, s32[3,16]{1,0:T(4,128)} %bitcast.22, s32[16]{0:T(128)} %count.1, bf16[3,4096]{1,0:T(4,128)(2,1)} %bitcast.19, bf16[3,4096]{1,0:T(4,128)(2,1)} %bitcast.20), custom_call_target="tpu_custom_call" | custom-call | tf_op jit(solution)/shard_map/prep/pallas_call | solution.py:236
  11.5 1.4 %collective-permute-start = (bf16[192,128]{1,0:T(8,128)(2,1)}, bf16[192,128]{1,0:T(8,128)(2,1)S(1)}, u32[]{:S(2)}, u32[]{:S(2)}) collective-permute-start(bf16[192,128]{1,0:T(8,128)(2,1)} %prep.1), channel_id=1, source_target_pairs={{0,0},{1,1},{2,4},{3,5},{4,8},{5,9},{6,12},{7,13},{8,14},{9,15},{1... | collective-permute-start | bytes 147464 | tf_op jit(solution)/shard_map/ppermute | solution.py:244
  13.0 0.0 collective-permute-done.gown
  13.0 9.5 %all-to-all-done.sown = bf16[16,96,128]{2,1,0:T(8,128)(2,1)S(1)} async-done(((bf16[16,96,128]{2,1,0:T(8,128)(2,1)}), bf16[16,96,128]{2,1,0:T(8,128)(2,1)S(1)}, u32[]{:S(2)}, u32[]{:S(2)}) %all-to-all-start) | async-done | bytes 393248 | tf_op jit(solution)/shard_map/all_to_all | solution.py:245
  22.5 0.1 fusion
  22.6 0.5 %collective-permute-start.1 = (bf16[1152,128]{1,0:T(8,128)(2,1)S(1)}, bf16[1152,128]{1,0:T(8,128)(2,1)S(1)}, u32[]{:S(2)}, u32[]{:S(2)}) collective-permute-start(bf16[1152,128]{1,0:T(8,128)(2,1)S(1)} %pad_maximum_fusion), channel_id=1, source_target_pairs={{0,1},{1,4},{4,5},{5,8},{8,9},{9,12},{12,13},{13,14},{14,15},{15,1... | collective-permute-start | bytes 884744 | tf_op jit(solution)/shard_map/ppermute | solution.py:250
  23.1 0.0 copy-start.1
  23.1 1.3 %collective-permute-start.2 = (bf16[1152,128]{1,0:T(8,128)(2,1)S(1)}, bf16[1152,128]{1,0:T(8,128)(2,1)S(1)}, u32[]{:S(2)}, u32[]{:S(2)}) collective-permute-start(bf16[1152,128]{1,0:T(8,128)(2,1)S(1)} %pad_maximum_fusion.1), channel_id=1, source_target_pairs={{1,0},{4,1},{5,4},{8,5},{9,8},{12,9},{13,12},{14,13},{15,14},{10,1... | collective-permute-start | bytes 884744 | tf_op jit(solution)/shard_map/ppermute | solution.py:251
  24.5 4.3 %collective-permute-done.1.sprev = bf16[1152,128]{1,0:T(8,128)(2,1)S(1)} collective-permute-done((bf16[1152,128]{1,0:T(8,128)(2,1)S(1)}, bf16[1152,128]{1,0:T(8,128)(2,1)S(1)}, u32[]{:S(2)}, u32[]{:S(2)}) %collective-permute-start.1) | collective-permute-done | bytes 294944 | tf_op jit(solution)/shard_map/ppermute | solution.py:250
  28.8 0.0 collective-permute-done.2.snext
  28.8 0.0 copy-done.1
  28.8 2.1 %products.1 = f32[16,16]{1,0:T(8,128)S(1)} custom-call(s32[3,16]{1,0:T(4,128)S(1)} %bitcast.16, bf16[1152,128]{1,0:T(8,128)(2,1)S(1)} %collective-permute-done.1.sprev, bf16[16,96,128]{2,1,0:T(8,128)(2,1)S(1)} %all-to-all-done.sown, bf16[192,128]{1,0:T(8,128)(2,1)S(1)} %collective-permute-done.gown, bf16[1152,128]{1,0:T(8,128)(2,1)S(1)} %collective-permute-done.2.snext), custom_call_target="tpu_custom_call" | custom-call | tf_op jit(solution)/shard_map/products/pallas_call | solution.py:252
  31.0 11.2 %all_to_all.14 = f32[16,1,16]{2,1,0:T(1,128)S(1)} all-to-all(f32[16,1,16]{2,1,0:T(1,128)S(1)} %bitcast.15), channel_id=1, replica_groups=mesh['grp'=2,'blk'=16] {'blk'}, dimensions={0} | all-to-all | bytes 2048 | tf_op jit(solution)/shard_map/all_to_all | solution.py:266
  42.1 0.5 %reduce_sum.9 = f32[16]{0:T(128)} reduce(f32[16,1,16]{2,1,0:T(1,128)S(1)} %all_to_all.14, f32[]{:T(128)} %constant.0.clone.1), dimensions={0,1}, to_apply=%region_0.0 | reduce | flops 240 | bytes 1092 | tf_op jit(solution)/shard_map/reduce_sum | solution.py:267
  (3 shorter events, 0.0 us)
Async XLA Ops:
  0.0 1.0 %copy-start = (bf16[1,16,3,4096]{3,1,2,0:T(8,128)(2,1)S(1)}, bf16[1,16,3,4096]{3,1,2,0:T(8,128)(2,1)}, u32[]{:S(2)}) copy-start(bf16[1,16,3,4096]{3,1,2,0:T(8,128)(2,1)} %param.7) | copy-start | bytes 1179652
  2.4 20.1 %all-to-all-start = ((bf16[16,96,128]{2,1,0:T(8,128)(2,1)}), bf16[16,96,128]{2,1,0:T(8,128)(2,1)S(1)}, u32[]{:S(2)}, u32[]{:S(2)}) async-start(bf16[16,96,128]{2,1,0:T(8,128)(2,1)} %pack.1), calls=%async_computation | async-start | bytes 786432 | tf_op jit(solution)/shard_map/all_to_all | solution.py:245
  11.5 1.4 %collective-permute-start = (bf16[192,128]{1,0:T(8,128)(2,1)}, bf16[192,128]{1,0:T(8,128)(2,1)S(1)}, u32[]{:S(2)}, u32[]{:S(2)}) collective-permute-start(bf16[192,128]{1,0:T(8,128)(2,1)} %prep.1), channel_id=1, source_target_pairs={{0,0},{1,1},{2,4},{3,5},{4,8},{5,9},{6,12},{7,13},{8,14},{9,15},{1... | collective-permute-start | bytes 147464 | tf_op jit(solution)/shard_map/ppermute | solution.py:244
  22.6 6.2 %collective-permute-start.1 = (bf16[1152,128]{1,0:T(8,128)(2,1)S(1)}, bf16[1152,128]{1,0:T(8,128)(2,1)S(1)}, u32[]{:S(2)}, u32[]{:S(2)}) collective-permute-start(bf16[1152,128]{1,0:T(8,128)(2,1)S(1)} %pad_maximum_fusion), channel_id=1, source_target_pairs={{0,1},{1,4},{4,5},{5,8},{8,9},{9,12},{12,13},{13,14},{14,15},{15,1... | collective-permute-start | bytes 884744 | tf_op jit(solution)/shard_map/ppermute | solution.py:250
  23.1 5.7 %copy-start.1 = (s32[16,3]{0,1:T(4,128)S(1)}, s32[16,3]{0,1:T(4,128)}, u32[]{:S(2)}) copy-start(s32[16,3]{0,1:T(4,128)} %param.10) | copy-start | bytes 580
  23.1 5.7 %collective-permute-start.2 = (bf16[1152,128]{1,0:T(8,128)(2,1)S(1)}, bf16[1152,128]{1,0:T(8,128)(2,1)S(1)}, u32[]{:S(2)}, u32[]{:S(2)}) collective-permute-start(bf16[1152,128]{1,0:T(8,128)(2,1)S(1)} %pad_maximum_fusion.1), channel_id=1, source_target_pairs={{1,0},{4,1},{5,4},{8,5},{9,8},{12,9},{13,12},{14,13},{15,14},{10,1... | collective-permute-start | bytes 884744 | tf_op jit(solution)/shard_map/ppermute | solution.py:251

commit v6 on v4

--- a/solution.py
+++ b/solution.py
@@ -17,7 +17,7 @@
 
 def block_order(count):
     if count == 16:
-        chips = [0, 2, 4, 6, 7, 5, 3, 1]
+        chips = [3, 1, 0, 2, 4, 6, 7, 5]
         return [2 * chip + core for chip in chips for core in (0, 1)]
     return list(range(count))
 

time: 42.4 us -> 41.2 us (0.972)
  starting transfers between devices: 10.7 us -> 14 us
  waiting for transfers between devices: 13.8 us -> 10.6 us
  blocking collectives: 11.2 us -> 10 us
    all_to_all x1, waiting for transfers between devices: 9.51 us -> 3.07 us  [body(): own = lax.all_to_all(rows, 'blk', split_axis=0, concat_axis=0, tiled=True)]
    ppermute x1, starting transfers between devices: 1.44 us -> 4.72 us  [body(): greens = lax.ppermute(greens, 'blk', list(enumerate(order)))]
    ppermute x1, waiting for transfers between devices: 0.01 us -> 3.17 us  [body(): greens = lax.ppermute(greens, 'blk', list(enumerate(order)))]
    all_to_all x1, blocking collectives: 11.2 us -> 10 us  [body(): mine = lax.all_to_all(part, 'blk', split_axis=0, concat_axis=0, tiled=True)]
    ppermute x1, starting transfers between devices: 0.5 us -> 0.06 us  [body(): sprev = lax.ppermute(later, 'blk', forth)]
    ppermute x1, starting transfers between devices: 1.35 us -> 1.78 us  [body(): snext = lax.ppermute(early, 'blk', back)]
  transfers between devices with their start and end apart: 4 -> 4, of which waited for: 2 -> 3; matrix products, arithmetic and copies ran while one was open for 0% -> 0% of each run, Pallas kernels for 4% -> 4%
where the time goes in v6:
time: 41.2 us; the launch traced here: 40.8 us
  starting transfers between devices  14 us (34%)
  waiting for transfers between devices  10.6 us (26%)
  blocking collectives  10 us (24%)
  Pallas kernels  5.58 us (14%)
  other arithmetic  0.59 us (1%)
    all_to_all x1, blocking collectives, body(): mine = lax.all_to_all(part, 'blk', split_axis=0, concat_axis=0, tiled=True)  10 us
    all_to_all x1, starting transfers between devices, body(): own = lax.all_to_all(rows, 'blk', split_axis=0, concat_axis=0, tiled=True)  7.4 us
    ppermute x1, starting transfers between devices, body(): greens = lax.ppermute(greens, 'blk', list(enumerate(order)))  4.72 us
    ppermute x1, waiting for transfers between devices, body(): sprev = lax.ppermute(later, 'blk', forth)  4.33 us
    ppermute x1, waiting for transfers between devices, body(): greens = lax.ppermute(greens, 'blk', list(enumerate(order)))  3.17 us
    all_to_all x1, waiting for transfers between devices, body(): own = lax.all_to_all(rows, 'blk', split_axis=0, concat_axis=0, tiled=True)  3.07 us
    pallas_call x1, Pallas kernels, body(): pl.pallas_call(functools.partial(pack_kernel, works_on), out_shape=jax.Sh...  2.35 us
    ppermute x1, starting transfers between devices, body(): snext = lax.ppermute(early, 'blk', back)  1.78 us
  transfers between devices with their start and end apart: 4, of which 3 were waited for; matrix products, arithmetic and copies ran while one was open for 0% of the time, Pallas kernels for 4%

profile of v6, /device:TPU:0, one launch (start us, length us, event | category | flops | bytes accessed | tf_op | source)
XLA Modules:
  0.0 40.8 jit_solution(1586784872881091592)
XLA Ops:
  0.0 2.3 %pack.1 = bf16[16,96,128]{2,1,0:T(8,128)(2,1)} custom-call(bf16[3,16,4096]{2,1,0:T(8,128)(2,1)} %bitcast.17, s32[3,16]{1,0:T(4,128)} %bitcast.20), custom_call_target="tpu_custom_call" | custom-call | tf_op jit(solution)/shard_map/pack/pallas_call | solution.py:237
  2.4 7.4 %all-to-all-start = ((bf16[16,96,128]{2,1,0:T(8,128)(2,1)}), bf16[16,96,128]{2,1,0:T(8,128)(2,1)S(1)}, u32[]{:S(2)}, u32[]{:S(2)}) async-start(bf16[16,96,128]{2,1,0:T(8,128)(2,1)} %pack.1), calls=%async_computation | async-start | bytes 786432 | tf_op jit(solution)/shard_map/all_to_all | solution.py:261
  9.8 1.7 %prep.1 = bf16[192,128]{1,0:T(8,128)(2,1)} custom-call(s32[3,16]{1,0:T(4,128)} %bitcast.21, s32[3,16]{1,0:T(4,128)} %bitcast.22, s32[16]{0:T(128)} %count.1, bf16[3,4096]{1,0:T(4,128)(2,1)} %bitcast.18, bf16[3,4096]{1,0:T(4,128)(2,1)} %bitcast.19), custom_call_target="tpu_custom_call" | custom-call | tf_op jit(solution)/shard_map/prep/pallas_call | solution.py:252
  11.5 4.7 %collective-permute-start = (bf16[192,128]{1,0:T(8,128)(2,1)}, bf16[192,128]{1,0:T(8,128)(2,1)S(1)}, u32[]{:S(2)}, u32[]{:S(2)}) collective-permute-start(bf16[192,128]{1,0:T(8,128)(2,1)} %prep.1), channel_id=1, source_target_pairs={{0,6},{1,7},{2,2},{3,3},{4,0},{5,1},{6,4},{7,5},{8,8},{9,9},{10,12... | collective-permute-start | bytes 147464 | tf_op jit(solution)/shard_map/ppermute | solution.py:260
  16.2 3.2 %collective-permute-done.gown = bf16[192,128]{1,0:T(8,128)(2,1)S(1)} collective-permute-done((bf16[192,128]{1,0:T(8,128)(2,1)}, bf16[192,128]{1,0:T(8,128)(2,1)S(1)}, u32[]{:S(2)}, u32[]{:S(2)}) %collective-permute-start) | collective-permute-done | bytes 49184 | tf_op jit(solution)/shard_map/ppermute | solution.py:260
  19.4 3.1 %all-to-all-done.sown = bf16[16,96,128]{2,1,0:T(8,128)(2,1)S(1)} async-done(((bf16[16,96,128]{2,1,0:T(8,128)(2,1)}), bf16[16,96,128]{2,1,0:T(8,128)(2,1)S(1)}, u32[]{:S(2)}, u32[]{:S(2)}) %all-to-all-start) | async-done | bytes 393248 | tf_op jit(solution)/shard_map/all_to_all | solution.py:261
  22.4 0.1 fusion
  22.5 0.1 collective-permute-start.1
  22.6 1.8 %collective-permute-start.2 = (bf16[1152,128]{1,0:T(8,128)(2,1)S(1)}, bf16[1152,128]{1,0:T(8,128)(2,1)S(1)}, u32[]{:S(2)}, u32[]{:S(2)}) collective-permute-start(bf16[1152,128]{1,0:T(8,128)(2,1)S(1)} %pad_maximum_fusion.1), channel_id=1, source_target_pairs={{7,6},{2,7},{3,2},{0,3},{1,0},{4,1},{5,4},{8,5},{9,8},{12,9},{13,1... | collective-permute-start | bytes 884744 | tf_op jit(solution)/shard_map/ppermute | solution.py:267
  24.4 4.3 %collective-permute-done.1.sprev = bf16[1152,128]{1,0:T(8,128)(2,1)S(1)} collective-permute-done((bf16[1152,128]{1,0:T(8,128)(2,1)S(1)}, bf16[1152,128]{1,0:T(8,128)(2,1)S(1)}, u32[]{:S(2)}, u32[]{:S(2)}) %collective-permute-start.1) | collective-permute-done | bytes 294944 | tf_op jit(solution)/shard_map/ppermute | solution.py:266
  28.7 0.0 collective-permute-done.2.snext
  28.7 1.5 %products.1 = f32[16,16]{1,0:T(8,128)S(1)} custom-call(bf16[1152,128]{1,0:T(8,128)(2,1)S(1)} %collective-permute-done.1.sprev, bf16[16,96,128]{2,1,0:T(8,128)(2,1)S(1)} %all-to-all-done.sown, bf16[192,128]{1,0:T(8,128)(2,1)S(1)} %collective-permute-done.gown, bf16[1152,128]{1,0:T(8,128)(2,1)S(1)} %collective-permute-done.2.snext), custom_call_target="tpu_custom_call" | custom-call | tf_op jit(solution)/shard_map/products/pallas_call | solution.py:268
  30.3 10.0 %all_to_all.14 = f32[16,1,16]{2,1,0:T(1,128)S(1)} all-to-all(f32[16,1,16]{2,1,0:T(1,128)S(1)} %bitcast.14), channel_id=1, replica_groups=mesh['grp'=2,'blk'=16] {'blk'}, dimensions={0} | all-to-all | bytes 2048 | tf_op jit(solution)/shard_map/all_to_all | solution.py:282
  40.3 0.5 %reduce_sum.9 = f32[16]{0:T(128)} reduce(f32[16,1,16]{2,1,0:T(1,128)S(1)} %all_to_all.14, f32[]{:T(128)} %constant.0.clone.1), dimensions={0,1}, to_apply=%region_0.0 | reduce | flops 240 | bytes 1092 | tf_op jit(solution)/shard_map/reduce_sum | solution.py:283
  (3 shorter events, 0.0 us)
Async XLA Ops:
  2.4 20.1 %all-to-all-start = ((bf16[16,96,128]{2,1,0:T(8,128)(2,1)}), bf16[16,96,128]{2,1,0:T(8,128)(2,1)S(1)}, u32[]{:S(2)}, u32[]{:S(2)}) async-start(bf16[16,96,128]{2,1,0:T(8,128)(2,1)} %pack.1), calls=%async_computation | async-start | bytes 786432 | tf_op jit(solution)/shard_map/all_to_all | solution.py:261
  11.5 7.9 %collective-permute-start = (bf16[192,128]{1,0:T(8,128)(2,1)}, bf16[192,128]{1,0:T(8,128)(2,1)S(1)}, u32[]{:S(2)}, u32[]{:S(2)}) collective-permute-start(bf16[192,128]{1,0:T(8,128)(2,1)} %prep.1), channel_id=1, source_target_pairs={{0,6},{1,7},{2,2},{3,3},{4,0},{5,1},{6,4},{7,5},{8,8},{9,9},{10,12... | collective-permute-start | bytes 147464 | tf_op jit(solution)/shard_map/ppermute | solution.py:260
  22.5 6.2 %collective-permute-start.1 = (bf16[1152,128]{1,0:T(8,128)(2,1)S(1)}, bf16[1152,128]{1,0:T(8,128)(2,1)S(1)}, u32[]{:S(2)}, u32[]{:S(2)}) collective-permute-start(bf16[1152,128]{1,0:T(8,128)(2,1)S(1)} %pad_maximum_fusion), channel_id=1, source_target_pairs={{6,7},{7,2},{2,3},{3,0},{0,1},{1,4},{4,5},{5,8},{8,9},{9,12},{12,1... | collective-permute-start | bytes 884744 | tf_op jit(solution)/shard_map/ppermute | solution.py:266
  22.6 6.1 %collective-permute-start.2 = (bf16[1152,128]{1,0:T(8,128)(2,1)S(1)}, bf16[1152,128]{1,0:T(8,128)(2,1)S(1)}, u32[]{:S(2)}, u32[]{:S(2)}) collective-permute-start(bf16[1152,128]{1,0:T(8,128)(2,1)S(1)} %pad_maximum_fusion.1), channel_id=1, source_target_pairs={{7,6},{2,7},{3,2},{0,3},{1,0},{4,1},{5,4},{8,5},{9,8},{12,9},{13,1... | collective-permute-start | bytes 884744 | tf_op jit(solution)/shard_map/ppermute | solution.py:267

commit v7 on v6

--- a/solution.py
+++ b/solution.py
@@ -11,6 +11,7 @@
 EDGE = 64
 HALF = 32
 LANES = 128
+PITCH = 40
 VMEM = pl.BlockSpec(memory_space=pltpu.VMEM)
 SMEM = pl.BlockSpec(memory_space=pltpu.SMEM)
 
@@ -39,12 +40,12 @@
         mask = jnp.broadcast_to(jnp.sum(mask, axis=1, keepdims=True), (blocks, LANES))
         copies[a].wait()
         for c in range(HALF):
-            rows_ref[a, pl.ds(c, blocks, stride=HALF), :] = (
+            rows_ref[a, pl.ds(c, blocks, stride=PITCH), :] = (
                 x_ref[a, :, c * LANES : (c + 1) * LANES].astype(jnp.float32) * mask
             )
         part = pl.ds(a * HALF, HALF)
         for d, b in enumerate(works_on):
-            out_ref[d, part, :] = rows_ref[a, pl.ds(b * HALF, HALF), :].astype(jnp.bfloat16)
+            out_ref[d, part, :] = rows_ref[a, pl.ds(b * PITCH, HALF), :].astype(jnp.bfloat16)
         sent.append(
             pltpu.make_async_copy(out_ref.at[:, part, :], out_hbm.at[:, part, :], sems.at[4 + a])
         )
@@ -57,7 +58,7 @@
     own = lax.axis_index("blk")
     for k, ref in enumerate((occ_ref, vir_ref)):
         for c in range(HALF):
-            rows_ref[k, pl.ds(c, 3, stride=HALF), :] = ref[
+            rows_ref[k, pl.ds(c, 3, stride=PITCH), :] = ref[
                 :, c * LANES : (c + 1) * LANES
             ].astype(jnp.float32)
     lane = lax.broadcasted_iota(jnp.int32, (HALF, LANES), 1)
@@ -68,9 +69,9 @@
     vir, occ = [], []
     for a in range(3):
         used = (col < count[lax.rem(own + (total + a - 1), total)]).astype(jnp.float32)
-        v = rows_ref[1, pl.ds(a * HALF, HALF), :] * (used * vmask[a, own].astype(jnp.float32))
+        v = rows_ref[1, pl.ds(a * PITCH, HALF), :] * (used * vmask[a, own].astype(jnp.float32))
         vir += [v * keep[0], pltpu.roll(v, EDGE, 1) * keep[1]]
-        o = rows_ref[0, pl.ds(a * HALF, HALF), :] * (used * omask[a, own].astype(jnp.float32))
+        o = rows_ref[0, pl.ds(a * PITCH, HALF), :] * (used * omask[a, own].astype(jnp.float32))
         occ.append((pltpu.roll(o, EDGE, 1) * keep[0], o * keep[1]))
     vir += [jnp.zeros((HALF, LANES), jnp.float32)] * 2
     first = jnp.concatenate(vir[:4], 0).T[:EDGE]
@@ -242,7 +243,7 @@
         scratch_shapes=[
             pltpu.VMEM((3, total, EDGE * EDGE), jnp.bfloat16),
             pltpu.VMEM((3, total), jnp.int32),
-            pltpu.VMEM((3, total * HALF, LANES), jnp.float32),
+            pltpu.VMEM((3, total * PITCH, LANES), jnp.float32),
             pltpu.VMEM((members, 3 * HALF, LANES), jnp.bfloat16),
             pltpu.SemaphoreType.DMA((7,)),
         ],
@@ -254,7 +255,7 @@
         out_shape=jax.ShapeDtypeStruct((6 * HALF, LANES), jnp.bfloat16),
         in_specs=[SMEM] * 3 + [VMEM] * 2,
         out_specs=VMEM,
-        scratch_shapes=[pltpu.VMEM((2, 3 * HALF, LANES), jnp.float32)],
+        scratch_shapes=[pltpu.VMEM((2, 3 * PITCH, LANES), jnp.float32)],
         name="prep",
     )(omask.T, vmask.T, count, occupied[0], virtual[0])
     greens = lax.ppermute(greens, "blk", list(enumerate(order)))

time: 41.2 us -> 40.7 us (0.988)
  Pallas kernels: 5.58 us -> 5.07 us
    pallas_call x1, Pallas kernels: 2.35 us -> 1.87 us  [body(): pl.pallas_call(functools.partial(pack_kernel, works_on), out_shape=jax.Sh...]
where the time goes in v7:
time: 40.7 us; the launch traced here: 40.3 us
  starting transfers between devices  14 us (34%)
  waiting for transfers between devices  10.6 us (26%)
  blocking collectives  10 us (25%)
  Pallas kernels  5.07 us (12%)
  other arithmetic  0.59 us (1%)
    all_to_all x1, blocking collectives, body(): mine = lax.all_to_all(part, 'blk', split_axis=0, concat_axis=0, tiled=True)  10 us
    all_to_all x1, starting transfers between devices, body(): own = lax.all_to_all(rows, 'blk', split_axis=0, concat_axis=0, tiled=True)  7.4 us
    ppermute x1, starting transfers between devices, body(): greens = lax.ppermute(greens, 'blk', list(enumerate(order)))  4.72 us
    ppermute x1, waiting for transfers between devices, body(): sprev = lax.ppermute(later, 'blk', forth)  4.33 us
    ppermute x1, waiting for transfers between devices, body(): greens = lax.ppermute(greens, 'blk', list(enumerate(order)))  3.2 us
    all_to_all x1, waiting for transfers between devices, body(): own = lax.all_to_all(rows, 'blk', split_axis=0, concat_axis=0, tiled=True)  3.07 us
    pallas_call x1, Pallas kernels, body(): pl.pallas_call(functools.partial(pack_kernel, works_on), out_shape=jax.Sh...  1.87 us
    ppermute x1, starting transfers between devices, body(): snext = lax.ppermute(early, 'blk', back)  1.78 us
  transfers between devices with their start and end apart: 4, of which 3 were waited for; matrix products, arithmetic and copies ran while one was open for 0% of the time, Pallas kernels for 4%

profile of v7, /device:TPU:0, one launch (start us, length us, event | category | flops | bytes accessed | tf_op | source)
XLA Modules:
  0.0 40.3 jit_solution(390097113885456881)
XLA Ops:
  0.0 1.9 %pack.1 = bf16[16,96,128]{2,1,0:T(8,128)(2,1)} custom-call(bf16[3,16,4096]{2,1,0:T(8,128)(2,1)} %bitcast.17, s32[3,16]{1,0:T(4,128)} %bitcast.20), custom_call_target="tpu_custom_call" | custom-call | tf_op jit(solution)/shard_map/pack/pallas_call | solution.py:238
  1.9 7.4 %all-to-all-start = ((bf16[16,96,128]{2,1,0:T(8,128)(2,1)}), bf16[16,96,128]{2,1,0:T(8,128)(2,1)S(1)}, u32[]{:S(2)}, u32[]{:S(2)}) async-start(bf16[16,96,128]{2,1,0:T(8,128)(2,1)} %pack.1), calls=%async_computation | async-start | bytes 786432 | tf_op jit(solution)/shard_map/all_to_all | solution.py:262
  9.3 1.7 %prep.1 = bf16[192,128]{1,0:T(8,128)(2,1)} custom-call(s32[3,16]{1,0:T(4,128)} %bitcast.21, s32[3,16]{1,0:T(4,128)} %bitcast.22, s32[16]{0:T(128)} %count.1, bf16[3,4096]{1,0:T(4,128)(2,1)} %bitcast.18, bf16[3,4096]{1,0:T(4,128)(2,1)} %bitcast.19), custom_call_target="tpu_custom_call" | custom-call | tf_op jit(solution)/shard_map/prep/pallas_call | solution.py:253
  11.0 4.7 %collective-permute-start = (bf16[192,128]{1,0:T(8,128)(2,1)}, bf16[192,128]{1,0:T(8,128)(2,1)S(1)}, u32[]{:S(2)}, u32[]{:S(2)}) collective-permute-start(bf16[192,128]{1,0:T(8,128)(2,1)} %prep.1), channel_id=1, source_target_pairs={{0,6},{1,7},{2,2},{3,3},{4,0},{5,1},{6,4},{7,5},{8,8},{9,9},{10,12... | collective-permute-start | bytes 147464 | tf_op jit(solution)/shard_map/ppermute | solution.py:261
  15.7 3.2 %collective-permute-done.gown = bf16[192,128]{1,0:T(8,128)(2,1)S(1)} collective-permute-done((bf16[192,128]{1,0:T(8,128)(2,1)}, bf16[192,128]{1,0:T(8,128)(2,1)S(1)}, u32[]{:S(2)}, u32[]{:S(2)}) %collective-permute-start) | collective-permute-done | bytes 49184 | tf_op jit(solution)/shard_map/ppermute | solution.py:261
  18.9 3.1 %all-to-all-done.sown = bf16[16,96,128]{2,1,0:T(8,128)(2,1)S(1)} async-done(((bf16[16,96,128]{2,1,0:T(8,128)(2,1)}), bf16[16,96,128]{2,1,0:T(8,128)(2,1)S(1)}, u32[]{:S(2)}, u32[]{:S(2)}) %all-to-all-start) | async-done | bytes 393248 | tf_op jit(solution)/shard_map/all_to_all | solution.py:262
  21.9 0.1 fusion
  22.0 0.1 collective-permute-start.1
  22.1 1.8 %collective-permute-start.2 = (bf16[1152,128]{1,0:T(8,128)(2,1)S(1)}, bf16[1152,128]{1,0:T(8,128)(2,1)S(1)}, u32[]{:S(2)}, u32[]{:S(2)}) collective-permute-start(bf16[1152,128]{1,0:T(8,128)(2,1)S(1)} %pad_maximum_fusion.1), channel_id=1, source_target_pairs={{7,6},{2,7},{3,2},{0,3},{1,0},{4,1},{5,4},{8,5},{9,8},{12,9},{13,1... | collective-permute-start | bytes 884744 | tf_op jit(solution)/shard_map/ppermute | solution.py:268
  23.9 4.3 %collective-permute-done.1.sprev = bf16[1152,128]{1,0:T(8,128)(2,1)S(1)} collective-permute-done((bf16[1152,128]{1,0:T(8,128)(2,1)S(1)}, bf16[1152,128]{1,0:T(8,128)(2,1)S(1)}, u32[]{:S(2)}, u32[]{:S(2)}) %collective-permute-start.1) | collective-permute-done | bytes 294944 | tf_op jit(solution)/shard_map/ppermute | solution.py:267
  28.2 0.0 collective-permute-done.2.snext
  28.2 1.5 %products.1 = f32[16,16]{1,0:T(8,128)S(1)} custom-call(bf16[1152,128]{1,0:T(8,128)(2,1)S(1)} %collective-permute-done.1.sprev, bf16[16,96,128]{2,1,0:T(8,128)(2,1)S(1)} %all-to-all-done.sown, bf16[192,128]{1,0:T(8,128)(2,1)S(1)} %collective-permute-done.gown, bf16[1152,128]{1,0:T(8,128)(2,1)S(1)} %collective-permute-done.2.snext), custom_call_target="tpu_custom_call" | custom-call | tf_op jit(solution)/shard_map/products/pallas_call | solution.py:269
  29.8 10.0 %all_to_all.14 = f32[16,1,16]{2,1,0:T(1,128)S(1)} all-to-all(f32[16,1,16]{2,1,0:T(1,128)S(1)} %bitcast.14), channel_id=1, replica_groups=mesh['grp'=2,'blk'=16] {'blk'}, dimensions={0} | all-to-all | bytes 2048 | tf_op jit(solution)/shard_map/all_to_all | solution.py:283
  39.8 0.5 %reduce_sum.9 = f32[16]{0:T(128)} reduce(f32[16,1,16]{2,1,0:T(1,128)S(1)} %all_to_all.14, f32[]{:T(128)} %constant.0.clone.1), dimensions={0,1}, to_apply=%region_0.0 | reduce | flops 240 | bytes 1092 | tf_op jit(solution)/shard_map/reduce_sum | solution.py:284
  (3 shorter events, 0.0 us)
Async XLA Ops:
  1.9 20.1 %all-to-all-start = ((bf16[16,96,128]{2,1,0:T(8,128)(2,1)}), bf16[16,96,128]{2,1,0:T(8,128)(2,1)S(1)}, u32[]{:S(2)}, u32[]{:S(2)}) async-start(bf16[16,96,128]{2,1,0:T(8,128)(2,1)} %pack.1), calls=%async_computation | async-start | bytes 786432 | tf_op jit(solution)/shard_map/all_to_all | solution.py:262
  11.0 7.9 %collective-permute-start = (bf16[192,128]{1,0:T(8,128)(2,1)}, bf16[192,128]{1,0:T(8,128)(2,1)S(1)}, u32[]{:S(2)}, u32[]{:S(2)}) collective-permute-start(bf16[192,128]{1,0:T(8,128)(2,1)} %prep.1), channel_id=1, source_target_pairs={{0,6},{1,7},{2,2},{3,3},{4,0},{5,1},{6,4},{7,5},{8,8},{9,9},{10,12... | collective-permute-start | bytes 147464 | tf_op jit(solution)/shard_map/ppermute | solution.py:261
  22.0 6.2 %collective-permute-start.1 = (bf16[1152,128]{1,0:T(8,128)(2,1)S(1)}, bf16[1152,128]{1,0:T(8,128)(2,1)S(1)}, u32[]{:S(2)}, u32[]{:S(2)}) collective-permute-start(bf16[1152,128]{1,0:T(8,128)(2,1)S(1)} %pad_maximum_fusion), channel_id=1, source_target_pairs={{6,7},{7,2},{2,3},{3,0},{0,1},{1,4},{4,5},{5,8},{8,9},{9,12},{12,1... | collective-permute-start | bytes 884744 | tf_op jit(solution)/shard_map/ppermute | solution.py:267
  22.1 6.1 %collective-permute-start.2 = (bf16[1152,128]{1,0:T(8,128)(2,1)S(1)}, bf16[1152,128]{1,0:T(8,128)(2,1)S(1)}, u32[]{:S(2)}, u32[]{:S(2)}) collective-permute-start(bf16[1152,128]{1,0:T(8,128)(2,1)S(1)} %pad_maximum_fusion.1), channel_id=1, source_target_pairs={{7,6},{2,7},{3,2},{0,3},{1,0},{4,1},{5,4},{8,5},{9,8},{12,9},{13,1... | collective-permute-start | bytes 884744 | tf_op jit(solution)/shard_map/ppermute | solution.py:268

commit v8 on v7

--- a/solution.py
+++ b/solution.py
@@ -35,7 +35,7 @@
     )
     masks.wait()
     sent = []
-    for a in range(3):
+    for a in (1, 0, 2):
         mask = jnp.where(diagonal, imask_ref[pl.ds(a, 1), :].astype(jnp.float32), 0.0)
         mask = jnp.broadcast_to(jnp.sum(mask, axis=1, keepdims=True), (blocks, LANES))
         copies[a].wait()
@@ -43,13 +43,18 @@
             rows_ref[a, pl.ds(c, blocks, stride=PITCH), :] = (
                 x_ref[a, :, c * LANES : (c + 1) * LANES].astype(jnp.float32) * mask
             )
-        part = pl.ds(a * HALF, HALF)
         for d, b in enumerate(works_on):
-            out_ref[d, part, :] = rows_ref[a, pl.ds(b * PITCH, HALF), :].astype(jnp.bfloat16)
-        sent.append(
-            pltpu.make_async_copy(out_ref.at[:, part, :], out_hbm.at[:, part, :], sems.at[4 + a])
-        )
-        sent[a].start()
+            to = 2 - a if b % 2 else a
+            out_ref[d, pl.ds(to * HALF, HALF), :] = rows_ref[a, pl.ds(b * PITCH, HALF), :].astype(
+                jnp.bfloat16
+            )
+        for to in {0: (), 1: (1,), 2: (0, 2)}[a]:
+            part = pl.ds(to * HALF, HALF)
+            copy = pltpu.make_async_copy(
+                out_ref.at[:, part, :], out_hbm.at[:, part, :], sems.at[4 + to]
+            )
+            copy.start()
+            sent.append(copy)
     for copy in sent:
         copy.wait()
 
@@ -76,30 +81,32 @@
     vir += [jnp.zeros((HALF, LANES), jnp.float32)] * 2
     first = jnp.concatenate(vir[:4], 0).T[:EDGE]
     second = jnp.concatenate(vir[4:], 0).T[:EDGE]
+    odd = lax.rem(own, 2)
     for a, turned in enumerate((first, pltpu.roll(first, EDGE, 1), second)):
+        at = pl.multiple_of((a + odd * (2 - 2 * a)) * EDGE, EDGE)
         for par in range(2):
-            out_ref[pl.ds((2 * a + par) * HALF, HALF), :] = jnp.where(
+            out_ref[pl.ds(at + par * HALF, HALF), :] = jnp.where(
                 left, turned[par * HALF : (par + 1) * HALF], occ[a][par]
             ).astype(jnp.bfloat16)
 
 
 def main_kernel(
-    scale, rows, sprev, sown, gown, snext, out_ref, occ_ref, far_ref, half_ref, full_ref
+    scale, rows, schip, sown, gown, score, out_ref, occ_ref, far_ref, half_ref, full_ref
 ):
     pair = 2 * HALF
 
     def slab(s, q, a):
         if s == 0:
-            return sprev[pl.ds(q * pair + (a - 1) * HALF, HALF), :]
+            return schip[pl.ds(q * pair + (2 - a) * HALF, HALF), :]
         if s == 2:
-            return snext[pl.ds(q * pair + a * HALF, HALF), :]
+            return score[pl.ds(q * pair + (1 - a) * HALF, HALF), :]
         return sown[q, pl.ds(a * HALF, HALF), :]
 
     def green(s, a):
         if s == 0:
-            return sprev[pl.ds(rows * pair + (a - 1) * EDGE, EDGE), :]
+            return schip[pl.ds(rows * pair + (2 - a) * EDGE, EDGE), :]
         if s == 2:
-            return snext[pl.ds(rows * pair + a * EDGE, EDGE), :]
+            return score[pl.ds(rows * pair + (1 - a) * EDGE, EDGE), :]
         return gown[pl.ds(a * EDGE, EDGE), :]
 
     none = jnp.zeros((EDGE, EDGE), jnp.bfloat16)
@@ -260,12 +267,12 @@
     )(omask.T, vmask.T, count, occupied[0], virtual[0])
     greens = lax.ppermute(greens, "blk", list(enumerate(order)))
     own = lax.all_to_all(rows, "blk", split_axis=0, concat_axis=0, tiled=True)
-    forth = [(order[j], order[(j + 1) % members]) for j in range(members)]
-    back = [(order[(j + 1) % members], order[j]) for j in range(members)]
-    later = jnp.concatenate([own[:, HALF:].reshape(-1, LANES), greens[EDGE:]], 0)
-    early = jnp.concatenate([own[:, : 2 * HALF].reshape(-1, LANES), greens[: 2 * EDGE]], 0)
-    sprev = lax.ppermute(later, "blk", forth)
-    snext = lax.ppermute(early, "blk", back)
+    core_pairs = [(order[j], order[j + 1 - 2 * (j % 2)]) for j in range(members)]
+    chip_pairs = [(order[j], order[(j - 1 + 2 * (j % 2)) % members]) for j in range(members)]
+    to_chip = jnp.concatenate([own[:, : 2 * HALF].reshape(-1, LANES), greens[: 2 * EDGE]], 0)
+    to_core = jnp.concatenate([own[:, HALF:].reshape(-1, LANES), greens[EDGE:]], 0)
+    schip = lax.ppermute(to_chip, "blk", chip_pairs)
+    score = lax.ppermute(to_core, "blk", core_pairs)
     part = pl.pallas_call(
         functools.partial(main_kernel, 1.0 / math.sqrt(5 * EDGE * EDGE * total), members),
         out_shape=jax.ShapeDtypeStruct((members, members), jnp.float32),
@@ -279,7 +286,7 @@
         ],
         compiler_params=pltpu.CompilerParams(vmem_limit_bytes=48 * 1024 * 1024),
         name="products",
-    )(sprev, own, greens, snext)
+    )(schip, own, greens, score)
     mine = lax.all_to_all(part, "blk", split_axis=0, concat_axis=0, tiled=True)
     return jnp.sum(mine, axis=0, keepdims=True)
 

time: 40.7 us -> 40.1 us (0.985)
  starting transfers between devices: 14 us -> 12.3 us
  waiting for transfers between devices: 10.6 us -> 12.2 us
  blocking collectives: 10 us -> 9.26 us
    ppermute x2, waiting for transfers between devices: 4.33 us -> 5.96 us  [the longest x1 5.95 us: body(): schip = lax.ppermute(to_chip, 'blk', chip_pairs)]
    ppermute x2, starting transfers between devices: 1.84 us -> 0.23 us  [the longest x1 0.16 us: body(): schip = lax.ppermute(to_chip, 'blk', chip_pairs)]
    all_to_all x1, blocking collectives: 10 us -> 9.26 us  [body(): mine = lax.all_to_all(part, 'blk', split_axis=0, concat_axis=0, tiled=True)]
where the time goes in v8:
time: 40.1 us; the launch traced here: 39.7 us
  starting transfers between devices  12.3 us (31%)
  waiting for transfers between devices  12.2 us (30%)
  blocking collectives  9.26 us (23%)
  Pallas kernels  5.18 us (13%)
  other arithmetic  0.59 us (1%)
    all_to_all x1, blocking collectives, body(): mine = lax.all_to_all(part, 'blk', split_axis=0, concat_axis=0, tiled=True)  9.26 us
    all_to_all x1, starting transfers between devices, body(): own = lax.all_to_all(rows, 'blk', split_axis=0, concat_axis=0, tiled=True)  7.4 us
    ppermute x1, waiting for transfers between devices, body(): schip = lax.ppermute(to_chip, 'blk', chip_pairs)  5.95 us
    ppermute x1, starting transfers between devices, body(): greens = lax.ppermute(greens, 'blk', list(enumerate(order)))  4.72 us
    ppermute x1, waiting for transfers between devices, body(): greens = lax.ppermute(greens, 'blk', list(enumerate(order)))  3.2 us
    all_to_all x1, waiting for transfers between devices, body(): own = lax.all_to_all(rows, 'blk', split_axis=0, concat_axis=0, tiled=True)  3.07 us
    pallas_call x1, Pallas kernels, body(): pl.pallas_call(functools.partial(pack_kernel, works_on), out_shape=jax.Sh...  1.97 us
    pallas_call x1, Pallas kernels, body(): pl.pallas_call(functools.partial(prep_kernel, total), out_shape=jax.Shape...  1.67 us
  transfers between devices with their start and end apart: 4, of which 3 were waited for; matrix products, arithmetic and copies ran while one was open for 0% of the time, Pallas kernels for 4%

profile of v8, /device:TPU:0, one launch (start us, length us, event | category | flops | bytes accessed | tf_op | source)
XLA Modules:
  0.0 39.7 jit_solution(15424867875352250599)
XLA Ops:
  0.0 2.0 %pack.1 = bf16[16,96,128]{2,1,0:T(8,128)(2,1)} custom-call(bf16[3,16,4096]{2,1,0:T(8,128)(2,1)} %bitcast.17, s32[3,16]{1,0:T(4,128)} %bitcast.20), custom_call_target="tpu_custom_call" | custom-call | tf_op jit(solution)/shard_map/pack/pallas_call | solution.py:245
  2.0 7.4 %all-to-all-start = ((bf16[16,96,128]{2,1,0:T(8,128)(2,1)}), bf16[16,96,128]{2,1,0:T(8,128)(2,1)S(1)}, u32[]{:S(2)}, u32[]{:S(2)}) async-start(bf16[16,96,128]{2,1,0:T(8,128)(2,1)} %pack.1), calls=%async_computation | async-start | bytes 786432 | tf_op jit(solution)/shard_map/all_to_all | solution.py:269
  9.4 1.7 %prep.1 = bf16[192,128]{1,0:T(8,128)(2,1)} custom-call(s32[3,16]{1,0:T(4,128)} %bitcast.21, s32[3,16]{1,0:T(4,128)} %bitcast.22, s32[16]{0:T(128)} %count.1, bf16[3,4096]{1,0:T(4,128)(2,1)} %bitcast.18, bf16[3,4096]{1,0:T(4,128)(2,1)} %bitcast.19), custom_call_target="tpu_custom_call" | custom-call | tf_op jit(solution)/shard_map/prep/pallas_call | solution.py:260
  11.1 4.7 %collective-permute-start = (bf16[192,128]{1,0:T(8,128)(2,1)}, bf16[192,128]{1,0:T(8,128)(2,1)S(1)}, u32[]{:S(2)}, u32[]{:S(2)}) collective-permute-start(bf16[192,128]{1,0:T(8,128)(2,1)} %prep.1), channel_id=1, source_target_pairs={{0,6},{1,7},{2,2},{3,3},{4,0},{5,1},{6,4},{7,5},{8,8},{9,9},{10,12... | collective-permute-start | bytes 147464 | tf_op jit(solution)/shard_map/ppermute | solution.py:268
  15.8 3.2 %collective-permute-done.gown = bf16[192,128]{1,0:T(8,128)(2,1)S(1)} collective-permute-done((bf16[192,128]{1,0:T(8,128)(2,1)}, bf16[192,128]{1,0:T(8,128)(2,1)S(1)}, u32[]{:S(2)}, u32[]{:S(2)}) %collective-permute-start) | collective-permute-done | bytes 49184 | tf_op jit(solution)/shard_map/ppermute | solution.py:268
  19.0 3.1 %all-to-all-done.sown = bf16[16,96,128]{2,1,0:T(8,128)(2,1)S(1)} async-done(((bf16[16,96,128]{2,1,0:T(8,128)(2,1)}), bf16[16,96,128]{2,1,0:T(8,128)(2,1)S(1)}, u32[]{:S(2)}, u32[]{:S(2)}) %all-to-all-start) | async-done | bytes 393248 | tf_op jit(solution)/shard_map/all_to_all | solution.py:269
  22.1 0.1 fusion
  22.1 0.2 collective-permute-start.1
  22.3 0.1 collective-permute-start.2
  22.4 6.0 %collective-permute-done.1.schip = bf16[1152,128]{1,0:T(8,128)(2,1)S(1)} collective-permute-done((bf16[1152,128]{1,0:T(8,128)(2,1)S(1)}, bf16[1152,128]{1,0:T(8,128)(2,1)S(1)}, u32[]{:S(2)}, u32[]{:S(2)}) %collective-permute-start.1) | collective-permute-done | bytes 294944 | tf_op jit(solution)/shard_map/ppermute | solution.py:274
  28.4 0.0 collective-permute-done.2.score
  28.4 1.5 %products.1 = f32[16,16]{1,0:T(8,128)S(1)} custom-call(bf16[1152,128]{1,0:T(8,128)(2,1)S(1)} %collective-permute-done.1.schip, bf16[16,96,128]{2,1,0:T(8,128)(2,1)S(1)} %all-to-all-done.sown, bf16[192,128]{1,0:T(8,128)(2,1)S(1)} %collective-permute-done.gown, bf16[1152,128]{1,0:T(8,128)(2,1)S(1)} %collective-permute-done.2.score), custom_call_target="tpu_custom_call" | custom-call | tf_op jit(solution)/shard_map/products/pallas_call | solution.py:276
  29.9 9.3 %all_to_all.14 = f32[16,1,16]{2,1,0:T(1,128)S(1)} all-to-all(f32[16,1,16]{2,1,0:T(1,128)S(1)} %bitcast.14), channel_id=1, replica_groups=mesh['grp'=2,'blk'=16] {'blk'}, dimensions={0} | all-to-all | bytes 2048 | tf_op jit(solution)/shard_map/all_to_all | solution.py:290
  39.2 0.5 %reduce_sum.9 = f32[16]{0:T(128)} reduce(f32[16,1,16]{2,1,0:T(1,128)S(1)} %all_to_all.14, f32[]{:T(128)} %constant.0.clone.1), dimensions={0,1}, to_apply=%region_0.0 | reduce | flops 240 | bytes 1092 | tf_op jit(solution)/shard_map/reduce_sum | solution.py:291
  (3 shorter events, 0.0 us)
Async XLA Ops:
  2.0 20.1 %all-to-all-start = ((bf16[16,96,128]{2,1,0:T(8,128)(2,1)}), bf16[16,96,128]{2,1,0:T(8,128)(2,1)S(1)}, u32[]{:S(2)}, u32[]{:S(2)}) async-start(bf16[16,96,128]{2,1,0:T(8,128)(2,1)} %pack.1), calls=%async_computation | async-start | bytes 786432 | tf_op jit(solution)/shard_map/all_to_all | solution.py:269
  11.1 7.9 %collective-permute-start = (bf16[192,128]{1,0:T(8,128)(2,1)}, bf16[192,128]{1,0:T(8,128)(2,1)S(1)}, u32[]{:S(2)}, u32[]{:S(2)}) collective-permute-start(bf16[192,128]{1,0:T(8,128)(2,1)} %prep.1), channel_id=1, source_target_pairs={{0,6},{1,7},{2,2},{3,3},{4,0},{5,1},{6,4},{7,5},{8,8},{9,9},{10,12... | collective-permute-start | bytes 147464 | tf_op jit(solution)/shard_map/ppermute | solution.py:268
  22.1 6.2 %collective-permute-start.1 = (bf16[1152,128]{1,0:T(8,128)(2,1)S(1)}, bf16[1152,128]{1,0:T(8,128)(2,1)S(1)}, u32[]{:S(2)}, u32[]{:S(2)}) collective-permute-start(bf16[1152,128]{1,0:T(8,128)(2,1)S(1)} %pad_maximum_fusion), channel_id=1, source_target_pairs={{6,11},{7,2},{2,7},{3,0},{0,3},{1,4},{4,1},{5,8},{8,5},{9,12},{12,... | collective-permute-start | bytes 884744 | tf_op jit(solution)/shard_map/ppermute | solution.py:274
  22.3 6.0 %collective-permute-start.2 = (bf16[1152,128]{1,0:T(8,128)(2,1)S(1)}, bf16[1152,128]{1,0:T(8,128)(2,1)S(1)}, u32[]{:S(2)}, u32[]{:S(2)}) collective-permute-start(bf16[1152,128]{1,0:T(8,128)(2,1)S(1)} %pad_maximum_fusion.1), channel_id=1, source_target_pairs={{6,7},{7,6},{2,3},{3,2},{0,1},{1,0},{4,5},{5,4},{8,9},{9,8},{12,13... | collective-permute-start | bytes 884744 | tf_op jit(solution)/shard_map/ppermute | solution.py:275

commit v9 on v8

--- a/solution.py
+++ b/solution.py
@@ -14,6 +14,7 @@
 PITCH = 40
 VMEM = pl.BlockSpec(memory_space=pltpu.VMEM)
 SMEM = pl.BlockSpec(memory_space=pltpu.SMEM)
+NT = (((1,), (1,)), ((), ()))
 
 
 def block_order(count):
@@ -90,119 +91,31 @@
             ).astype(jnp.bfloat16)
 
 
-def main_kernel(
-    scale, rows, schip, sown, gown, score, out_ref, occ_ref, far_ref, half_ref, full_ref
-):
-    pair = 2 * HALF
-
-    def slab(s, q, a):
-        if s == 0:
-            return schip[pl.ds(q * pair + (2 - a) * HALF, HALF), :]
-        if s == 2:
-            return score[pl.ds(q * pair + (1 - a) * HALF, HALF), :]
-        return sown[q, pl.ds(a * HALF, HALF), :]
-
-    def green(s, a):
-        if s == 0:
-            return schip[pl.ds(rows * pair + (2 - a) * EDGE, EDGE), :]
-        if s == 2:
-            return score[pl.ds(rows * pair + (1 - a) * EDGE, EDGE), :]
-        return gown[pl.ds(a * EDGE, EDGE), :]
-
-    none = jnp.zeros((EDGE, EDGE), jnp.bfloat16)
-    near = [green(0, 2)[:, :EDGE], green(1, 1)[:, :EDGE], green(2, 0)[:, :EDGE]]
-    vir = [
-        jnp.concatenate(
-            [
-                jnp.concatenate(near[:2], 1),
-                jnp.concatenate([none, green(1, 2)[:, :EDGE]], 1),
-            ],
-            0,
-        ),
-        jnp.concatenate(near, 1),
-        jnp.concatenate(
-            [
-                jnp.concatenate(near[1:], 1),
-                jnp.concatenate([green(1, 0)[:, :EDGE], none], 1),
-            ],
-            0,
-        ),
-    ]
-    used = ({0: 1, 1: 2}, {0: 0, 1: 1, 2: 2}, {1: 0, 2: 1})
-    for s in range(3):
-        for t in range(3):
-            for half in range(2):
-                at = pl.ds((half * 3 + s) * EDGE, EDGE)
-                to = pl.ds(t * LANES, LANES)
-                if t in used[s]:
-                    o = green(s, used[s][t])[:, EDGE:]
-                    occ_ref[at, to] = jnp.concatenate([none, o] if half else [o, none], 1)
-                else:
-                    occ_ref[at, to] = jnp.zeros((EDGE, LANES), jnp.bfloat16)
+def halves(slab, rows_at, j):
+    even, odd = [], []
+    for k in range(j, j + 2):
+        one, two = slab(2 * k, *rows_at), slab(2 * k + 1, *rows_at)
+        even.append(jnp.concatenate([one[:, :EDGE], two[:, :EDGE]], 1))
+        odd.append(jnp.concatenate([one[:, EDGE:], two[:, EDGE:]], 1))
+    return [jnp.concatenate(even, 1), jnp.concatenate(odd, 1)]
+
+
+def unfold(block, j, g, half, full_ref):
+    left = lax.broadcasted_iota(jnp.int32, (HALF, LANES), 1) < EDGE
+    place = pl.ds(g * HALF, HALF)
     for k in range(2):
-        o = green(1, 2 * k)[:, EDGE:]
-        far_ref[k] = jnp.concatenate(
-            [jnp.concatenate([o, none], 1), jnp.concatenate([none, o], 1)], 0
+        even = block[:HALF, k * LANES : (k + 1) * LANES]
+        odd = block[HALF:, k * LANES : (k + 1) * LANES]
+        first = 2 * (j + 2 * k) + half
+        full_ref[first, place, :] = jnp.where(left, even, pltpu.roll(odd, EDGE, 1)).astype(
+            jnp.bfloat16
         )
-
-    members = (((0, 1), (1, 0)), ((0, 2), (1, 1), (2, 0)), ((1, 2), (2, 1)))
-    for j in range(0, rows // 2, 2):
-
-        def side(s, a):
-            even, odd = [], []
-            for k in range(j, j + 2):
-                one, two = slab(s, 2 * k, a), slab(s, 2 * k + 1, a)
-                even.append(jnp.concatenate([one[:, :EDGE], two[:, :EDGE]], 1))
-                odd.append(jnp.concatenate([one[:, EDGE:], two[:, EDGE:]], 1))
-            return [jnp.concatenate(even, 1), jnp.concatenate(odd, 1)]
-
-        for t in range(3):
-            parts = []
-            for s, a in members[t]:
-                parts += side(s, a)
-            both = jnp.dot(vir[t], jnp.concatenate(parts, 0), preferred_element_type=jnp.float32)
-            both = both.astype(jnp.bfloat16)
-            for k in range(2):
-                at = pl.ds((j + k) * EDGE, EDGE)
-                piece = both[:, k * LANES : (k + 1) * LANES]
-                half_ref[at, pl.ds(t * LANES, LANES)] = piece[:EDGE]
-                if t != 1:
-                    half_ref[at, pl.ds((3 + t // 2) * LANES, LANES)] = piece[EDGE:]
-
-    left = lax.broadcasted_iota(jnp.int32, (HALF, LANES), 1) < EDGE
-    for j in range(0, rows // 2, 4):
-        at = pl.ds(j * EDGE, 4 * EDGE)
-        nt = (((1,), (1,)), ((), ()))
-        full = lax.dot_general(
-            occ_ref[...], half_ref[at, pl.ds(0, 3 * LANES)], nt, preferred_element_type=jnp.float32
+        full_ref[first + 2, place, :] = jnp.where(left, pltpu.roll(even, EDGE, 1), odd).astype(
+            jnp.bfloat16
         )
-        far = [
-            lax.dot_general(
-                far_ref[k],
-                half_ref[at, pl.ds((3 + k) * LANES, LANES)],
-                nt,
-                preferred_element_type=jnp.float32,
-            )
-            for k in range(2)
-        ]
-        for half in range(2):
-            for g in range(5):
-                if g < 3:
-                    block = full[(half * 3 + g) * EDGE : (half * 3 + g + 1) * EDGE]
-                else:
-                    block = far[g - 3][half * EDGE : (half + 1) * EDGE]
-                for k in range(2):
-                    even = block[:HALF, k * LANES : (k + 1) * LANES]
-                    odd = block[HALF:, k * LANES : (k + 1) * LANES]
-                    first = 2 * (j + 2 * k) + half
-                    place = pl.ds(g * HALF, HALF)
-                    full_ref[first, place, :] = jnp.where(
-                        left, even, pltpu.roll(odd, EDGE, 1)
-                    ).astype(jnp.bfloat16)
-                    full_ref[first + 2, place, :] = jnp.where(
-                        left, pltpu.roll(even, EDGE, 1), odd
-                    ).astype(jnp.bfloat16)
-
+
+
+def inner(slabs, full_ref, rows, store):
     group = 16
     span = group * 16
     ri = lax.broadcasted_iota(jnp.int32, (span, span), 0)
@@ -215,8 +128,8 @@
     for p in range(0, rows, group):
         for q in range(0, rows, group):
             acc = None
-            for g, (s, a) in enumerate(((0, 2), (1, 1), (2, 0), (1, 2), (1, 0))):
-                lhs = [slab(s, k, a) for k in range(p, p + group)]
+            for g, slab in enumerate(slabs):
+                lhs = [slab(k) for k in range(p, p + group)]
                 lhs = [jnp.concatenate([x[:16], x[16:]], 1) for x in lhs]
                 rhs = [
                     full_ref[pl.ds(q, group), pl.ds(g * HALF + c * 16, 16), :].reshape(span, LANES)
@@ -225,15 +138,141 @@
                 one = lax.dot_general(
                     jnp.concatenate(lhs, 0),
                     jnp.concatenate(rhs, 1),
-                    (((1,), (1,)), ((), ())),
+                    NT,
                     preferred_element_type=jnp.float32,
                 )
                 acc = one if acc is None else acc + one
             kept = jnp.where(same, acc, 0.0).reshape(group, 16, span)
-            summed = jnp.sum(kept, axis=1)
-            out_ref[pl.ds(p, group), pl.ds(q, group)] = scale * jnp.dot(
-                summed, pick, preferred_element_type=jnp.float32, precision=lax.Precision.HIGHEST
-            )
+            store(
+                pl.ds(p, group),
+                pl.ds(q, group),
+                jnp.dot(
+                    jnp.sum(kept, axis=1),
+                    pick,
+                    preferred_element_type=jnp.float32,
+                    precision=lax.Precision.HIGHEST,
+                ),
+            )
+
+
+def readers(rows, schip, sown, gown, score):
+    pair = 2 * HALF
+
+    def slab(q, s, a):
+        if s == 0:
+            return schip[pl.ds(q * pair + (2 - a) * HALF, HALF), :]
+        if s == 2:
+            return score[pl.ds(q * pair + (1 - a) * HALF, HALF), :]
+        return sown[q, pl.ds(a * HALF, HALF), :]
+
+    def green(s, a):
+        if s == 0:
+            return schip[pl.ds(rows * pair + (2 - a) * EDGE, EDGE), :]
+        if s == 2:
+            return score[pl.ds(rows * pair + (1 - a) * EDGE, EDGE), :]
+        return gown[pl.ds(a * EDGE, EDGE), :]
+
+    return slab, green
+
+
+def early_kernel(rows, sown, gown, score, part_ref, right_ref, far_ref, half_ref, full_ref):
+    slab, green = readers(rows, None, sown, gown, score)
+    none = jnp.zeros((EDGE, EDGE), jnp.bfloat16)
+    for k in range(2):
+        o = green(1, 2 * k)[:, EDGE:]
+        far_ref[k] = jnp.concatenate(
+            [jnp.concatenate([o, none], 1), jnp.concatenate([none, o], 1)], 0
+        )
+    vir = jnp.concatenate(
+        [
+            jnp.concatenate([green(1, 1)[:, :EDGE], green(2, 0)[:, :EDGE]], 1),
+            jnp.concatenate([green(1, 0)[:, :EDGE], none], 1),
+        ],
+        0,
+    )
+    for j in range(0, rows // 2, 2):
+        low = jnp.dot(
+            green(1, 2)[:, :EDGE],
+            jnp.concatenate(halves(slab, (1, 0), j), 0),
+            preferred_element_type=jnp.float32,
+        ).astype(jnp.bfloat16)
+        high = jnp.dot(
+            vir,
+            jnp.concatenate(halves(slab, (1, 2), j) + halves(slab, (2, 1), j), 0),
+            preferred_element_type=jnp.float32,
+        ).astype(jnp.bfloat16)
+        for k in range(2):
+            at = pl.ds((j + k) * EDGE, EDGE)
+            lanes = slice(k * LANES, (k + 1) * LANES)
+            right_ref[at, :] = high[:EDGE, lanes]
+            half_ref[0, at, :] = low[:, lanes]
+            half_ref[1, at, :] = high[EDGE:, lanes]
+    for j in range(0, rows // 2, 4):
+        for k in range(2):
+            full = lax.dot_general(
+                far_ref[k],
+                half_ref[k, pl.ds(j * EDGE, 4 * EDGE), :],
+                NT,
+                preferred_element_type=jnp.float32,
+            )
+            for half in range(2):
+                unfold(full[half * EDGE : (half + 1) * EDGE], j, k, half, full_ref)
+
+    def store(p, q, sums):
+        part_ref[p, q] = sums
+
+    inner([lambda q: slab(q, 1, 2), lambda q: slab(q, 1, 0)], full_ref, rows, store)
+
+
+def main_kernel(
+    scale, rows, part_ref, right_ref, schip, sown, gown, score, out_ref, occ_ref, half_ref, full_ref
+):
+    slab, green = readers(rows, schip, sown, gown, score)
+    none = jnp.zeros((EDGE, EDGE), jnp.bfloat16)
+    near = [green(s, 2 - s)[:, :EDGE] for s in range(3)]
+    vir = [jnp.concatenate(near[:2], 1), jnp.concatenate(near, 1)]
+    used = ({0: 1, 1: 2}, {0: 0, 1: 1, 2: 2}, {1: 0, 2: 1})
+    for s in range(3):
+        for t in range(3):
+            for half in range(2):
+                at = pl.ds((half * 3 + s) * EDGE, EDGE)
+                to = pl.ds(t * LANES, LANES)
+                if t in used[s]:
+                    o = green(s, used[s][t])[:, EDGE:]
+                    occ_ref[at, to] = jnp.concatenate([none, o] if half else [o, none], 1)
+                else:
+                    occ_ref[at, to] = jnp.zeros((EDGE, LANES), jnp.bfloat16)
+
+    members = (((0, 1), (1, 0)), ((0, 2), (1, 1), (2, 0)))
+    for j in range(0, rows // 2, 2):
+        for t in range(2):
+            parts = []
+            for at in members[t]:
+                parts += halves(slab, at, j)
+            both = jnp.dot(vir[t], jnp.concatenate(parts, 0), preferred_element_type=jnp.float32)
+            both = both.astype(jnp.bfloat16)
+            for k in range(2):
+                half_ref[pl.ds((j + k) * EDGE, EDGE), pl.ds(t * LANES, LANES)] = both[
+                    :, k * LANES : (k + 1) * LANES
+                ]
+
+    for j in range(0, rows // 2, 4):
+        at = pl.ds(j * EDGE, 4 * EDGE)
+        full = lax.dot_general(
+            occ_ref[...],
+            jnp.concatenate([half_ref[at, :], right_ref[at, :]], 1),
+            NT,
+            preferred_element_type=jnp.float32,
+        )
+        for half in range(2):
+            for s in range(3):
+                block = full[(half * 3 + s) * EDGE : (half * 3 + s + 1) * EDGE]
+                unfold(block, j, s, half, full_ref)
+
+    def store(p, q, sums):
+        out_ref[p, q] = scale * (sums + part_ref[p, q])
+
+    inner([lambda q, s=s: slab(q, s, 2 - s) for s in range(3)], full_ref, rows, store)
 
 
 def body(integrals, occupied, virtual, imask, omask, vmask, count):
@@ -273,20 +312,35 @@
     to_core = jnp.concatenate([own[:, HALF:].reshape(-1, LANES), greens[EDGE:]], 0)
     schip = lax.ppermute(to_chip, "blk", chip_pairs)
     score = lax.ppermute(to_core, "blk", core_pairs)
+    early, right = pl.pallas_call(
+        functools.partial(early_kernel, members),
+        out_shape=(
+            jax.ShapeDtypeStruct((members, members), jnp.float32),
+            jax.ShapeDtypeStruct((members // 2 * EDGE, LANES), jnp.bfloat16),
+        ),
+        in_specs=[VMEM] * 3,
+        out_specs=(VMEM, VMEM),
+        scratch_shapes=[
+            pltpu.VMEM((2, 2 * EDGE, LANES), jnp.bfloat16),
+            pltpu.VMEM((2, members // 2 * EDGE, LANES), jnp.bfloat16),
+            pltpu.VMEM((members, 2 * HALF, LANES), jnp.bfloat16),
+        ],
+        compiler_params=pltpu.CompilerParams(vmem_limit_bytes=24 * 1024 * 1024),
+        name="early",
+    )(own, greens, score)
     part = pl.pallas_call(
         functools.partial(main_kernel, 1.0 / math.sqrt(5 * EDGE * EDGE * total), members),
         out_shape=jax.ShapeDtypeStruct((members, members), jnp.float32),
-        in_specs=[VMEM] * 4,
+        in_specs=[VMEM] * 6,
         out_specs=VMEM,
         scratch_shapes=[
             pltpu.VMEM((6 * EDGE, 3 * LANES), jnp.bfloat16),
-            pltpu.VMEM((2, 2 * EDGE, LANES), jnp.bfloat16),
-            pltpu.VMEM((members // 2 * EDGE, 5 * LANES), jnp.bfloat16),
-            pltpu.VMEM((members, 5 * HALF, LANES), jnp.bfloat16),
+            pltpu.VMEM((members // 2 * EDGE, 2 * LANES), jnp.bfloat16),
+            pltpu.VMEM((members, 3 * HALF, LANES), jnp.bfloat16),
         ],
-        compiler_params=pltpu.CompilerParams(vmem_limit_bytes=48 * 1024 * 1024),
+        compiler_params=pltpu.CompilerParams(vmem_limit_bytes=24 * 1024 * 1024),
         name="products",
-    )(schip, own, greens, score)
+    )(early, right, schip, own, greens, score)
     mine = lax.all_to_all(part, "blk", split_axis=0, concat_axis=0, tiled=True)
     return jnp.sum(mine, axis=0, keepdims=True)
 

time: 40.1 us -> 40.3 us (level)
  waiting for transfers between devices: 12.2 us -> 11.2 us
  Pallas kernels: 5.18 us -> 6.09 us
    ppermute x1, waiting for transfers between devices: 5.95 us -> 3.58 us  [body(): schip = lax.ppermute(to_chip, 'blk', chip_pairs)]
    ppermute x1, waiting for transfers between devices: 0.01 us -> 1.38 us  [body(): score = lax.ppermute(to_core, 'blk', core_pairs)]
    pallas_call x0 -> x1, Pallas kernels: none -> 1.1 us  [body(): pl.pallas_call(functools.partial(early_kernel, members), out_shape=(jax.S...]
  transfers between devices with their start and end apart: 4 -> 4, of which waited for: 3 -> 4; matrix products, arithmetic and copies ran while one was open for 0% -> 0% of each run, Pallas kernels for 4% -> 7%
where the time goes in v9:
time: 40.3 us; the launch traced here: 39.9 us
  starting transfers between devices  12.3 us (31%)
  waiting for transfers between devices  11.2 us (28%)
  blocking collectives  9.54 us (24%)
  Pallas kernels  6.09 us (15%)
  other arithmetic  0.59 us (1%)
    all_to_all x1, blocking collectives, body(): mine = lax.all_to_all(part, 'blk', split_axis=0, concat_axis=0, tiled=True)  9.54 us
    all_to_all x1, starting transfers between devices, body(): own = lax.all_to_all(rows, 'blk', split_axis=0, concat_axis=0, tiled=True)  7.4 us
    ppermute x1, starting transfers between devices, body(): greens = lax.ppermute(greens, 'blk', list(enumerate(order)))  4.72 us
    ppermute x1, waiting for transfers between devices, body(): schip = lax.ppermute(to_chip, 'blk', chip_pairs)  3.58 us
    ppermute x1, waiting for transfers between devices, body(): greens = lax.ppermute(greens, 'blk', list(enumerate(order)))  3.2 us
    all_to_all x1, waiting for transfers between devices, body(): own = lax.all_to_all(rows, 'blk', split_axis=0, concat_axis=0, tiled=True)  3.07 us
    pallas_call x1, Pallas kernels, body(): pl.pallas_call(functools.partial(pack_kernel, works_on), out_shape=jax.Sh...  1.98 us
    pallas_call x1, Pallas kernels, body(): pl.pallas_call(functools.partial(prep_kernel, total), out_shape=jax.Shape...  1.67 us
  transfers between devices with their start and end apart: 4, of which 4 were waited for; matrix products, arithmetic and copies ran while one was open for 0% of the time, Pallas kernels for 7%

profile of v9, /device:TPU:0, one launch (start us, length us, event | category | flops | bytes accessed | tf_op | source)
XLA Modules:
  0.0 39.9 jit_solution(7585967735689781392)
XLA Ops:
  0.0 2.0 %pack.1 = bf16[16,96,128]{2,1,0:T(8,128)(2,1)} custom-call(bf16[3,16,4096]{2,1,0:T(8,128)(2,1)} %bitcast.17, s32[3,16]{1,0:T(4,128)} %bitcast.20), custom_call_target="tpu_custom_call" | custom-call | tf_op jit(solution)/shard_map/pack/pallas_call | solution.py:284
  2.0 7.4 %all-to-all-start = ((bf16[16,96,128]{2,1,0:T(8,128)(2,1)}), bf16[16,96,128]{2,1,0:T(8,128)(2,1)S(1)}, u32[]{:S(2)}, u32[]{:S(2)}) async-start(bf16[16,96,128]{2,1,0:T(8,128)(2,1)} %pack.1), calls=%async_computation | async-start | bytes 786432 | tf_op jit(solution)/shard_map/all_to_all | solution.py:308
  9.4 1.7 %prep.1 = bf16[192,128]{1,0:T(8,128)(2,1)} custom-call(s32[3,16]{1,0:T(4,128)} %bitcast.21, s32[3,16]{1,0:T(4,128)} %bitcast.22, s32[16]{0:T(128)} %count.1, bf16[3,4096]{1,0:T(4,128)(2,1)} %bitcast.18, bf16[3,4096]{1,0:T(4,128)(2,1)} %bitcast.19), custom_call_target="tpu_custom_call" | custom-call | tf_op jit(solution)/shard_map/prep/pallas_call | solution.py:299
  11.1 4.7 %collective-permute-start = (bf16[192,128]{1,0:T(8,128)(2,1)}, bf16[192,128]{1,0:T(8,128)(2,1)S(1)}, u32[]{:S(2)}, u32[]{:S(2)}) collective-permute-start(bf16[192,128]{1,0:T(8,128)(2,1)} %prep.1), channel_id=1, source_target_pairs={{0,6},{1,7},{2,2},{3,3},{4,0},{5,1},{6,4},{7,5},{8,8},{9,9},{10,12... | collective-permute-start | bytes 147464 | tf_op jit(solution)/shard_map/ppermute | solution.py:307
  15.8 3.2 %collective-permute-done.gown = bf16[192,128]{1,0:T(8,128)(2,1)S(1)} collective-permute-done((bf16[192,128]{1,0:T(8,128)(2,1)}, bf16[192,128]{1,0:T(8,128)(2,1)S(1)}, u32[]{:S(2)}, u32[]{:S(2)}) %collective-permute-start) | collective-permute-done | bytes 49184 | tf_op jit(solution)/shard_map/ppermute | solution.py:307
  19.0 3.1 %all-to-all-done.sown = bf16[16,96,128]{2,1,0:T(8,128)(2,1)S(1)} async-done(((bf16[16,96,128]{2,1,0:T(8,128)(2,1)}), bf16[16,96,128]{2,1,0:T(8,128)(2,1)S(1)}, u32[]{:S(2)}, u32[]{:S(2)}) %all-to-all-start) | async-done | bytes 393248 | tf_op jit(solution)/shard_map/all_to_all | solution.py:308
  22.1 0.1 fusion
  22.2 0.1 collective-permute-start.1
  22.3 0.2 collective-permute-start.2
  22.4 1.4 %collective-permute-done.1.score = bf16[1152,128]{1,0:T(8,128)(2,1)S(1)} collective-permute-done((bf16[1152,128]{1,0:T(8,128)(2,1)S(1)}, bf16[1152,128]{1,0:T(8,128)(2,1)S(1)}, u32[]{:S(2)}, u32[]{:S(2)}) %collective-permute-start.1) | collective-permute-done | bytes 294944 | tf_op jit(solution)/shard_map/ppermute | solution.py:314
  23.8 1.1 %early.1 = (f32[16,16]{1,0:T(8,128)S(1)}, bf16[512,128]{1,0:T(8,128)(2,1)S(1)}) custom-call(bf16[16,96,128]{2,1,0:T(8,128)(2,1)S(1)} %all-to-all-done.sown, bf16[192,128]{1,0:T(8,128)(2,1)S(1)} %collective-permute-done.gown, bf16[1152,128]{1,0:T(8,128)(2,1)S(1)} %collective-permute-done.1.score), custom_call_target="tpu_custom_call" | custom-call | tf_op jit(solution)/shard_map/early/pallas_call | solution.py:315
  24.9 3.6 %collective-permute-done.2.schip = bf16[1152,128]{1,0:T(8,128)(2,1)S(1)} collective-permute-done((bf16[1152,128]{1,0:T(8,128)(2,1)S(1)}, bf16[1152,128]{1,0:T(8,128)(2,1)S(1)}, u32[]{:S(2)}, u32[]{:S(2)}) %collective-permute-start.2) | collective-permute-done | bytes 294944 | tf_op jit(solution)/shard_map/ppermute | solution.py:313
  28.5 1.3 %products.1 = f32[16,16]{1,0:T(8,128)S(1)} custom-call(f32[16,16]{1,0:T(8,128)S(1)} %get-tuple-element.7.part_ref, bf16[512,128]{1,0:T(8,128)(2,1)S(1)} %get-tuple-element.8.right_ref, bf16[1152,128]{1,0:T(8,128)(2,1)S(1)} %collective-permute-done.2.schip, bf16[16,96,128]{2,1,0:T(8,128)(2,1)S(1)} %all-to-all-done.sown, ...), custom_call_target="tpu_custom_call" | custom-call | tf_op jit(solution)/shard_map/products/pallas_call | solution.py:331
  29.8 9.5 %all_to_all.14 = f32[16,1,16]{2,1,0:T(1,128)S(1)} all-to-all(f32[16,1,16]{2,1,0:T(1,128)S(1)} %bitcast.14), channel_id=1, replica_groups=mesh['grp'=2,'blk'=16] {'blk'}, dimensions={0} | all-to-all | bytes 2048 | tf_op jit(solution)/shard_map/all_to_all | solution.py:344
  39.4 0.5 %reduce_sum.9 = f32[16]{0:T(128)} reduce(f32[16,1,16]{2,1,0:T(1,128)S(1)} %all_to_all.14, f32[]{:T(128)} %constant.0.clone.1), dimensions={0,1}, to_apply=%region_0.0 | reduce | flops 240 | bytes 1092 | tf_op jit(solution)/shard_map/reduce_sum | solution.py:345
  (3 shorter events, 0.0 us)
Async XLA Ops:
  2.0 20.1 %all-to-all-start = ((bf16[16,96,128]{2,1,0:T(8,128)(2,1)}), bf16[16,96,128]{2,1,0:T(8,128)(2,1)S(1)}, u32[]{:S(2)}, u32[]{:S(2)}) async-start(bf16[16,96,128]{2,1,0:T(8,128)(2,1)} %pack.1), calls=%async_computation | async-start | bytes 786432 | tf_op jit(solution)/shard_map/all_to_all | solution.py:308
  11.1 7.9 %collective-permute-start = (bf16[192,128]{1,0:T(8,128)(2,1)}, bf16[192,128]{1,0:T(8,128)(2,1)S(1)}, u32[]{:S(2)}, u32[]{:S(2)}) collective-permute-start(bf16[192,128]{1,0:T(8,128)(2,1)} %prep.1), channel_id=1, source_target_pairs={{0,6},{1,7},{2,2},{3,3},{4,0},{5,1},{6,4},{7,5},{8,8},{9,9},{10,12... | collective-permute-start | bytes 147464 | tf_op jit(solution)/shard_map/ppermute | solution.py:307
  22.2 1.6 %collective-permute-start.1 = (bf16[1152,128]{1,0:T(8,128)(2,1)S(1)}, bf16[1152,128]{1,0:T(8,128)(2,1)S(1)}, u32[]{:S(2)}, u32[]{:S(2)}) collective-permute-start(bf16[1152,128]{1,0:T(8,128)(2,1)S(1)} %pad_maximum_fusion), channel_id=1, source_target_pairs={{6,7},{7,6},{2,3},{3,2},{0,1},{1,0},{4,5},{5,4},{8,9},{9,8},{12,13... | collective-permute-start | bytes 884744 | tf_op jit(solution)/shard_map/ppermute | solution.py:314
  22.3 6.2 %collective-permute-start.2 = (bf16[1152,128]{1,0:T(8,128)(2,1)S(1)}, bf16[1152,128]{1,0:T(8,128)(2,1)S(1)}, u32[]{:S(2)}, u32[]{:S(2)}) collective-permute-start(bf16[1152,128]{1,0:T(8,128)(2,1)S(1)} %pad_maximum_fusion.1), channel_id=1, source_target_pairs={{6,11},{7,2},{2,7},{3,0},{0,3},{1,4},{4,1},{5,8},{8,5},{9,12},{12,... | collective-permute-start | bytes 884744 | tf_op jit(solution)/shard_map/ppermute | solution.py:313

commit v10 on v9

--- a/solution.py
+++ b/solution.py
@@ -175,38 +175,27 @@
     return slab, green
 
 
-def early_kernel(rows, sown, gown, score, part_ref, right_ref, far_ref, half_ref, full_ref):
-    slab, green = readers(rows, None, sown, gown, score)
+def early_kernel(rows, sown, gown, part_ref, sides_ref, far_ref, half_ref, full_ref):
+    slab, green = readers(rows, None, sown, gown, None)
     none = jnp.zeros((EDGE, EDGE), jnp.bfloat16)
     for k in range(2):
         o = green(1, 2 * k)[:, EDGE:]
         far_ref[k] = jnp.concatenate(
             [jnp.concatenate([o, none], 1), jnp.concatenate([none, o], 1)], 0
         )
-    vir = jnp.concatenate(
-        [
-            jnp.concatenate([green(1, 1)[:, :EDGE], green(2, 0)[:, :EDGE]], 1),
-            jnp.concatenate([green(1, 0)[:, :EDGE], none], 1),
-        ],
-        0,
-    )
     for j in range(0, rows // 2, 2):
-        low = jnp.dot(
-            green(1, 2)[:, :EDGE],
-            jnp.concatenate(halves(slab, (1, 0), j), 0),
-            preferred_element_type=jnp.float32,
-        ).astype(jnp.bfloat16)
-        high = jnp.dot(
-            vir,
-            jnp.concatenate(halves(slab, (1, 2), j) + halves(slab, (2, 1), j), 0),
-            preferred_element_type=jnp.float32,
-        ).astype(jnp.bfloat16)
-        for k in range(2):
-            at = pl.ds((j + k) * EDGE, EDGE)
-            lanes = slice(k * LANES, (k + 1) * LANES)
-            right_ref[at, :] = high[:EDGE, lanes]
-            half_ref[0, at, :] = low[:, lanes]
-            half_ref[1, at, :] = high[EDGE:, lanes]
+        for a in range(3):
+            side = jnp.concatenate(halves(slab, (1, a), j), 0)
+            sides_ref[a, :, pl.ds(j * LANES, 2 * LANES)] = side
+            if a == 1:
+                continue
+            both = jnp.dot(
+                green(1, 2 - a)[:, :EDGE], side, preferred_element_type=jnp.float32
+            ).astype(jnp.bfloat16)
+            for k in range(2):
+                half_ref[a // 2, pl.ds((j + k) * EDGE, EDGE), :] = both[
+                    :, k * LANES : (k + 1) * LANES
+                ]
     for j in range(0, rows // 2, 4):
         for k in range(2):
             full = lax.dot_general(
@@ -225,12 +214,12 @@
 
 
 def main_kernel(
-    scale, rows, part_ref, right_ref, schip, sown, gown, score, out_ref, occ_ref, half_ref, full_ref
+    scale, rows, part_ref, sides_ref, schip, sown, gown, score, out_ref, occ_ref, half_ref, full_ref
 ):
     slab, green = readers(rows, schip, sown, gown, score)
     none = jnp.zeros((EDGE, EDGE), jnp.bfloat16)
     near = [green(s, 2 - s)[:, :EDGE] for s in range(3)]
-    vir = [jnp.concatenate(near[:2], 1), jnp.concatenate(near, 1)]
+    vir = [jnp.concatenate(x, 1) for x in (near[:2], near, near[1:])]
     used = ({0: 1, 1: 2}, {0: 0, 1: 1, 2: 2}, {1: 0, 2: 1})
     for s in range(3):
         for t in range(3):
@@ -243,12 +232,15 @@
                 else:
                     occ_ref[at, to] = jnp.zeros((EDGE, LANES), jnp.bfloat16)
 
-    members = (((0, 1), (1, 0)), ((0, 2), (1, 1), (2, 0)))
+    members = (((0, 1), (1, 0)), ((0, 2), (1, 1), (2, 0)), ((1, 2), (2, 1)))
     for j in range(0, rows // 2, 2):
-        for t in range(2):
+        for t in range(3):
             parts = []
-            for at in members[t]:
-                parts += halves(slab, at, j)
+            for s, a in members[t]:
+                if s == 1:
+                    parts.append(sides_ref[a, :, pl.ds(j * LANES, 2 * LANES)])
+                else:
+                    parts += halves(slab, (s, a), j)
             both = jnp.dot(vir[t], jnp.concatenate(parts, 0), preferred_element_type=jnp.float32)
             both = both.astype(jnp.bfloat16)
             for k in range(2):
@@ -260,7 +252,7 @@
         at = pl.ds(j * EDGE, 4 * EDGE)
         full = lax.dot_general(
             occ_ref[...],
-            jnp.concatenate([half_ref[at, :], right_ref[at, :]], 1),
+            half_ref[at, :],
             NT,
             preferred_element_type=jnp.float32,
         )
@@ -312,13 +304,13 @@
     to_core = jnp.concatenate([own[:, HALF:].reshape(-1, LANES), greens[EDGE:]], 0)
     schip = lax.ppermute(to_chip, "blk", chip_pairs)
     score = lax.ppermute(to_core, "blk", core_pairs)
-    early, right = pl.pallas_call(
+    early, sides = pl.pallas_call(
         functools.partial(early_kernel, members),
         out_shape=(
             jax.ShapeDtypeStruct((members, members), jnp.float32),
-            jax.ShapeDtypeStruct((members // 2 * EDGE, LANES), jnp.bfloat16),
+            jax.ShapeDtypeStruct((3, EDGE, members // 2 * LANES), jnp.bfloat16),
         ),
-        in_specs=[VMEM] * 3,
+        in_specs=[VMEM] * 2,
         out_specs=(VMEM, VMEM),
         scratch_shapes=[
             pltpu.VMEM((2, 2 * EDGE, LANES), jnp.bfloat16),
@@ -327,7 +319,7 @@
         ],
         compiler_params=pltpu.CompilerParams(vmem_limit_bytes=24 * 1024 * 1024),
         name="early",
-    )(own, greens, score)
+    )(own, greens)
     part = pl.pallas_call(
         functools.partial(main_kernel, 1.0 / math.sqrt(5 * EDGE * EDGE * total), members),
         out_shape=jax.ShapeDtypeStruct((members, members), jnp.float32),
@@ -335,12 +327,12 @@
         out_specs=VMEM,
         scratch_shapes=[
             pltpu.VMEM((6 * EDGE, 3 * LANES), jnp.bfloat16),
-            pltpu.VMEM((members // 2 * EDGE, 2 * LANES), jnp.bfloat16),
+            pltpu.VMEM((members // 2 * EDGE, 3 * LANES), jnp.bfloat16),
             pltpu.VMEM((members, 3 * HALF, LANES), jnp.bfloat16),
         ],
         compiler_params=pltpu.CompilerParams(vmem_limit_bytes=24 * 1024 * 1024),
         name="products",
-    )(early, right, schip, own, greens, score)
+    )(early, sides, schip, own, greens, score)
     mine = lax.all_to_all(part, "blk", split_axis=0, concat_axis=0, tiled=True)
     return jnp.sum(mine, axis=0, keepdims=True)
 

time: 40.3 us -> 39.9 us (0.990)
    ppermute x1, waiting for transfers between devices: 1.38 us -> 0.01 us  [body(): score = lax.ppermute(to_core, 'blk', core_pairs)]
    ppermute x1, waiting for transfers between devices: 3.58 us -> 4.91 us  [body(): schip = lax.ppermute(to_chip, 'blk', chip_pairs)]
  transfers between devices with their start and end apart: 4 -> 4, of which waited for: 4 -> 3; matrix products, arithmetic and copies ran while one was open for 0% -> 0% of each run, Pallas kernels for 7% -> 7%
where the time goes in v10:
time: 39.9 us; the launch traced here: 39.5 us
  starting transfers between devices  12.3 us (31%)
  waiting for transfers between devices  11.2 us (28%)
  blocking collectives  9.26 us (23%)
  Pallas kernels  6.04 us (15%)
  other arithmetic  0.59 us (1%)
    all_to_all x1, blocking collectives, body(): mine = lax.all_to_all(part, 'blk', split_axis=0, concat_axis=0, tiled=True)  9.26 us
    all_to_all x1, starting transfers between devices, body(): own = lax.all_to_all(rows, 'blk', split_axis=0, concat_axis=0, tiled=True)  7.4 us
    ppermute x1, waiting for transfers between devices, body(): schip = lax.ppermute(to_chip, 'blk', chip_pairs)  4.91 us
    ppermute x1, starting transfers between devices, body(): greens = lax.ppermute(greens, 'blk', list(enumerate(order)))  4.72 us
    ppermute x1, waiting for transfers between devices, body(): greens = lax.ppermute(greens, 'blk', list(enumerate(order)))  3.2 us
    all_to_all x1, waiting for transfers between devices, body(): own = lax.all_to_all(rows, 'blk', split_axis=0, concat_axis=0, tiled=True)  3.07 us
    pallas_call x1, Pallas kernels, body(): pl.pallas_call(functools.partial(pack_kernel, works_on), out_shape=jax.Sh...  1.98 us
    pallas_call x1, Pallas kernels, body(): pl.pallas_call(functools.partial(prep_kernel, total), out_shape=jax.Shape...  1.67 us
  transfers between devices with their start and end apart: 4, of which 3 were waited for; matrix products, arithmetic and copies ran while one was open for 0% of the time, Pallas kernels for 7%

profile of v10, /device:TPU:0, one launch (start us, length us, event | category | flops | bytes accessed | tf_op | source)
XLA Modules:
  0.0 39.5 jit_solution(16118244954587054739)
XLA Ops:
  0.0 2.0 %pack.1 = bf16[16,96,128]{2,1,0:T(8,128)(2,1)} custom-call(bf16[3,16,4096]{2,1,0:T(8,128)(2,1)} %bitcast.17, s32[3,16]{1,0:T(4,128)} %bitcast.20), custom_call_target="tpu_custom_call" | custom-call | tf_op jit(solution)/shard_map/pack/pallas_call | solution.py:276
  2.0 7.4 %all-to-all-start = ((bf16[16,96,128]{2,1,0:T(8,128)(2,1)}), bf16[16,96,128]{2,1,0:T(8,128)(2,1)S(1)}, u32[]{:S(2)}, u32[]{:S(2)}) async-start(bf16[16,96,128]{2,1,0:T(8,128)(2,1)} %pack.1), calls=%async_computation | async-start | bytes 786432 | tf_op jit(solution)/shard_map/all_to_all | solution.py:300
  9.4 1.7 %prep.1 = bf16[192,128]{1,0:T(8,128)(2,1)} custom-call(s32[3,16]{1,0:T(4,128)} %bitcast.21, s32[3,16]{1,0:T(4,128)} %bitcast.22, s32[16]{0:T(128)} %count.1, bf16[3,4096]{1,0:T(4,128)(2,1)} %bitcast.18, bf16[3,4096]{1,0:T(4,128)(2,1)} %bitcast.19), custom_call_target="tpu_custom_call" | custom-call | tf_op jit(solution)/shard_map/prep/pallas_call | solution.py:291
  11.1 4.7 %collective-permute-start = (bf16[192,128]{1,0:T(8,128)(2,1)}, bf16[192,128]{1,0:T(8,128)(2,1)S(1)}, u32[]{:S(2)}, u32[]{:S(2)}) collective-permute-start(bf16[192,128]{1,0:T(8,128)(2,1)} %prep.1), channel_id=1, source_target_pairs={{0,6},{1,7},{2,2},{3,3},{4,0},{5,1},{6,4},{7,5},{8,8},{9,9},{10,12... | collective-permute-start | bytes 147464 | tf_op jit(solution)/shard_map/ppermute | solution.py:299
  15.8 3.2 %collective-permute-done.gown = bf16[192,128]{1,0:T(8,128)(2,1)S(1)} collective-permute-done((bf16[192,128]{1,0:T(8,128)(2,1)}, bf16[192,128]{1,0:T(8,128)(2,1)S(1)}, u32[]{:S(2)}, u32[]{:S(2)}) %collective-permute-start) | collective-permute-done | bytes 49184 | tf_op jit(solution)/shard_map/ppermute | solution.py:299
  19.0 3.1 %all-to-all-done.sown = bf16[16,96,128]{2,1,0:T(8,128)(2,1)S(1)} async-done(((bf16[16,96,128]{2,1,0:T(8,128)(2,1)}), bf16[16,96,128]{2,1,0:T(8,128)(2,1)S(1)}, u32[]{:S(2)}, u32[]{:S(2)}) %all-to-all-start) | async-done | bytes 393248 | tf_op jit(solution)/shard_map/all_to_all | solution.py:300
  22.1 0.1 fusion
  22.2 0.2 collective-permute-start.1
  22.3 0.1 collective-permute-start.2
  22.4 1.0 %early.1 = (f32[16,16]{1,0:T(8,128)S(1)}, bf16[3,64,1024]{2,1,0:T(8,128)(2,1)S(1)}) custom-call(bf16[16,96,128]{2,1,0:T(8,128)(2,1)S(1)} %all-to-all-done.sown, bf16[192,128]{1,0:T(8,128)(2,1)S(1)} %collective-permute-done.gown), custom_call_target="tpu_custom_call" | custom-call | tf_op jit(solution)/shard_map/early/pallas_call | solution.py:307
  23.5 4.9 %collective-permute-done.1.schip = bf16[1152,128]{1,0:T(8,128)(2,1)S(1)} collective-permute-done((bf16[1152,128]{1,0:T(8,128)(2,1)S(1)}, bf16[1152,128]{1,0:T(8,128)(2,1)S(1)}, u32[]{:S(2)}, u32[]{:S(2)}) %collective-permute-start.1) | collective-permute-done | bytes 294944 | tf_op jit(solution)/shard_map/ppermute | solution.py:305
  28.4 0.0 collective-permute-done.2.score
  28.4 1.3 %products.1 = f32[16,16]{1,0:T(8,128)S(1)} custom-call(f32[16,16]{1,0:T(8,128)S(1)} %get-tuple-element.7.part_ref, bf16[3,64,1024]{2,1,0:T(8,128)(2,1)S(1)} %get-tuple-element.8.sides_ref, bf16[1152,128]{1,0:T(8,128)(2,1)S(1)} %collective-permute-done.1.schip, bf16[16,96,128]{2,1,0:T(8,128)(2,1)S(1)} %all-to-all-done.sown, ...), custom_call_target="tpu_custom_call" | custom-call | tf_op jit(solution)/shard_map/products/pallas_call | solution.py:323
  29.7 9.3 %all_to_all.14 = f32[16,1,16]{2,1,0:T(1,128)S(1)} all-to-all(f32[16,1,16]{2,1,0:T(1,128)S(1)} %bitcast.14), channel_id=1, replica_groups=mesh['grp'=2,'blk'=16] {'blk'}, dimensions={0} | all-to-all | bytes 2048 | tf_op jit(solution)/shard_map/all_to_all | solution.py:336
  39.0 0.5 %reduce_sum.9 = f32[16]{0:T(128)} reduce(f32[16,1,16]{2,1,0:T(1,128)S(1)} %all_to_all.14, f32[]{:T(128)} %constant.0.clone.1), dimensions={0,1}, to_apply=%region_0.0 | reduce | flops 240 | bytes 1092 | tf_op jit(solution)/shard_map/reduce_sum | solution.py:337
  (3 shorter events, 0.0 us)
Async XLA Ops:
  2.0 20.1 %all-to-all-start = ((bf16[16,96,128]{2,1,0:T(8,128)(2,1)}), bf16[16,96,128]{2,1,0:T(8,128)(2,1)S(1)}, u32[]{:S(2)}, u32[]{:S(2)}) async-start(bf16[16,96,128]{2,1,0:T(8,128)(2,1)} %pack.1), calls=%async_computation | async-start | bytes 786432 | tf_op jit(solution)/shard_map/all_to_all | solution.py:300
  11.1 7.9 %collective-permute-start = (bf16[192,128]{1,0:T(8,128)(2,1)}, bf16[192,128]{1,0:T(8,128)(2,1)S(1)}, u32[]{:S(2)}, u32[]{:S(2)}) collective-permute-start(bf16[192,128]{1,0:T(8,128)(2,1)} %prep.1), channel_id=1, source_target_pairs={{0,6},{1,7},{2,2},{3,3},{4,0},{5,1},{6,4},{7,5},{8,8},{9,9},{10,12... | collective-permute-start | bytes 147464 | tf_op jit(solution)/shard_map/ppermute | solution.py:299
  22.2 6.2 %collective-permute-start.1 = (bf16[1152,128]{1,0:T(8,128)(2,1)S(1)}, bf16[1152,128]{1,0:T(8,128)(2,1)S(1)}, u32[]{:S(2)}, u32[]{:S(2)}) collective-permute-start(bf16[1152,128]{1,0:T(8,128)(2,1)S(1)} %pad_maximum_fusion), channel_id=1, source_target_pairs={{6,11},{7,2},{2,7},{3,0},{0,3},{1,4},{4,1},{5,8},{8,5},{9,12},{12,... | collective-permute-start | bytes 884744 | tf_op jit(solution)/shard_map/ppermute | solution.py:305
  22.3 6.0 %collective-permute-start.2 = (bf16[1152,128]{1,0:T(8,128)(2,1)S(1)}, bf16[1152,128]{1,0:T(8,128)(2,1)S(1)}, u32[]{:S(2)}, u32[]{:S(2)}) collective-permute-start(bf16[1152,128]{1,0:T(8,128)(2,1)S(1)} %pad_maximum_fusion.1), channel_id=1, source_target_pairs={{6,7},{7,6},{2,3},{3,2},{0,1},{1,0},{4,5},{5,4},{8,9},{9,8},{12,13... | collective-permute-start | bytes 884744 | tf_op jit(solution)/shard_map/ppermute | solution.py:306

commit v11 on v10

--- a/solution.py
+++ b/solution.py
@@ -101,18 +101,14 @@
 
 
 def unfold(block, j, g, half, full_ref):
-    left = lax.broadcasted_iota(jnp.int32, (HALF, LANES), 1) < EDGE
+    block = block.astype(jnp.bfloat16)
     place = pl.ds(g * HALF, HALF)
     for k in range(2):
         even = block[:HALF, k * LANES : (k + 1) * LANES]
         odd = block[HALF:, k * LANES : (k + 1) * LANES]
         first = 2 * (j + 2 * k) + half
-        full_ref[first, place, :] = jnp.where(left, even, pltpu.roll(odd, EDGE, 1)).astype(
-            jnp.bfloat16
-        )
-        full_ref[first + 2, place, :] = jnp.where(left, pltpu.roll(even, EDGE, 1), odd).astype(
-            jnp.bfloat16
-        )
+        full_ref[first, place, :] = jnp.concatenate([even[:, :EDGE], odd[:, :EDGE]], 1)
+        full_ref[first + 2, place, :] = jnp.concatenate([even[:, EDGE:], odd[:, EDGE:]], 1)
 
 
 def inner(slabs, full_ref, rows, store):
@@ -219,7 +215,14 @@
     slab, green = readers(rows, schip, sown, gown, score)
     none = jnp.zeros((EDGE, EDGE), jnp.bfloat16)
     near = [green(s, 2 - s)[:, :EDGE] for s in range(3)]
-    vir = [jnp.concatenate(x, 1) for x in (near[:2], near, near[1:])]
+    mid = jnp.concatenate(near, 1)
+    ends = jnp.concatenate(
+        [
+            jnp.concatenate([near[0], near[1], none, none], 1),
+            jnp.concatenate([none, none, near[1], near[2]], 1),
+        ],
+        0,
+    )
     used = ({0: 1, 1: 2}, {0: 0, 1: 1, 2: 2}, {1: 0, 2: 1})
     for s in range(3):
         for t in range(3):
@@ -232,19 +235,21 @@
                 else:
                     occ_ref[at, to] = jnp.zeros((EDGE, LANES), jnp.bfloat16)
 
-    members = (((0, 1), (1, 0)), ((0, 2), (1, 1), (2, 0)), ((1, 2), (2, 1)))
     for j in range(0, rows // 2, 2):
-        for t in range(3):
-            parts = []
-            for s, a in members[t]:
-                if s == 1:
-                    parts.append(sides_ref[a, :, pl.ds(j * LANES, 2 * LANES)])
-                else:
-                    parts += halves(slab, (s, a), j)
-            both = jnp.dot(vir[t], jnp.concatenate(parts, 0), preferred_element_type=jnp.float32)
-            both = both.astype(jnp.bfloat16)
+        own = [sides_ref[a, :, pl.ds(j * LANES, 2 * LANES)] for a in range(3)]
+        both = jnp.dot(
+            ends,
+            jnp.concatenate(halves(slab, (0, 1), j) + [own[0], own[2]] + halves(slab, (2, 1), j), 0),
+            preferred_element_type=jnp.float32,
+        ).astype(jnp.bfloat16)
+        middle = jnp.dot(
+            mid,
+            jnp.concatenate(halves(slab, (0, 2), j) + [own[1]] + halves(slab, (2, 0), j), 0),
+            preferred_element_type=jnp.float32,
+        ).astype(jnp.bfloat16)
+        for t, piece in enumerate((both[:EDGE], middle, both[EDGE:])):
             for k in range(2):
-                half_ref[pl.ds((j + k) * EDGE, EDGE), pl.ds(t * LANES, LANES)] = both[
+                half_ref[pl.ds((j + k) * EDGE, EDGE), pl.ds(t * LANES, LANES)] = piece[
                     :, k * LANES : (k + 1) * LANES
                 ]
 

time: 39.9 us -> 39.9 us (level)
  no operation moved by 1% of the time
where the time goes in v11:
time: 39.9 us; the launch traced here: 39.5 us
  starting transfers between devices  12.3 us (31%)
  waiting for transfers between devices  11.2 us (28%)
  blocking collectives  9.27 us (23%)
  Pallas kernels  6.06 us (15%)
  other arithmetic  0.59 us (1%)
    all_to_all x1, blocking collectives, body(): mine = lax.all_to_all(part, 'blk', split_axis=0, concat_axis=0, tiled=True)  9.27 us
    all_to_all x1, starting transfers between devices, body(): own = lax.all_to_all(rows, 'blk', split_axis=0, concat_axis=0, tiled=True)  7.4 us
    ppermute x1, waiting for transfers between devices, body(): schip = lax.ppermute(to_chip, 'blk', chip_pairs)  4.9 us
    ppermute x1, starting transfers between devices, body(): greens = lax.ppermute(greens, 'blk', list(enumerate(order)))  4.72 us
    ppermute x1, waiting for transfers between devices, body(): greens = lax.ppermute(greens, 'blk', list(enumerate(order)))  3.2 us
    all_to_all x1, waiting for transfers between devices, body(): own = lax.all_to_all(rows, 'blk', split_axis=0, concat_axis=0, tiled=True)  3.07 us
    pallas_call x1, Pallas kernels, body(): pl.pallas_call(functools.partial(pack_kernel, works_on), out_shape=jax.Sh...  1.98 us
    pallas_call x1, Pallas kernels, body(): pl.pallas_call(functools.partial(prep_kernel, total), out_shape=jax.Shape...  1.67 us
  transfers between devices with their start and end apart: 4, of which 3 were waited for; matrix products, arithmetic and copies ran while one was open for 0% of the time, Pallas kernels for 7%

profile of v11, /device:TPU:0, one launch (start us, length us, event | category | flops | bytes accessed | tf_op | source)
XLA Modules:
  0.0 39.5 jit_solution(6720651628492122947)
XLA Ops:
  0.0 2.0 %pack.1 = bf16[16,96,128]{2,1,0:T(8,128)(2,1)} custom-call(bf16[3,16,4096]{2,1,0:T(8,128)(2,1)} %bitcast.17, s32[3,16]{1,0:T(4,128)} %bitcast.20), custom_call_target="tpu_custom_call" | custom-call | tf_op jit(solution)/shard_map/pack/pallas_call | solution.py:281
  2.0 7.4 %all-to-all-start = ((bf16[16,96,128]{2,1,0:T(8,128)(2,1)}), bf16[16,96,128]{2,1,0:T(8,128)(2,1)S(1)}, u32[]{:S(2)}, u32[]{:S(2)}) async-start(bf16[16,96,128]{2,1,0:T(8,128)(2,1)} %pack.1), calls=%async_computation | async-start | bytes 786432 | tf_op jit(solution)/shard_map/all_to_all | solution.py:305
  9.4 1.7 %prep.1 = bf16[192,128]{1,0:T(8,128)(2,1)} custom-call(s32[3,16]{1,0:T(4,128)} %bitcast.21, s32[3,16]{1,0:T(4,128)} %bitcast.22, s32[16]{0:T(128)} %count.1, bf16[3,4096]{1,0:T(4,128)(2,1)} %bitcast.18, bf16[3,4096]{1,0:T(4,128)(2,1)} %bitcast.19), custom_call_target="tpu_custom_call" | custom-call | tf_op jit(solution)/shard_map/prep/pallas_call | solution.py:296
  11.1 4.7 %collective-permute-start = (bf16[192,128]{1,0:T(8,128)(2,1)}, bf16[192,128]{1,0:T(8,128)(2,1)S(1)}, u32[]{:S(2)}, u32[]{:S(2)}) collective-permute-start(bf16[192,128]{1,0:T(8,128)(2,1)} %prep.1), channel_id=1, source_target_pairs={{0,6},{1,7},{2,2},{3,3},{4,0},{5,1},{6,4},{7,5},{8,8},{9,9},{10,12... | collective-permute-start | bytes 147464 | tf_op jit(solution)/shard_map/ppermute | solution.py:304
  15.8 3.2 %collective-permute-done.gown = bf16[192,128]{1,0:T(8,128)(2,1)S(1)} collective-permute-done((bf16[192,128]{1,0:T(8,128)(2,1)}, bf16[192,128]{1,0:T(8,128)(2,1)S(1)}, u32[]{:S(2)}, u32[]{:S(2)}) %collective-permute-start) | collective-permute-done | bytes 49184 | tf_op jit(solution)/shard_map/ppermute | solution.py:304
  19.0 3.1 %all-to-all-done.sown = bf16[16,96,128]{2,1,0:T(8,128)(2,1)S(1)} async-done(((bf16[16,96,128]{2,1,0:T(8,128)(2,1)}), bf16[16,96,128]{2,1,0:T(8,128)(2,1)S(1)}, u32[]{:S(2)}, u32[]{:S(2)}) %all-to-all-start) | async-done | bytes 393248 | tf_op jit(solution)/shard_map/all_to_all | solution.py:305
  22.1 0.1 fusion
  22.2 0.2 collective-permute-start.1
  22.3 0.1 collective-permute-start.2
  22.4 1.1 %early.1 = (f32[16,16]{1,0:T(8,128)S(1)}, bf16[3,64,1024]{2,1,0:T(8,128)(2,1)S(1)}) custom-call(bf16[16,96,128]{2,1,0:T(8,128)(2,1)S(1)} %all-to-all-done.sown, bf16[192,128]{1,0:T(8,128)(2,1)S(1)} %collective-permute-done.gown), custom_call_target="tpu_custom_call" | custom-call | tf_op jit(solution)/shard_map/early/pallas_call | solution.py:312
  23.5 4.9 %collective-permute-done.1.schip = bf16[1152,128]{1,0:T(8,128)(2,1)S(1)} collective-permute-done((bf16[1152,128]{1,0:T(8,128)(2,1)S(1)}, bf16[1152,128]{1,0:T(8,128)(2,1)S(1)}, u32[]{:S(2)}, u32[]{:S(2)}) %collective-permute-start.1) | collective-permute-done | bytes 294944 | tf_op jit(solution)/shard_map/ppermute | solution.py:310
  28.4 0.0 collective-permute-done.2.score
  28.4 1.3 %products.1 = f32[16,16]{1,0:T(8,128)S(1)} custom-call(f32[16,16]{1,0:T(8,128)S(1)} %get-tuple-element.7.part_ref, bf16[3,64,1024]{2,1,0:T(8,128)(2,1)S(1)} %get-tuple-element.8.sides_ref, bf16[1152,128]{1,0:T(8,128)(2,1)S(1)} %collective-permute-done.1.schip, bf16[16,96,128]{2,1,0:T(8,128)(2,1)S(1)} %all-to-all-done.sown, ...), custom_call_target="tpu_custom_call" | custom-call | tf_op jit(solution)/shard_map/products/pallas_call | solution.py:328
  29.7 9.3 %all_to_all.14 = f32[16,1,16]{2,1,0:T(1,128)S(1)} all-to-all(f32[16,1,16]{2,1,0:T(1,128)S(1)} %bitcast.14), channel_id=1, replica_groups=mesh['grp'=2,'blk'=16] {'blk'}, dimensions={0} | all-to-all | bytes 2048 | tf_op jit(solution)/shard_map/all_to_all | solution.py:341
  39.0 0.5 %reduce_sum.9 = f32[16]{0:T(128)} reduce(f32[16,1,16]{2,1,0:T(1,128)S(1)} %all_to_all.14, f32[]{:T(128)} %constant.0.clone.1), dimensions={0,1}, to_apply=%region_0.0 | reduce | flops 240 | bytes 1092 | tf_op jit(solution)/shard_map/reduce_sum | solution.py:342
  (3 shorter events, 0.0 us)
Async XLA Ops:
  2.0 20.1 %all-to-all-start = ((bf16[16,96,128]{2,1,0:T(8,128)(2,1)}), bf16[16,96,128]{2,1,0:T(8,128)(2,1)S(1)}, u32[]{:S(2)}, u32[]{:S(2)}) async-start(bf16[16,96,128]{2,1,0:T(8,128)(2,1)} %pack.1), calls=%async_computation | async-start | bytes 786432 | tf_op jit(solution)/shard_map/all_to_all | solution.py:305
  11.1 7.9 %collective-permute-start = (bf16[192,128]{1,0:T(8,128)(2,1)}, bf16[192,128]{1,0:T(8,128)(2,1)S(1)}, u32[]{:S(2)}, u32[]{:S(2)}) collective-permute-start(bf16[192,128]{1,0:T(8,128)(2,1)} %prep.1), channel_id=1, source_target_pairs={{0,6},{1,7},{2,2},{3,3},{4,0},{5,1},{6,4},{7,5},{8,8},{9,9},{10,12... | collective-permute-start | bytes 147464 | tf_op jit(solution)/shard_map/ppermute | solution.py:304
  22.2 6.2 %collective-permute-start.1 = (bf16[1152,128]{1,0:T(8,128)(2,1)S(1)}, bf16[1152,128]{1,0:T(8,128)(2,1)S(1)}, u32[]{:S(2)}, u32[]{:S(2)}) collective-permute-start(bf16[1152,128]{1,0:T(8,128)(2,1)S(1)} %pad_maximum_fusion), channel_id=1, source_target_pairs={{6,11},{7,2},{2,7},{3,0},{0,3},{1,4},{4,1},{5,8},{8,5},{9,12},{12,... | collective-permute-start | bytes 884744 | tf_op jit(solution)/shard_map/ppermute | solution.py:310
  22.3 6.0 %collective-permute-start.2 = (bf16[1152,128]{1,0:T(8,128)(2,1)S(1)}, bf16[1152,128]{1,0:T(8,128)(2,1)S(1)}, u32[]{:S(2)}, u32[]{:S(2)}) collective-permute-start(bf16[1152,128]{1,0:T(8,128)(2,1)S(1)} %pad_maximum_fusion.1), channel_id=1, source_target_pairs={{6,7},{7,6},{2,3},{3,2},{0,1},{1,0},{4,5},{5,4},{8,9},{9,8},{12,13... | collective-permute-start | bytes 884744 | tf_op jit(solution)/shard_map/ppermute | solution.py:311

commit v12 on v11

--- a/solution.py
+++ b/solution.py
@@ -151,7 +151,7 @@
             )
 
 
-def readers(rows, schip, sown, gown, score):
+def readers(rows, schip, gchip, sown, gown, score):
     pair = 2 * HALF
 
     def slab(q, s, a):
@@ -163,7 +163,7 @@
 
     def green(s, a):
         if s == 0:
-            return schip[pl.ds(rows * pair + (2 - a) * EDGE, EDGE), :]
+            return gchip[pl.ds((2 - a) * EDGE, EDGE), :]
         if s == 2:
             return score[pl.ds(rows * pair + (1 - a) * EDGE, EDGE), :]
         return gown[pl.ds(a * EDGE, EDGE), :]
@@ -172,7 +172,7 @@
 
 
 def early_kernel(rows, sown, gown, part_ref, sides_ref, far_ref, half_ref, full_ref):
-    slab, green = readers(rows, None, sown, gown, None)
+    slab, green = readers(rows, None, None, sown, gown, None)
     none = jnp.zeros((EDGE, EDGE), jnp.bfloat16)
     for k in range(2):
         o = green(1, 2 * k)[:, EDGE:]
@@ -210,9 +210,9 @@
 
 
 def main_kernel(
-    scale, rows, part_ref, sides_ref, schip, sown, gown, score, out_ref, occ_ref, half_ref, full_ref
+    scale, rows, part_ref, sides_ref, schip, gchip, sown, gown, score, out_ref, occ_ref, half_ref, full_ref
 ):
-    slab, green = readers(rows, schip, sown, gown, score)
+    slab, green = readers(rows, schip, gchip, sown, gown, score)
     none = jnp.zeros((EDGE, EDGE), jnp.bfloat16)
     near = [green(s, 2 - s)[:, :EDGE] for s in range(3)]
     mid = jnp.concatenate(near, 1)
@@ -301,11 +301,13 @@
         scratch_shapes=[pltpu.VMEM((2, 3 * PITCH, LANES), jnp.float32)],
         name="prep",
     )(omask.T, vmask.T, count, occupied[0], virtual[0])
+    chip_next = [order[(j - 1 + 2 * (j % 2)) % members] for j in range(members)]
+    gchip = lax.ppermute(greens[: 2 * EDGE], "blk", list(enumerate(chip_next)))
     greens = lax.ppermute(greens, "blk", list(enumerate(order)))
     own = lax.all_to_all(rows, "blk", split_axis=0, concat_axis=0, tiled=True)
     core_pairs = [(order[j], order[j + 1 - 2 * (j % 2)]) for j in range(members)]
-    chip_pairs = [(order[j], order[(j - 1 + 2 * (j % 2)) % members]) for j in range(members)]
-    to_chip = jnp.concatenate([own[:, : 2 * HALF].reshape(-1, LANES), greens[: 2 * EDGE]], 0)
+    chip_pairs = list(zip(order, chip_next))
+    to_chip = own[:, : 2 * HALF].reshape(-1, LANES)
     to_core = jnp.concatenate([own[:, HALF:].reshape(-1, LANES), greens[EDGE:]], 0)
     schip = lax.ppermute(to_chip, "blk", chip_pairs)
     score = lax.ppermute(to_core, "blk", core_pairs)
@@ -328,7 +330,7 @@
     part = pl.pallas_call(
         functools.partial(main_kernel, 1.0 / math.sqrt(5 * EDGE * EDGE * total), members),
         out_shape=jax.ShapeDtypeStruct((members, members), jnp.float32),
-        in_specs=[VMEM] * 6,
+        in_specs=[VMEM] * 7,
         out_specs=VMEM,
         scratch_shapes=[
             pltpu.VMEM((6 * EDGE, 3 * LANES), jnp.bfloat16),
@@ -337,7 +339,7 @@
         ],
         compiler_params=pltpu.CompilerParams(vmem_limit_bytes=24 * 1024 * 1024),
         name="products",
-    )(early, sides, schip, own, greens, score)
+    )(early, sides, schip, gchip, own, greens, score)
     mine = lax.all_to_all(part, "blk", split_axis=0, concat_axis=0, tiled=True)
     return jnp.sum(mine, axis=0, keepdims=True)
 

time: 39.9 us -> 40.1 us (level)
  waiting for transfers between devices: 11.2 us -> 9.54 us
  starting transfers between devices: 12.3 us -> 13.9 us
  local copies, waits for them, and re-layouts: 0.07 us -> 0.58 us
    ppermute x1, waiting for transfers between devices: 4.9 us -> 0.01 us  [body(): schip = lax.ppermute(to_chip, 'blk', chip_pairs)]
    ppermute x0 -> x1, waiting for transfers between devices: none -> 3.27 us  [body(): gchip = lax.ppermute(greens[:2 * EDGE], 'blk', list(enumerate(chip_next)))]
    ppermute x0 -> x1, starting transfers between devices: none -> 1.56 us  [body(): gchip = lax.ppermute(greens[:2 * EDGE], 'blk', list(enumerate(chip_next)))]
    unnamed x0 -> x2, local copies, waits for them, and re-layouts: none -> 0.53 us
  transfers between devices with their start and end apart: 4 -> 5, of which waited for: 3 -> 3; matrix products, arithmetic and copies ran while one was open for 0% -> 0% of each run, Pallas kernels for 7% -> 7%
where the time goes in v12:
time: 40.1 us; the launch traced here: 39.7 us
  starting transfers between devices  13.9 us (35%)
  waiting for transfers between devices  9.54 us (24%)
  blocking collectives  8.99 us (22%)
  Pallas kernels  6.05 us (15%)
  local copies, waits for them, and re-layouts  0.58 us (1%)
  other arithmetic  0.57 us (1%)
    all_to_all x1, blocking collectives, body(): mine = lax.all_to_all(part, 'blk', split_axis=0, concat_axis=0, tiled=True)  8.99 us
    all_to_all x1, starting transfers between devices, body(): own = lax.all_to_all(rows, 'blk', split_axis=0, concat_axis=0, tiled=True)  7.4 us
    ppermute x1, starting transfers between devices, body(): greens = lax.ppermute(greens, 'blk', list(enumerate(order)))  4.72 us
    ppermute x1, waiting for transfers between devices, body(): gchip = lax.ppermute(greens[:2 * EDGE], 'blk', list(enumerate(chip_next)))  3.27 us
    ppermute x1, waiting for transfers between devices, body(): greens = lax.ppermute(greens, 'blk', list(enumerate(order)))  3.2 us
    all_to_all x1, waiting for transfers between devices, body(): own = lax.all_to_all(rows, 'blk', split_axis=0, concat_axis=0, tiled=True)  3.07 us
    pallas_call x1, Pallas kernels, body(): pl.pallas_call(functools.partial(pack_kernel, works_on), out_shape=jax.Sh...  1.97 us
    pallas_call x1, Pallas kernels, body(): pl.pallas_call(functools.partial(prep_kernel, total), out_shape=jax.Shape...  1.67 us
  transfers between devices with their start and end apart: 5, of which 3 were waited for; matrix products, arithmetic and copies ran while one was open for 0% of the time, Pallas kernels for 7%

profile of v12, /device:TPU:0, one launch (start us, length us, event | category | flops | bytes accessed | tf_op | source)
XLA Modules:
  0.0 39.7 jit_solution(8874793794399499436)
XLA Ops:
  0.0 2.0 %pack.1 = bf16[16,96,128]{2,1,0:T(8,128)(2,1)} custom-call(bf16[3,16,4096]{2,1,0:T(8,128)(2,1)} %bitcast.16, s32[3,16]{1,0:T(4,128)} %bitcast.20), custom_call_target="tpu_custom_call" | custom-call | tf_op jit(solution)/shard_map/pack/pallas_call | solution.py:281
  2.0 7.4 %all-to-all-start = ((bf16[16,96,128]{2,1,0:T(8,128)(2,1)}), bf16[16,96,128]{2,1,0:T(8,128)(2,1)S(1)}, u32[]{:S(2)}, u32[]{:S(2)}) async-start(bf16[16,96,128]{2,1,0:T(8,128)(2,1)} %pack.1), calls=%async_computation | async-start | bytes 786432 | tf_op jit(solution)/shard_map/all_to_all | solution.py:307
  9.4 1.7 %prep.1 = bf16[192,128]{1,0:T(8,128)(2,1)} custom-call(s32[3,16]{1,0:T(4,128)} %bitcast.21, s32[3,16]{1,0:T(4,128)} %bitcast.22, s32[16]{0:T(128)} %count.1, bf16[3,4096]{1,0:T(4,128)(2,1)} %bitcast.18, bf16[3,4096]{1,0:T(4,128)(2,1)} %bitcast.19), custom_call_target="tpu_custom_call" | custom-call | tf_op jit(solution)/shard_map/prep/pallas_call | solution.py:296
  11.1 4.7 %collective-permute-start = (bf16[192,128]{1,0:T(8,128)(2,1)}, bf16[192,128]{1,0:T(8,128)(2,1)S(1)}, u32[]{:S(2)}, u32[]{:S(2)}) collective-permute-start(bf16[192,128]{1,0:T(8,128)(2,1)} %prep.1), channel_id=1, source_target_pairs={{0,6},{1,7},{2,2},{3,3},{4,0},{5,1},{6,4},{7,5},{8,8},{9,9},{10,12... | collective-permute-start | bytes 147464 | tf_op jit(solution)/shard_map/ppermute | solution.py:306
  15.8 3.2 %collective-permute-done.gown = bf16[192,128]{1,0:T(8,128)(2,1)S(1)} collective-permute-done((bf16[192,128]{1,0:T(8,128)(2,1)}, bf16[192,128]{1,0:T(8,128)(2,1)S(1)}, u32[]{:S(2)}, u32[]{:S(2)}) %collective-permute-start) | collective-permute-done | bytes 49184 | tf_op jit(solution)/shard_map/ppermute | solution.py:306
  19.0 3.1 %all-to-all-done.sown = bf16[16,96,128]{2,1,0:T(8,128)(2,1)S(1)} async-done(((bf16[16,96,128]{2,1,0:T(8,128)(2,1)}), bf16[16,96,128]{2,1,0:T(8,128)(2,1)S(1)}, u32[]{:S(2)}, u32[]{:S(2)}) %all-to-all-start) | async-done | bytes 393248 | tf_op jit(solution)/shard_map/all_to_all | solution.py:307
  22.1 0.1 fusion
  22.1 0.0 copy-start
  22.2 0.1 collective-permute-start.3
  22.2 0.2 collective-permute-start.1
  22.4 0.5 %copy-done = bf16[192,128]{1,0:T(8,128)(2,1)S(1)} copy-done((bf16[192,128]{1,0:T(8,128)(2,1)S(1)}, bf16[192,128]{1,0:T(8,128)(2,1)}, u32[]{:S(2)}) %copy-start) | copy-done | bytes 49176
  22.9 1.6 %collective-permute-start.2 = (bf16[128,128]{1,0:T(8,128)(2,1)S(1)}, bf16[128,128]{1,0:T(8,128)(2,1)S(1)}, u32[]{:S(2)}, u32[]{:S(2)}) collective-permute-start(bf16[128,128]{1,0:T(8,128)(2,1)S(1)} %slice.17), channel_id=1, source_target_pairs={{0,11},{1,2},{2,7},{3,0},{4,3},{5,4},{6,1},{7,8},{8,5},{9,12},{10,... | collective-permute-start | bytes 98312 | tf_op jit(solution)/shard_map/ppermute | solution.py:305
  24.5 1.1 %early.1 = (f32[16,16]{1,0:T(8,128)S(1)}, bf16[3,64,1024]{2,1,0:T(8,128)(2,1)S(1)}) custom-call(bf16[16,96,128]{2,1,0:T(8,128)(2,1)S(1)} %all-to-all-done.sown, bf16[192,128]{1,0:T(8,128)(2,1)S(1)} %collective-permute-done.gown), custom_call_target="tpu_custom_call" | custom-call | tf_op jit(solution)/shard_map/early/pallas_call | solution.py:314
  25.5 3.3 %collective-permute-done.2.gchip = bf16[128,128]{1,0:T(8,128)(2,1)S(1)} collective-permute-done((bf16[128,128]{1,0:T(8,128)(2,1)S(1)}, bf16[128,128]{1,0:T(8,128)(2,1)S(1)}, u32[]{:S(2)}, u32[]{:S(2)}) %collective-permute-start.2) | collective-permute-done | bytes 32800 | tf_op jit(solution)/shard_map/ppermute | solution.py:305
  28.8 0.0 collective-permute-done.1.schip
  28.8 0.0 collective-permute-done.3.score
  28.8 1.4 %products.1 = f32[16,16]{1,0:T(8,128)S(1)} custom-call(f32[16,16]{1,0:T(8,128)S(1)} %get-tuple-element.7.part_ref, bf16[3,64,1024]{2,1,0:T(8,128)(2,1)S(1)} %get-tuple-element.8.sides_ref, bf16[1024,128]{1,0:T(8,128)(2,1)S(1)} %collective-permute-done.1.schip, bf16[128,128]{1,0:T(8,128)(2,1)S(1)} %collective-permute-done.2.gchip, ...), custom_call_target="tpu_custom_call" | custom-call | tf_op jit(solution)/shard_map/products/pallas_call | solution.py:330
  30.2 9.0 %all_to_all.14 = f32[16,1,16]{2,1,0:T(1,128)S(1)} all-to-all(f32[16,1,16]{2,1,0:T(1,128)S(1)} %bitcast.14), channel_id=1, replica_groups=mesh['grp'=2,'blk'=16] {'blk'}, dimensions={0} | all-to-all | bytes 2048 | tf_op jit(solution)/shard_map/all_to_all | solution.py:343
  39.1 0.5 %reduce_sum.9 = f32[16]{0:T(128)} reduce(f32[16,1,16]{2,1,0:T(1,128)S(1)} %all_to_all.14, f32[]{:T(128)} %constant.0.clone.1), dimensions={0,1}, to_apply=%region_0.0 | reduce | flops 240 | bytes 1092 | tf_op jit(solution)/shard_map/reduce_sum | solution.py:344
  (3 shorter events, 0.0 us)
Async XLA Ops:
  2.0 20.1 %all-to-all-start = ((bf16[16,96,128]{2,1,0:T(8,128)(2,1)}), bf16[16,96,128]{2,1,0:T(8,128)(2,1)S(1)}, u32[]{:S(2)}, u32[]{:S(2)}) async-start(bf16[16,96,128]{2,1,0:T(8,128)(2,1)} %pack.1), calls=%async_computation | async-start | bytes 786432 | tf_op jit(solution)/shard_map/all_to_all | solution.py:307
  11.1 7.9 %collective-permute-start = (bf16[192,128]{1,0:T(8,128)(2,1)}, bf16[192,128]{1,0:T(8,128)(2,1)S(1)}, u32[]{:S(2)}, u32[]{:S(2)}) collective-permute-start(bf16[192,128]{1,0:T(8,128)(2,1)} %prep.1), channel_id=1, source_target_pairs={{0,6},{1,7},{2,2},{3,3},{4,0},{5,1},{6,4},{7,5},{8,8},{9,9},{10,12... | collective-permute-start | bytes 147464 | tf_op jit(solution)/shard_map/ppermute | solution.py:306
  22.1 0.8 %copy-start = (bf16[192,128]{1,0:T(8,128)(2,1)S(1)}, bf16[192,128]{1,0:T(8,128)(2,1)}, u32[]{:S(2)}) copy-start(bf16[192,128]{1,0:T(8,128)(2,1)} %prep.1) | copy-start | bytes 147460
  22.2 6.7 %collective-permute-start.3 = (bf16[1152,128]{1,0:T(8,128)(2,1)S(1)}, bf16[1152,128]{1,0:T(8,128)(2,1)S(1)}, u32[]{:S(2)}, u32[]{:S(2)}) collective-permute-start(bf16[1152,128]{1,0:T(8,128)(2,1)S(1)} %pad_maximum_fusion), channel_id=1, source_target_pairs={{6,7},{7,6},{2,3},{3,2},{0,1},{1,0},{4,5},{5,4},{8,9},{9,8},{12,13... | collective-permute-start | bytes 884744 | tf_op jit(solution)/shard_map/ppermute | solution.py:313
  22.2 6.6 %collective-permute-start.1 = (bf16[1024,128]{1,0:T(8,128)(2,1)S(1)}, bf16[1024,128]{1,0:T(8,128)(2,1)S(1)}, u32[]{:S(2)}, u32[]{:S(2)}) collective-permute-start(bf16[1024,128]{1,0:T(8,128)(2,1)S(1)} %bitcast.17), channel_id=1, source_target_pairs={{6,11},{7,2},{2,7},{3,0},{0,3},{1,4},{4,1},{5,8},{8,5},{9,12},{12,... | collective-permute-start | bytes 786440 | tf_op jit(solution)/shard_map/ppermute | solution.py:312
  22.9 5.9 %collective-permute-start.2 = (bf16[128,128]{1,0:T(8,128)(2,1)S(1)}, bf16[128,128]{1,0:T(8,128)(2,1)S(1)}, u32[]{:S(2)}, u32[]{:S(2)}) collective-permute-start(bf16[128,128]{1,0:T(8,128)(2,1)S(1)} %slice.17), channel_id=1, source_target_pairs={{0,11},{1,2},{2,7},{3,0},{4,3},{5,4},{6,1},{7,8},{8,5},{9,12},{10,... | collective-permute-start | bytes 98312 | tf_op jit(solution)/shard_map/ppermute | solution.py:305

commit v13 on v12

--- a/solution.py
+++ b/solution.py
@@ -151,7 +151,7 @@
             )
 
 
-def readers(rows, schip, gchip, sown, gown, score):
+def readers(schip, gchip, sown, gown, score, gcore):
     pair = 2 * HALF
 
     def slab(q, s, a):
@@ -165,14 +165,14 @@
         if s == 0:
             return gchip[pl.ds((2 - a) * EDGE, EDGE), :]
         if s == 2:
-            return score[pl.ds(rows * pair + (1 - a) * EDGE, EDGE), :]
+            return gcore[pl.ds((1 - a) * EDGE, EDGE), :]
         return gown[pl.ds(a * EDGE, EDGE), :]
 
     return slab, green
 
 
 def early_kernel(rows, sown, gown, part_ref, sides_ref, far_ref, half_ref, full_ref):
-    slab, green = readers(rows, None, None, sown, gown, None)
+    slab, green = readers(None, None, sown, gown, None, None)
     none = jnp.zeros((EDGE, EDGE), jnp.bfloat16)
     for k in range(2):
         o = green(1, 2 * k)[:, EDGE:]
@@ -210,9 +210,22 @@
 
 
 def main_kernel(
-    scale, rows, part_ref, sides_ref, schip, gchip, sown, gown, score, out_ref, occ_ref, half_ref, full_ref
+    scale,
+    rows,
+    part_ref,
+    sides_ref,
+    schip,
+    gchip,
+    sown,
+    gown,
+    score,
+    gcore,
+    out_ref,
+    occ_ref,
+    half_ref,
+    full_ref,
 ):
-    slab, green = readers(rows, schip, gchip, sown, gown, score)
+    slab, green = readers(schip, gchip, sown, gown, score, gcore)
     none = jnp.zeros((EDGE, EDGE), jnp.bfloat16)
     near = [green(s, 2 - s)[:, :EDGE] for s in range(3)]
     mid = jnp.concatenate(near, 1)
@@ -305,12 +318,14 @@
     gchip = lax.ppermute(greens[: 2 * EDGE], "blk", list(enumerate(chip_next)))
     greens = lax.ppermute(greens, "blk", list(enumerate(order)))
     own = lax.all_to_all(rows, "blk", split_axis=0, concat_axis=0, tiled=True)
+    own, greens, gchip = lax.optimization_barrier((own, greens, gchip))
     core_pairs = [(order[j], order[j + 1 - 2 * (j % 2)]) for j in range(members)]
     chip_pairs = list(zip(order, chip_next))
     to_chip = own[:, : 2 * HALF].reshape(-1, LANES)
-    to_core = jnp.concatenate([own[:, HALF:].reshape(-1, LANES), greens[EDGE:]], 0)
+    to_core = own[:, HALF:].reshape(-1, LANES)
     schip = lax.ppermute(to_chip, "blk", chip_pairs)
     score = lax.ppermute(to_core, "blk", core_pairs)
+    gcore = lax.ppermute(greens[EDGE:], "blk", core_pairs)
     early, sides = pl.pallas_call(
         functools.partial(early_kernel, members),
         out_shape=(
@@ -330,7 +345,7 @@
     part = pl.pallas_call(
         functools.partial(main_kernel, 1.0 / math.sqrt(5 * EDGE * EDGE * total), members),
         out_shape=jax.ShapeDtypeStruct((members, members), jnp.float32),
-        in_specs=[VMEM] * 7,
+        in_specs=[VMEM] * 8,
         out_specs=VMEM,
         scratch_shapes=[
             pltpu.VMEM((6 * EDGE, 3 * LANES), jnp.bfloat16),
@@ -339,7 +354,7 @@
         ],
         compiler_params=pltpu.CompilerParams(vmem_limit_bytes=24 * 1024 * 1024),
         name="products",
-    )(early, sides, schip, gchip, own, greens, score)
+    )(early, sides, schip, gchip, own, greens, score, gcore)
     mine = lax.all_to_all(part, "blk", split_axis=0, concat_axis=0, tiled=True)
     return jnp.sum(mine, axis=0, keepdims=True)
 

time: 40.1 us -> 39.8 us (level)
  waiting for transfers between devices: 9.54 us -> 7.8 us
  starting transfers between devices: 13.9 us -> 14.6 us
  blocking collectives: 8.99 us -> 9.44 us
    ppermute x1, waiting for transfers between devices: 0.01 us -> 4.12 us  [body(): schip = lax.ppermute(to_chip, 'blk', chip_pairs)]
    ppermute x1, waiting for transfers between devices: 3.2 us -> 0.01 us  [body(): greens = lax.ppermute(greens, 'blk', list(enumerate(order)))]
    ppermute x1, waiting for transfers between devices: 3.27 us -> 1.6 us  [body(): gchip = lax.ppermute(greens[:2 * EDGE], 'blk', list(enumerate(chip_next)))]
    all_to_all x1, waiting for transfers between devices: 3.07 us -> 2.06 us  [body(): own = lax.all_to_all(rows, 'blk', split_axis=0, concat_axis=0, tiled=True)]
    slice x1, local copies, waits for them, and re-layouts: 0.01 us -> 0.77 us  [body(): gchip = lax.ppermute(greens[:2 * EDGE], 'blk', list(enumerate(chip_next)))]
    unnamed x2 -> x0, local copies, waits for them, and re-layouts: 0.53 us -> none
    ppermute x0 -> x1, starting transfers between devices: none -> 0.5 us  [body(): gcore = lax.ppermute(greens[EDGE:], 'blk', core_pairs)]
    all_to_all x1, blocking collectives: 8.99 us -> 9.44 us  [body(): mine = lax.all_to_all(part, 'blk', split_axis=0, concat_axis=0, tiled=True)]
  transfers between devices with their start and end apart: 5 -> 6, of which waited for: 3 -> 3; matrix products, arithmetic and copies ran while one was open for 0% -> 2% of each run, Pallas kernels for 7% -> 7%
where the time goes in v13:
time: 39.8 us; the launch traced here: 39.3 us
  starting transfers between devices  14.6 us (37%)
  blocking collectives  9.44 us (24%)
  waiting for transfers between devices  7.8 us (20%)
  Pallas kernels  6.05 us (15%)
  local copies, waits for them, and re-layouts  0.84 us (2%)
  other arithmetic  0.54 us (1%)
    all_to_all x1, blocking collectives, body(): mine = lax.all_to_all(part, 'blk', split_axis=0, concat_axis=0, tiled=True)  9.44 us
    all_to_all x1, starting transfers between devices, body(): own = lax.all_to_all(rows, 'blk', split_axis=0, concat_axis=0, tiled=True)  7.4 us
    ppermute x1, starting transfers between devices, body(): greens = lax.ppermute(greens, 'blk', list(enumerate(order)))  4.72 us
    ppermute x1, waiting for transfers between devices, body(): schip = lax.ppermute(to_chip, 'blk', chip_pairs)  4.12 us
    all_to_all x1, waiting for transfers between devices, body(): own = lax.all_to_all(rows, 'blk', split_axis=0, concat_axis=0, tiled=True)  2.06 us
    pallas_call x1, Pallas kernels, body(): pl.pallas_call(functools.partial(pack_kernel, works_on), out_shape=jax.Sh...  1.97 us
    ppermute x1, starting transfers between devices, body(): gchip = lax.ppermute(greens[:2 * EDGE], 'blk', list(enumerate(chip_next)))  1.84 us
    pallas_call x1, Pallas kernels, body(): pl.pallas_call(functools.partial(prep_kernel, total), out_shape=jax.Shape...  1.67 us
  transfers between devices with their start and end apart: 6, of which 3 were waited for; matrix products, arithmetic and copies ran while one was open for 2% of the time, Pallas kernels for 7%

profile of v13, /device:TPU:0, one launch (start us, length us, event | category | flops | bytes accessed | tf_op | source)
XLA Modules:
  0.0 39.3 jit_solution(9440230411256852496)
XLA Ops:
  0.0 2.0 %pack.1 = bf16[16,96,128]{2,1,0:T(8,128)(2,1)} custom-call(bf16[3,16,4096]{2,1,0:T(8,128)(2,1)} %bitcast.15, s32[3,16]{1,0:T(4,128)} %bitcast.20), custom_call_target="tpu_custom_call" | custom-call | tf_op jit(solution)/shard_map/pack/pallas_call | solution.py:294
  2.0 7.4 %all-to-all-start = ((bf16[16,96,128]{2,1,0:T(8,128)(2,1)}), bf16[16,96,128]{2,1,0:T(8,128)(2,1)S(1)}, u32[]{:S(2)}, u32[]{:S(2)}) async-start(bf16[16,96,128]{2,1,0:T(8,128)(2,1)} %pack.1), calls=%async_computation | async-start | bytes 786432 | tf_op jit(solution)/shard_map/all_to_all | solution.py:320
  9.4 1.7 %prep.1 = bf16[192,128]{1,0:T(8,128)(2,1)} custom-call(s32[3,16]{1,0:T(4,128)} %bitcast.21, s32[3,16]{1,0:T(4,128)} %bitcast.22, s32[16]{0:T(128)} %count.1, bf16[3,4096]{1,0:T(4,128)(2,1)} %bitcast.18, bf16[3,4096]{1,0:T(4,128)(2,1)} %bitcast.19), custom_call_target="tpu_custom_call" | custom-call | tf_op jit(solution)/shard_map/prep/pallas_call | solution.py:309
  11.1 4.7 %collective-permute-start = (bf16[192,128]{1,0:T(8,128)(2,1)}, bf16[192,128]{1,0:T(8,128)(2,1)S(1)}, u32[]{:S(2)}, u32[]{:S(2)}) collective-permute-start(bf16[192,128]{1,0:T(8,128)(2,1)} %prep.1), channel_id=1, source_target_pairs={{0,6},{1,7},{2,2},{3,3},{4,0},{5,1},{6,4},{7,5},{8,8},{9,9},{10,12... | collective-permute-start | bytes 147464 | tf_op jit(solution)/shard_map/ppermute | solution.py:319
  15.8 0.8 %slice.16 = bf16[128,128]{1,0:T(8,128)(2,1)S(1)} slice(bf16[192,128]{1,0:T(8,128)(2,1)} %prep.1), slice={[0:128], [0:128]} | slice | bytes 65536 | tf_op jit(solution)/shard_map/slice | solution.py:318
  16.6 1.8 %collective-permute-start.1 = (bf16[128,128]{1,0:T(8,128)(2,1)S(1)}, bf16[128,128]{1,0:T(8,128)(2,1)S(1)}, u32[]{:S(2)}, u32[]{:S(2)}) collective-permute-start(bf16[128,128]{1,0:T(8,128)(2,1)S(1)} %slice.16), channel_id=1, source_target_pairs={{0,11},{1,2},{2,7},{3,0},{4,3},{5,4},{6,1},{7,8},{8,5},{9,12},{10,... | collective-permute-start | bytes 98312 | tf_op jit(solution)/shard_map/ppermute | solution.py:318
  18.4 1.6 %collective-permute-done.1.gchip = bf16[128,128]{1,0:T(8,128)(2,1)S(1)} collective-permute-done((bf16[128,128]{1,0:T(8,128)(2,1)S(1)}, bf16[128,128]{1,0:T(8,128)(2,1)S(1)}, u32[]{:S(2)}, u32[]{:S(2)}) %collective-permute-start.1) | collective-permute-done | bytes 32800 | tf_op jit(solution)/shard_map/ppermute | solution.py:318
  20.0 0.0 collective-permute-done.gown
  20.0 2.1 %all-to-all-done.sown = bf16[16,96,128]{2,1,0:T(8,128)(2,1)S(1)} async-done(((bf16[16,96,128]{2,1,0:T(8,128)(2,1)}), bf16[16,96,128]{2,1,0:T(8,128)(2,1)S(1)}, u32[]{:S(2)}, u32[]{:S(2)}) %all-to-all-start) | async-done | bytes 393248 | tf_op jit(solution)/shard_map/all_to_all | solution.py:320
  22.1 0.1 fusion
  22.1 0.2 collective-permute-start.2
  22.3 0.0 collective-permute-start.3
  22.3 0.5 %collective-permute-start.4 = (bf16[128,128]{1,0:T(8,128)(2,1)S(1)}, bf16[128,128]{1,0:T(8,128)(2,1)S(1)}, u32[]{:S(2)}, u32[]{:S(2)}) collective-permute-start(bf16[128,128]{1,0:T(8,128)(2,1)S(1)} %slice.15), channel_id=1, source_target_pairs={{6,7},{7,6},{2,3},{3,2},{0,1},{1,0},{4,5},{5,4},{8,9},{9,8},{12,13... | collective-permute-start | bytes 98312 | tf_op jit(solution)/shard_map/ppermute | solution.py:328
  22.8 1.0 %early.1 = (f32[16,16]{1,0:T(8,128)S(1)}, bf16[3,64,1024]{2,1,0:T(8,128)(2,1)S(1)}) custom-call(bf16[16,96,128]{2,1,0:T(8,128)(2,1)S(1)} %all-to-all-done.sown, bf16[192,128]{1,0:T(8,128)(2,1)S(1)} %collective-permute-done.gown), custom_call_target="tpu_custom_call" | custom-call | tf_op jit(solution)/shard_map/early/pallas_call | solution.py:329
  23.8 0.0 collective-permute-done.4.gcore
  23.9 4.1 %collective-permute-done.2.schip = bf16[1024,128]{1,0:T(8,128)(2,1)S(1)} collective-permute-done((bf16[1024,128]{1,0:T(8,128)(2,1)S(1)}, bf16[1024,128]{1,0:T(8,128)(2,1)S(1)}, u32[]{:S(2)}, u32[]{:S(2)}) %collective-permute-start.2) | collective-permute-done | bytes 262176 | tf_op jit(solution)/shard_map/ppermute | solution.py:326
  28.0 0.0 collective-permute-done.3.score
  28.0 1.4 %products.1 = f32[16,16]{1,0:T(8,128)S(1)} custom-call(f32[16,16]{1,0:T(8,128)S(1)} %get-tuple-element.12.part_ref, bf16[3,64,1024]{2,1,0:T(8,128)(2,1)S(1)} %get-tuple-element.13.sides_ref, bf16[1024,128]{1,0:T(8,128)(2,1)S(1)} %collective-permute-done.2.schip, bf16[128,128]{1,0:T(8,128)(2,1)S(1)} %collective-permute-done.1.gchip, ...), custom_call_target="tpu_custom_call" | custom-call | tf_op jit(solution)/shard_map/products/pallas_call | solution.py:345
  29.3 9.4 %all_to_all.14 = f32[16,1,16]{2,1,0:T(1,128)S(1)} all-to-all(f32[16,1,16]{2,1,0:T(1,128)S(1)} %bitcast.14), channel_id=1, replica_groups=mesh['grp'=2,'blk'=16] {'blk'}, dimensions={0} | all-to-all | bytes 2048 | tf_op jit(solution)/shard_map/all_to_all | solution.py:358
  38.8 0.5 %reduce_sum.9 = f32[16]{0:T(128)} reduce(f32[16,1,16]{2,1,0:T(1,128)S(1)} %all_to_all.14, f32[]{:T(128)} %constant.0.clone.1), dimensions={0,1}, to_apply=%region_0.0 | reduce | flops 240 | bytes 1092 | tf_op jit(solution)/shard_map/reduce_sum | solution.py:359
  (1 shorter events, 0.0 us)
Async XLA Ops:
  2.0 20.1 %all-to-all-start = ((bf16[16,96,128]{2,1,0:T(8,128)(2,1)}), bf16[16,96,128]{2,1,0:T(8,128)(2,1)S(1)}, u32[]{:S(2)}, u32[]{:S(2)}) async-start(bf16[16,96,128]{2,1,0:T(8,128)(2,1)} %pack.1), calls=%async_computation | async-start | bytes 786432 | tf_op jit(solution)/shard_map/all_to_all | solution.py:320
  11.1 8.9 %collective-permute-start = (bf16[192,128]{1,0:T(8,128)(2,1)}, bf16[192,128]{1,0:T(8,128)(2,1)S(1)}, u32[]{:S(2)}, u32[]{:S(2)}) collective-permute-start(bf16[192,128]{1,0:T(8,128)(2,1)} %prep.1), channel_id=1, source_target_pairs={{0,6},{1,7},{2,2},{3,3},{4,0},{5,1},{6,4},{7,5},{8,8},{9,9},{10,12... | collective-permute-start | bytes 147464 | tf_op jit(solution)/shard_map/ppermute | solution.py:319
  16.6 3.4 %collective-permute-start.1 = (bf16[128,128]{1,0:T(8,128)(2,1)S(1)}, bf16[128,128]{1,0:T(8,128)(2,1)S(1)}, u32[]{:S(2)}, u32[]{:S(2)}) collective-permute-start(bf16[128,128]{1,0:T(8,128)(2,1)S(1)} %slice.16), channel_id=1, source_target_pairs={{0,11},{1,2},{2,7},{3,0},{4,3},{5,4},{6,1},{7,8},{8,5},{9,12},{10,... | collective-permute-start | bytes 98312 | tf_op jit(solution)/shard_map/ppermute | solution.py:318
  22.1 5.9 %collective-permute-start.2 = (bf16[1024,128]{1,0:T(8,128)(2,1)S(1)}, bf16[1024,128]{1,0:T(8,128)(2,1)S(1)}, u32[]{:S(2)}, u32[]{:S(2)}) collective-permute-start(bf16[1024,128]{1,0:T(8,128)(2,1)S(1)} %bitcast.17), channel_id=1, source_target_pairs={{6,11},{7,2},{2,7},{3,0},{0,3},{1,4},{4,1},{5,8},{8,5},{9,12},{12,... | collective-permute-start | bytes 786440 | tf_op jit(solution)/shard_map/ppermute | solution.py:326
  22.3 5.7 %collective-permute-start.3 = (bf16[1024,128]{1,0:T(8,128)(2,1)S(1)}, bf16[1024,128]{1,0:T(8,128)(2,1)S(1)}, u32[]{:S(2)}, u32[]{:S(2)}) collective-permute-start(bf16[1024,128]{1,0:T(8,128)(2,1)S(1)} %bitcast.16), channel_id=1, source_target_pairs={{6,7},{7,6},{2,3},{3,2},{0,1},{1,0},{4,5},{5,4},{8,9},{9,8},{12,13... | collective-permute-start | bytes 786440 | tf_op jit(solution)/shard_map/ppermute | solution.py:327
  22.3 1.6 %collective-permute-start.4 = (bf16[128,128]{1,0:T(8,128)(2,1)S(1)}, bf16[128,128]{1,0:T(8,128)(2,1)S(1)}, u32[]{:S(2)}, u32[]{:S(2)}) collective-permute-start(bf16[128,128]{1,0:T(8,128)(2,1)S(1)} %slice.15), channel_id=1, source_target_pairs={{6,7},{7,6},{2,3},{3,2},{0,1},{1,0},{4,5},{5,4},{8,9},{9,8},{12,13... | collective-permute-start | bytes 98312 | tf_op jit(solution)/shard_map/ppermute | solution.py:328

commit v14 on v13

--- a/solution.py
+++ b/solution.py
@@ -60,7 +60,7 @@
         copy.wait()
 
 
-def prep_kernel(total, omask, vmask, count, occ_ref, vir_ref, out_ref, rows_ref):
+def prep_kernel(total, omask, vmask, count, occ_ref, vir_ref, out_ref, chip_ref, rows_ref):
     own = lax.axis_index("blk")
     for k, ref in enumerate((occ_ref, vir_ref)):
         for c in range(HALF):
@@ -89,6 +89,7 @@
             out_ref[pl.ds(at + par * HALF, HALF), :] = jnp.where(
                 left, turned[par * HALF : (par + 1) * HALF], occ[a][par]
             ).astype(jnp.bfloat16)
+    chip_ref[...] = out_ref[pl.ds(0, 2 * EDGE), :]
 
 
 def halves(slab, rows_at, j):
@@ -306,16 +307,19 @@
         compiler_params=pltpu.CompilerParams(vmem_limit_bytes=63 * 1024 * 1024),
         name="pack",
     )(jnp.transpose(integrals[0], (1, 0, 2)), imask.T)
-    greens = pl.pallas_call(
+    greens, gchip = pl.pallas_call(
         functools.partial(prep_kernel, total),
-        out_shape=jax.ShapeDtypeStruct((6 * HALF, LANES), jnp.bfloat16),
+        out_shape=(
+            jax.ShapeDtypeStruct((6 * HALF, LANES), jnp.bfloat16),
+            jax.ShapeDtypeStruct((4 * HALF, LANES), jnp.bfloat16),
+        ),
         in_specs=[SMEM] * 3 + [VMEM] * 2,
-        out_specs=VMEM,
+        out_specs=(VMEM, VMEM),
         scratch_shapes=[pltpu.VMEM((2, 3 * PITCH, LANES), jnp.float32)],
         name="prep",
     )(omask.T, vmask.T, count, occupied[0], virtual[0])
     chip_next = [order[(j - 1 + 2 * (j % 2)) % members] for j in range(members)]
-    gchip = lax.ppermute(greens[: 2 * EDGE], "blk", list(enumerate(chip_next)))
+    gchip = lax.ppermute(gchip, "blk", list(enumerate(chip_next)))
     greens = lax.ppermute(greens, "blk", list(enumerate(order)))
     own = lax.all_to_all(rows, "blk", split_axis=0, concat_axis=0, tiled=True)
     own, greens, gchip = lax.optimization_barrier((own, greens, gchip))

time: 39.8 us -> 39.7 us (level)
  local copies, waits for them, and re-layouts: 0.84 us -> 0.07 us
  waiting for transfers between devices: 7.8 us -> 8.48 us
    slice x1 -> x0, local copies, waits for them, and re-layouts: 0.77 us -> none  [body(): gchip = lax.ppermute(greens[:2 * EDGE], 'blk', list(enumerate(chip_next)))]
  transfers between devices with their start and end apart: 6 -> 6, of which waited for: 3 -> 3; matrix products, arithmetic and copies ran while one was open for 2% -> 0% of each run, Pallas kernels for 7% -> 7%
where the time goes in v14:
time: 39.7 us; the launch traced here: 39.4 us
  starting transfers between devices  14.7 us (37%)
  blocking collectives  9.49 us (24%)
  waiting for transfers between devices  8.48 us (21%)
  Pallas kernels  6.09 us (15%)
  other arithmetic  0.54 us (1%)
    all_to_all x1, blocking collectives, body(): mine = lax.all_to_all(part, 'blk', split_axis=0, concat_axis=0, tiled=True)  9.49 us
    all_to_all x1, starting transfers between devices, body(): own = lax.all_to_all(rows, 'blk', split_axis=0, concat_axis=0, tiled=True)  7.4 us
    ppermute x1, starting transfers between devices, body(): greens = lax.ppermute(greens, 'blk', list(enumerate(order)))  4.72 us
    ppermute x1, waiting for transfers between devices, body(): schip = lax.ppermute(to_chip, 'blk', chip_pairs)  4.12 us
    all_to_all x1, waiting for transfers between devices, body(): own = lax.all_to_all(rows, 'blk', split_axis=0, concat_axis=0, tiled=True)  2.42 us
    pallas_call x1, Pallas kernels, body(): pl.pallas_call(functools.partial(pack_kernel, works_on), out_shape=jax.Sh...  1.98 us
    ppermute x1, waiting for transfers between devices, body(): gchip = lax.ppermute(gchip, 'blk', list(enumerate(chip_next)))  1.91 us
    ppermute x1, starting transfers between devices, body(): gchip = lax.ppermute(gchip, 'blk', list(enumerate(chip_next)))  1.9 us
  transfers between devices with their start and end apart: 6, of which 3 were waited for; matrix products, arithmetic and copies ran while one was open for 0% of the time, Pallas kernels for 7%

profile of v14, /device:TPU:0, one launch (start us, length us, event | category | flops | bytes accessed | tf_op | source)
XLA Modules:
  0.0 39.4 jit_solution(9622784359749145465)
XLA Ops:
  0.0 2.0 %pack.1 = bf16[16,96,128]{2,1,0:T(8,128)(2,1)} custom-call(bf16[3,16,4096]{2,1,0:T(8,128)(2,1)} %bitcast.15, s32[3,16]{1,0:T(4,128)} %bitcast.20), custom_call_target="tpu_custom_call" | custom-call | tf_op jit(solution)/shard_map/pack/pallas_call | solution.py:295
  2.0 7.4 %all-to-all-start = ((bf16[16,96,128]{2,1,0:T(8,128)(2,1)}), bf16[16,96,128]{2,1,0:T(8,128)(2,1)S(1)}, u32[]{:S(2)}, u32[]{:S(2)}) async-start(bf16[16,96,128]{2,1,0:T(8,128)(2,1)} %pack.1), calls=%async_computation | async-start | bytes 786432 | tf_op jit(solution)/shard_map/all_to_all | solution.py:324
  9.4 1.7 %prep.1 = (bf16[192,128]{1,0:T(8,128)(2,1)}, bf16[128,128]{1,0:T(8,128)(2,1)}) custom-call(s32[3,16]{1,0:T(4,128)} %bitcast.21, s32[3,16]{1,0:T(4,128)} %bitcast.22, s32[16]{0:T(128)} %count.1, bf16[3,4096]{1,0:T(4,128)(2,1)} %bitcast.18, bf16[3,4096]{1,0:T(4,128)(2,1)} %bitcast.19), custom_call_target="tpu_custom_call" | custom-call | tf_op jit(solution)/shard_map/prep/pallas_call | solution.py:310
  11.1 4.7 %collective-permute-start = (bf16[192,128]{1,0:T(8,128)(2,1)}, bf16[192,128]{1,0:T(8,128)(2,1)S(1)}, u32[]{:S(2)}, u32[]{:S(2)}) collective-permute-start(bf16[192,128]{1,0:T(8,128)(2,1)} %get-tuple-element.12), channel_id=1, source_target_pairs={{0,6},{1,7},{2,2},{3,3},{4,0},{5,1},{6,4},{7,5},{8,8},{9,9},{10,12... | collective-permute-start | bytes 147464 | tf_op jit(solution)/shard_map/ppermute | solution.py:323
  15.8 1.9 %collective-permute-start.1 = (bf16[128,128]{1,0:T(8,128)(2,1)}, bf16[128,128]{1,0:T(8,128)(2,1)S(1)}, u32[]{:S(2)}, u32[]{:S(2)}) collective-permute-start(bf16[128,128]{1,0:T(8,128)(2,1)} %get-tuple-element.13), channel_id=1, source_target_pairs={{0,11},{1,2},{2,7},{3,0},{4,3},{5,4},{6,1},{7,8},{8,5},{9,12},{10,... | collective-permute-start | bytes 98312 | tf_op jit(solution)/shard_map/ppermute | solution.py:322
  17.7 1.9 %collective-permute-done.1.gchip = bf16[128,128]{1,0:T(8,128)(2,1)S(1)} collective-permute-done((bf16[128,128]{1,0:T(8,128)(2,1)}, bf16[128,128]{1,0:T(8,128)(2,1)S(1)}, u32[]{:S(2)}, u32[]{:S(2)}) %collective-permute-start.1) | collective-permute-done | bytes 32800 | tf_op jit(solution)/shard_map/ppermute | solution.py:322
  19.6 0.0 collective-permute-done.gown
  19.6 2.4 %all-to-all-done.sown = bf16[16,96,128]{2,1,0:T(8,128)(2,1)S(1)} async-done(((bf16[16,96,128]{2,1,0:T(8,128)(2,1)}), bf16[16,96,128]{2,1,0:T(8,128)(2,1)S(1)}, u32[]{:S(2)}, u32[]{:S(2)}) %all-to-all-start) | async-done | bytes 393248 | tf_op jit(solution)/shard_map/all_to_all | solution.py:324
  22.1 0.1 fusion
  22.1 0.2 collective-permute-start.2
  22.3 0.0 collective-permute-start.3
  22.3 0.5 %collective-permute-start.4 = (bf16[128,128]{1,0:T(8,128)(2,1)S(1)}, bf16[128,128]{1,0:T(8,128)(2,1)S(1)}, u32[]{:S(2)}, u32[]{:S(2)}) collective-permute-start(bf16[128,128]{1,0:T(8,128)(2,1)S(1)} %slice.11), channel_id=1, source_target_pairs={{6,7},{7,6},{2,3},{3,2},{0,1},{1,0},{4,5},{5,4},{8,9},{9,8},{12,13... | collective-permute-start | bytes 98312 | tf_op jit(solution)/shard_map/ppermute | solution.py:332
  22.8 1.0 %early.1 = (f32[16,16]{1,0:T(8,128)S(1)}, bf16[3,64,1024]{2,1,0:T(8,128)(2,1)S(1)}) custom-call(bf16[16,96,128]{2,1,0:T(8,128)(2,1)S(1)} %all-to-all-done.sown, bf16[192,128]{1,0:T(8,128)(2,1)S(1)} %collective-permute-done.gown), custom_call_target="tpu_custom_call" | custom-call | tf_op jit(solution)/shard_map/early/pallas_call | solution.py:333
  23.9 0.0 collective-permute-done.4.gcore
  23.9 4.1 %collective-permute-done.2.schip = bf16[1024,128]{1,0:T(8,128)(2,1)S(1)} collective-permute-done((bf16[1024,128]{1,0:T(8,128)(2,1)S(1)}, bf16[1024,128]{1,0:T(8,128)(2,1)S(1)}, u32[]{:S(2)}, u32[]{:S(2)}) %collective-permute-start.2) | collective-permute-done | bytes 262176 | tf_op jit(solution)/shard_map/ppermute | solution.py:330
  28.0 0.0 collective-permute-done.3.score
  28.0 1.3 %products.1 = f32[16,16]{1,0:T(8,128)S(1)} custom-call(f32[16,16]{1,0:T(8,128)S(1)} %get-tuple-element.16.part_ref, bf16[3,64,1024]{2,1,0:T(8,128)(2,1)S(1)} %get-tuple-element.17.sides_ref, bf16[1024,128]{1,0:T(8,128)(2,1)S(1)} %collective-permute-done.2.schip, bf16[128,128]{1,0:T(8,128)(2,1)S(1)} %collective-permute-done.1.gchip, ...), custom_call_target="tpu_custom_call" | custom-call | tf_op jit(solution)/shard_map/products/pallas_call | solution.py:349
  29.4 9.5 %all_to_all.14 = f32[16,1,16]{2,1,0:T(1,128)S(1)} all-to-all(f32[16,1,16]{2,1,0:T(1,128)S(1)} %bitcast.14), channel_id=1, replica_groups=mesh['grp'=2,'blk'=16] {'blk'}, dimensions={0} | all-to-all | bytes 2048 | tf_op jit(solution)/shard_map/all_to_all | solution.py:362
  38.8 0.5 %reduce_sum.9 = f32[16]{0:T(128)} reduce(f32[16,1,16]{2,1,0:T(1,128)S(1)} %all_to_all.14, f32[]{:T(128)} %constant.0.clone.1), dimensions={0,1}, to_apply=%region_0.0 | reduce | flops 240 | bytes 1092 | tf_op jit(solution)/shard_map/reduce_sum | solution.py:363
  (1 shorter events, 0.0 us)
Async XLA Ops:
  2.0 20.1 %all-to-all-start = ((bf16[16,96,128]{2,1,0:T(8,128)(2,1)}), bf16[16,96,128]{2,1,0:T(8,128)(2,1)S(1)}, u32[]{:S(2)}, u32[]{:S(2)}) async-start(bf16[16,96,128]{2,1,0:T(8,128)(2,1)} %pack.1), calls=%async_computation | async-start | bytes 786432 | tf_op jit(solution)/shard_map/all_to_all | solution.py:324
  11.1 8.5 %collective-permute-start = (bf16[192,128]{1,0:T(8,128)(2,1)}, bf16[192,128]{1,0:T(8,128)(2,1)S(1)}, u32[]{:S(2)}, u32[]{:S(2)}) collective-permute-start(bf16[192,128]{1,0:T(8,128)(2,1)} %get-tuple-element.12), channel_id=1, source_target_pairs={{0,6},{1,7},{2,2},{3,3},{4,0},{5,1},{6,4},{7,5},{8,8},{9,9},{10,12... | collective-permute-start | bytes 147464 | tf_op jit(solution)/shard_map/ppermute | solution.py:323
  15.8 3.8 %collective-permute-start.1 = (bf16[128,128]{1,0:T(8,128)(2,1)}, bf16[128,128]{1,0:T(8,128)(2,1)S(1)}, u32[]{:S(2)}, u32[]{:S(2)}) collective-permute-start(bf16[128,128]{1,0:T(8,128)(2,1)} %get-tuple-element.13), channel_id=1, source_target_pairs={{0,11},{1,2},{2,7},{3,0},{4,3},{5,4},{6,1},{7,8},{8,5},{9,12},{10,... | collective-permute-start | bytes 98312 | tf_op jit(solution)/shard_map/ppermute | solution.py:322
  22.1 5.9 %collective-permute-start.2 = (bf16[1024,128]{1,0:T(8,128)(2,1)S(1)}, bf16[1024,128]{1,0:T(8,128)(2,1)S(1)}, u32[]{:S(2)}, u32[]{:S(2)}) collective-permute-start(bf16[1024,128]{1,0:T(8,128)(2,1)S(1)} %bitcast.17), channel_id=1, source_target_pairs={{6,11},{7,2},{2,7},{3,0},{0,3},{1,4},{4,1},{5,8},{8,5},{9,12},{12,... | collective-permute-start | bytes 786440 | tf_op jit(solution)/shard_map/ppermute | solution.py:330
  22.3 5.7 %collective-permute-start.3 = (bf16[1024,128]{1,0:T(8,128)(2,1)S(1)}, bf16[1024,128]{1,0:T(8,128)(2,1)S(1)}, u32[]{:S(2)}, u32[]{:S(2)}) collective-permute-start(bf16[1024,128]{1,0:T(8,128)(2,1)S(1)} %bitcast.16), channel_id=1, source_target_pairs={{6,7},{7,6},{2,3},{3,2},{0,1},{1,0},{4,5},{5,4},{8,9},{9,8},{12,13... | collective-permute-start | bytes 786440 | tf_op jit(solution)/shard_map/ppermute | solution.py:331
  22.3 1.6 %collective-permute-start.4 = (bf16[128,128]{1,0:T(8,128)(2,1)S(1)}, bf16[128,128]{1,0:T(8,128)(2,1)S(1)}, u32[]{:S(2)}, u32[]{:S(2)}) collective-permute-start(bf16[128,128]{1,0:T(8,128)(2,1)S(1)} %slice.11), channel_id=1, source_target_pairs={{6,7},{7,6},{2,3},{3,2},{0,1},{1,0},{4,5},{5,4},{8,9},{9,8},{12,13... | collective-permute-start | bytes 98312 | tf_op jit(solution)/shard_map/ppermute | solution.py:332

commit v15 on v14

--- a/solution.py
+++ b/solution.py
@@ -101,15 +101,13 @@
     return [jnp.concatenate(even, 1), jnp.concatenate(odd, 1)]
 
 
-def unfold(block, j, g, half, full_ref):
+def unfold(block, members, g, full_ref):
     block = block.astype(jnp.bfloat16)
-    place = pl.ds(g * HALF, HALF)
-    for k in range(2):
-        even = block[:HALF, k * LANES : (k + 1) * LANES]
-        odd = block[HALF:, k * LANES : (k + 1) * LANES]
-        first = 2 * (j + 2 * k) + half
-        full_ref[first, place, :] = jnp.concatenate([even[:, :EDGE], odd[:, :EDGE]], 1)
-        full_ref[first + 2, place, :] = jnp.concatenate([even[:, EDGE:], odd[:, EDGE:]], 1)
+    for k, q in enumerate(members):
+        lanes = slice(k * EDGE, (k + 1) * EDGE)
+        full_ref[q, pl.ds(g * HALF, HALF), :] = jnp.concatenate(
+            [block[:HALF, lanes], block[HALF:, lanes]], 1
+        )
 
 
 def inner(slabs, full_ref, rows, store):
@@ -202,7 +200,8 @@
                 preferred_element_type=jnp.float32,
             )
             for half in range(2):
-                unfold(full[half * EDGE : (half + 1) * EDGE], j, k, half, full_ref)
+                those = [2 * (j + n) + half for n in range(4)]
+                unfold(full[half * EDGE : (half + 1) * EDGE], those, k, full_ref)
 
     def store(p, q, sums):
         part_ref[p, q] = sums
@@ -239,15 +238,8 @@
     )
     used = ({0: 1, 1: 2}, {0: 0, 1: 1, 2: 2}, {1: 0, 2: 1})
     for s in range(3):
-        for t in range(3):
-            for half in range(2):
-                at = pl.ds((half * 3 + s) * EDGE, EDGE)
-                to = pl.ds(t * LANES, LANES)
-                if t in used[s]:
-                    o = green(s, used[s][t])[:, EDGE:]
-                    occ_ref[at, to] = jnp.concatenate([none, o] if half else [o, none], 1)
-                else:
-                    occ_ref[at, to] = jnp.zeros((EDGE, LANES), jnp.bfloat16)
+        o = [green(s, used[s][t])[:, EDGE:] if t in used[s] else none for t in range(3)]
+        occ_ref[pl.ds(s * EDGE, EDGE), :] = jnp.concatenate(o + [none], 1)
 
     for j in range(0, rows // 2, 2):
         own = [sides_ref[a, :, pl.ds(j * LANES, 2 * LANES)] for a in range(3)]
@@ -261,24 +253,21 @@
             jnp.concatenate(halves(slab, (0, 2), j) + [own[1]] + halves(slab, (2, 0), j), 0),
             preferred_element_type=jnp.float32,
         ).astype(jnp.bfloat16)
-        for t, piece in enumerate((both[:EDGE], middle, both[EDGE:])):
-            for k in range(2):
-                half_ref[pl.ds((j + k) * EDGE, EDGE), pl.ds(t * LANES, LANES)] = piece[
-                    :, k * LANES : (k + 1) * LANES
-                ]
-
-    for j in range(0, rows // 2, 4):
-        at = pl.ds(j * EDGE, 4 * EDGE)
+        pieces = (both[:EDGE], middle, both[EDGE:])
+        for k in range(4):
+            half_ref[pl.ds((2 * j + k) * EDGE, EDGE), :] = jnp.concatenate(
+                [piece[:, k * EDGE : (k + 1) * EDGE] for piece in pieces] + [none], 1
+            )
+
+    for q in range(0, rows, 4):
         full = lax.dot_general(
             occ_ref[...],
-            half_ref[at, :],
+            half_ref[pl.ds(q * EDGE, 4 * EDGE), :],
             NT,
             preferred_element_type=jnp.float32,
         )
-        for half in range(2):
-            for s in range(3):
-                block = full[(half * 3 + s) * EDGE : (half * 3 + s + 1) * EDGE]
-                unfold(block, j, s, half, full_ref)
+        for s in range(3):
+            unfold(full[s * EDGE : (s + 1) * EDGE], (q, q + 1, q + 2, q + 3), s, full_ref)
 
     def store(p, q, sums):
         out_ref[p, q] = scale * (sums + part_ref[p, q])
@@ -352,8 +341,8 @@
         in_specs=[VMEM] * 8,
         out_specs=VMEM,
         scratch_shapes=[
-            pltpu.VMEM((6 * EDGE, 3 * LANES), jnp.bfloat16),
-            pltpu.VMEM((members // 2 * EDGE, 3 * LANES), jnp.bfloat16),
+            pltpu.VMEM((3 * EDGE, 2 * LANES), jnp.bfloat16),
+            pltpu.VMEM((members * EDGE, 2 * LANES), jnp.bfloat16),
             pltpu.VMEM((members, 3 * HALF, LANES), jnp.bfloat16),
         ],
         compiler_params=pltpu.CompilerParams(vmem_limit_bytes=24 * 1024 * 1024),

time: 39.7 us -> 39.7 us (level)
  no operation moved by 1% of the time
where the time goes in v15:
time: 39.7 us; the launch traced here: 39.3 us
  starting transfers between devices  14.7 us (37%)
  blocking collectives  9.49 us (24%)
  waiting for transfers between devices  8.48 us (21%)
  Pallas kernels  6.02 us (15%)
  other arithmetic  0.54 us (1%)
    all_to_all x1, blocking collectives, body(): mine = lax.all_to_all(part, 'blk', split_axis=0, concat_axis=0, tiled=True)  9.49 us
    all_to_all x1, starting transfers between devices, body(): own = lax.all_to_all(rows, 'blk', split_axis=0, concat_axis=0, tiled=True)  7.4 us
    ppermute x1, starting transfers between devices, body(): greens = lax.ppermute(greens, 'blk', list(enumerate(order)))  4.72 us
    ppermute x1, waiting for transfers between devices, body(): schip = lax.ppermute(to_chip, 'blk', chip_pairs)  4.12 us
    all_to_all x1, waiting for transfers between devices, body(): own = lax.all_to_all(rows, 'blk', split_axis=0, concat_axis=0, tiled=True)  2.42 us
    pallas_call x1, Pallas kernels, body(): pl.pallas_call(functools.partial(pack_kernel, works_on), out_shape=jax.Sh...  1.98 us
    ppermute x1, waiting for transfers between devices, body(): gchip = lax.ppermute(gchip, 'blk', list(enumerate(chip_next)))  1.91 us
    ppermute x1, starting transfers between devices, body(): gchip = lax.ppermute(gchip, 'blk', list(enumerate(chip_next)))  1.9 us
  transfers between devices with their start and end apart: 6, of which 3 were waited for; matrix products, arithmetic and copies ran while one was open for 0% of the time, Pallas kernels for 7%

profile of v15, /device:TPU:0, one launch (start us, length us, event | category | flops | bytes accessed | tf_op | source)
XLA Modules:
  0.0 39.3 jit_solution(15941491854873309339)
XLA Ops:
  0.0 2.0 %pack.1 = bf16[16,96,128]{2,1,0:T(8,128)(2,1)} custom-call(bf16[3,16,4096]{2,1,0:T(8,128)(2,1)} %bitcast.15, s32[3,16]{1,0:T(4,128)} %bitcast.20), custom_call_target="tpu_custom_call" | custom-call | tf_op jit(solution)/shard_map/pack/pallas_call | solution.py:284
  2.0 7.4 %all-to-all-start = ((bf16[16,96,128]{2,1,0:T(8,128)(2,1)}), bf16[16,96,128]{2,1,0:T(8,128)(2,1)S(1)}, u32[]{:S(2)}, u32[]{:S(2)}) async-start(bf16[16,96,128]{2,1,0:T(8,128)(2,1)} %pack.1), calls=%async_computation | async-start | bytes 786432 | tf_op jit(solution)/shard_map/all_to_all | solution.py:313
  9.4 1.7 %prep.1 = (bf16[192,128]{1,0:T(8,128)(2,1)}, bf16[128,128]{1,0:T(8,128)(2,1)}) custom-call(s32[3,16]{1,0:T(4,128)} %bitcast.21, s32[3,16]{1,0:T(4,128)} %bitcast.22, s32[16]{0:T(128)} %count.1, bf16[3,4096]{1,0:T(4,128)(2,1)} %bitcast.18, bf16[3,4096]{1,0:T(4,128)(2,1)} %bitcast.19), custom_call_target="tpu_custom_call" | custom-call | tf_op jit(solution)/shard_map/prep/pallas_call | solution.py:299
  11.1 4.7 %collective-permute-start = (bf16[192,128]{1,0:T(8,128)(2,1)}, bf16[192,128]{1,0:T(8,128)(2,1)S(1)}, u32[]{:S(2)}, u32[]{:S(2)}) collective-permute-start(bf16[192,128]{1,0:T(8,128)(2,1)} %get-tuple-element.12), channel_id=1, source_target_pairs={{0,6},{1,7},{2,2},{3,3},{4,0},{5,1},{6,4},{7,5},{8,8},{9,9},{10,12... | collective-permute-start | bytes 147464 | tf_op jit(solution)/shard_map/ppermute | solution.py:312
  15.8 1.9 %collective-permute-start.1 = (bf16[128,128]{1,0:T(8,128)(2,1)}, bf16[128,128]{1,0:T(8,128)(2,1)S(1)}, u32[]{:S(2)}, u32[]{:S(2)}) collective-permute-start(bf16[128,128]{1,0:T(8,128)(2,1)} %get-tuple-element.13), channel_id=1, source_target_pairs={{0,11},{1,2},{2,7},{3,0},{4,3},{5,4},{6,1},{7,8},{8,5},{9,12},{10,... | collective-permute-start | bytes 98312 | tf_op jit(solution)/shard_map/ppermute | solution.py:311
  17.7 1.9 %collective-permute-done.1.gchip = bf16[128,128]{1,0:T(8,128)(2,1)S(1)} collective-permute-done((bf16[128,128]{1,0:T(8,128)(2,1)}, bf16[128,128]{1,0:T(8,128)(2,1)S(1)}, u32[]{:S(2)}, u32[]{:S(2)}) %collective-permute-start.1) | collective-permute-done | bytes 32800 | tf_op jit(solution)/shard_map/ppermute | solution.py:311
  19.6 0.0 collective-permute-done.gown
  19.6 2.4 %all-to-all-done.sown = bf16[16,96,128]{2,1,0:T(8,128)(2,1)S(1)} async-done(((bf16[16,96,128]{2,1,0:T(8,128)(2,1)}), bf16[16,96,128]{2,1,0:T(8,128)(2,1)S(1)}, u32[]{:S(2)}, u32[]{:S(2)}) %all-to-all-start) | async-done | bytes 393248 | tf_op jit(solution)/shard_map/all_to_all | solution.py:313
  22.1 0.1 fusion
  22.1 0.2 collective-permute-start.2
  22.3 0.0 collective-permute-start.3
  22.3 0.5 %collective-permute-start.4 = (bf16[128,128]{1,0:T(8,128)(2,1)S(1)}, bf16[128,128]{1,0:T(8,128)(2,1)S(1)}, u32[]{:S(2)}, u32[]{:S(2)}) collective-permute-start(bf16[128,128]{1,0:T(8,128)(2,1)S(1)} %slice.11), channel_id=1, source_target_pairs={{6,7},{7,6},{2,3},{3,2},{0,1},{1,0},{4,5},{5,4},{8,9},{9,8},{12,13... | collective-permute-start | bytes 98312 | tf_op jit(solution)/shard_map/ppermute | solution.py:321
  22.8 1.0 %early.1 = (f32[16,16]{1,0:T(8,128)S(1)}, bf16[3,64,1024]{2,1,0:T(8,128)(2,1)S(1)}) custom-call(bf16[16,96,128]{2,1,0:T(8,128)(2,1)S(1)} %all-to-all-done.sown, bf16[192,128]{1,0:T(8,128)(2,1)S(1)} %collective-permute-done.gown), custom_call_target="tpu_custom_call" | custom-call | tf_op jit(solution)/shard_map/early/pallas_call | solution.py:322
  23.9 0.0 collective-permute-done.4.gcore
  23.9 4.1 %collective-permute-done.2.schip = bf16[1024,128]{1,0:T(8,128)(2,1)S(1)} collective-permute-done((bf16[1024,128]{1,0:T(8,128)(2,1)S(1)}, bf16[1024,128]{1,0:T(8,128)(2,1)S(1)}, u32[]{:S(2)}, u32[]{:S(2)}) %collective-permute-start.2) | collective-permute-done | bytes 262176 | tf_op jit(solution)/shard_map/ppermute | solution.py:319
  28.0 0.0 collective-permute-done.3.score
  28.0 1.3 %products.1 = f32[16,16]{1,0:T(8,128)S(1)} custom-call(f32[16,16]{1,0:T(8,128)S(1)} %get-tuple-element.16.part_ref, bf16[3,64,1024]{2,1,0:T(8,128)(2,1)S(1)} %get-tuple-element.17.sides_ref, bf16[1024,128]{1,0:T(8,128)(2,1)S(1)} %collective-permute-done.2.schip, bf16[128,128]{1,0:T(8,128)(2,1)S(1)} %collective-permute-done.1.gchip, ...), custom_call_target="tpu_custom_call" | custom-call | tf_op jit(solution)/shard_map/products/pallas_call | solution.py:338
  29.3 9.5 %all_to_all.14 = f32[16,1,16]{2,1,0:T(1,128)S(1)} all-to-all(f32[16,1,16]{2,1,0:T(1,128)S(1)} %bitcast.14), channel_id=1, replica_groups=mesh['grp'=2,'blk'=16] {'blk'}, dimensions={0} | all-to-all | bytes 2048 | tf_op jit(solution)/shard_map/all_to_all | solution.py:351
  38.8 0.5 %reduce_sum.9 = f32[16]{0:T(128)} reduce(f32[16,1,16]{2,1,0:T(1,128)S(1)} %all_to_all.14, f32[]{:T(128)} %constant.0.clone.1), dimensions={0,1}, to_apply=%region_0.0 | reduce | flops 240 | bytes 1092 | tf_op jit(solution)/shard_map/reduce_sum | solution.py:352
  (1 shorter events, 0.0 us)
Async XLA Ops:
  2.0 20.1 %all-to-all-start = ((bf16[16,96,128]{2,1,0:T(8,128)(2,1)}), bf16[16,96,128]{2,1,0:T(8,128)(2,1)S(1)}, u32[]{:S(2)}, u32[]{:S(2)}) async-start(bf16[16,96,128]{2,1,0:T(8,128)(2,1)} %pack.1), calls=%async_computation | async-start | bytes 786432 | tf_op jit(solution)/shard_map/all_to_all | solution.py:313
  11.1 8.5 %collective-permute-start = (bf16[192,128]{1,0:T(8,128)(2,1)}, bf16[192,128]{1,0:T(8,128)(2,1)S(1)}, u32[]{:S(2)}, u32[]{:S(2)}) collective-permute-start(bf16[192,128]{1,0:T(8,128)(2,1)} %get-tuple-element.12), channel_id=1, source_target_pairs={{0,6},{1,7},{2,2},{3,3},{4,0},{5,1},{6,4},{7,5},{8,8},{9,9},{10,12... | collective-permute-start | bytes 147464 | tf_op jit(solution)/shard_map/ppermute | solution.py:312
  15.8 3.8 %collective-permute-start.1 = (bf16[128,128]{1,0:T(8,128)(2,1)}, bf16[128,128]{1,0:T(8,128)(2,1)S(1)}, u32[]{:S(2)}, u32[]{:S(2)}) collective-permute-start(bf16[128,128]{1,0:T(8,128)(2,1)} %get-tuple-element.13), channel_id=1, source_target_pairs={{0,11},{1,2},{2,7},{3,0},{4,3},{5,4},{6,1},{7,8},{8,5},{9,12},{10,... | collective-permute-start | bytes 98312 | tf_op jit(solution)/shard_map/ppermute | solution.py:311
  22.1 5.9 %collective-permute-start.2 = (bf16[1024,128]{1,0:T(8,128)(2,1)S(1)}, bf16[1024,128]{1,0:T(8,128)(2,1)S(1)}, u32[]{:S(2)}, u32[]{:S(2)}) collective-permute-start(bf16[1024,128]{1,0:T(8,128)(2,1)S(1)} %bitcast.17), channel_id=1, source_target_pairs={{6,11},{7,2},{2,7},{3,0},{0,3},{1,4},{4,1},{5,8},{8,5},{9,12},{12,... | collective-permute-start | bytes 786440 | tf_op jit(solution)/shard_map/ppermute | solution.py:319
  22.3 5.7 %collective-permute-start.3 = (bf16[1024,128]{1,0:T(8,128)(2,1)S(1)}, bf16[1024,128]{1,0:T(8,128)(2,1)S(1)}, u32[]{:S(2)}, u32[]{:S(2)}) collective-permute-start(bf16[1024,128]{1,0:T(8,128)(2,1)S(1)} %bitcast.16), channel_id=1, source_target_pairs={{6,7},{7,6},{2,3},{3,2},{0,1},{1,0},{4,5},{5,4},{8,9},{9,8},{12,13... | collective-permute-start | bytes 786440 | tf_op jit(solution)/shard_map/ppermute | solution.py:320
  22.3 1.6 %collective-permute-start.4 = (bf16[128,128]{1,0:T(8,128)(2,1)S(1)}, bf16[128,128]{1,0:T(8,128)(2,1)S(1)}, u32[]{:S(2)}, u32[]{:S(2)}) collective-permute-start(bf16[128,128]{1,0:T(8,128)(2,1)S(1)} %slice.11), channel_id=1, source_target_pairs={{6,7},{7,6},{2,3},{3,2},{0,1},{1,0},{4,5},{5,4},{8,9},{9,8},{12,13... | collective-permute-start | bytes 98312 | tf_op jit(solution)/shard_map/ppermute | solution.py:321

commit v16 on v15

--- a/solution.py
+++ b/solution.py
@@ -28,9 +28,10 @@
     blocks = x_ref.shape[1]
     copies = [pltpu.make_async_copy(x_hbm.at[a], x_ref.at[a], sems.at[a]) for a in range(3)]
     masks = pltpu.make_async_copy(imask_hbm, imask_ref, sems.at[3])
-    masks.start()
-    for copy in copies:
-        copy.start()
+    for a in (1, 0, 2):
+        copies[a].start()
+        if a == 1:
+            masks.start()
     diagonal = lax.broadcasted_iota(jnp.int32, (blocks, blocks), 0) == lax.broadcasted_iota(
         jnp.int32, (blocks, blocks), 1
     )

time: 39.7 us -> 39.6 us (level)
  no operation moved by 1% of the time
where the time goes in v16:
time: 39.6 us; the launch traced here: 39.2 us
  starting transfers between devices  14.7 us (37%)
  blocking collectives  9.49 us (24%)
  waiting for transfers between devices  8.48 us (21%)
  Pallas kernels  5.94 us (15%)
  other arithmetic  0.54 us (1%)
    all_to_all x1, blocking collectives, body(): mine = lax.all_to_all(part, 'blk', split_axis=0, concat_axis=0, tiled=True)  9.49 us
    all_to_all x1, starting transfers between devices, body(): own = lax.all_to_all(rows, 'blk', split_axis=0, concat_axis=0, tiled=True)  7.4 us
    ppermute x1, starting transfers between devices, body(): greens = lax.ppermute(greens, 'blk', list(enumerate(order)))  4.72 us
    ppermute x1, waiting for transfers between devices, body(): schip = lax.ppermute(to_chip, 'blk', chip_pairs)  4.12 us
    all_to_all x1, waiting for transfers between devices, body(): own = lax.all_to_all(rows, 'blk', split_axis=0, concat_axis=0, tiled=True)  2.42 us
    ppermute x1, waiting for transfers between devices, body(): gchip = lax.ppermute(gchip, 'blk', list(enumerate(chip_next)))  1.91 us
    pallas_call x1, Pallas kernels, body(): pl.pallas_call(functools.partial(pack_kernel, works_on), out_shape=jax.Sh...  1.9 us
    ppermute x1, starting transfers between devices, body(): gchip = lax.ppermute(gchip, 'blk', list(enumerate(chip_next)))  1.9 us
  transfers between devices with their start and end apart: 6, of which 3 were waited for; matrix products, arithmetic and copies ran while one was open for 0% of the time, Pallas kernels for 7%

profile of v16, /device:TPU:0, one launch (start us, length us, event | category | flops | bytes accessed | tf_op | source)
XLA Modules:
  0.0 39.2 jit_solution(15811255282284938460)
XLA Ops:
  0.0 1.9 %pack.1 = bf16[16,96,128]{2,1,0:T(8,128)(2,1)} custom-call(bf16[3,16,4096]{2,1,0:T(8,128)(2,1)} %bitcast.15, s32[3,16]{1,0:T(4,128)} %bitcast.20), custom_call_target="tpu_custom_call" | custom-call | tf_op jit(solution)/shard_map/pack/pallas_call | solution.py:285
  1.9 7.4 %all-to-all-start = ((bf16[16,96,128]{2,1,0:T(8,128)(2,1)}), bf16[16,96,128]{2,1,0:T(8,128)(2,1)S(1)}, u32[]{:S(2)}, u32[]{:S(2)}) async-start(bf16[16,96,128]{2,1,0:T(8,128)(2,1)} %pack.1), calls=%async_computation | async-start | bytes 786432 | tf_op jit(solution)/shard_map/all_to_all | solution.py:314
  9.3 1.7 %prep.1 = (bf16[192,128]{1,0:T(8,128)(2,1)}, bf16[128,128]{1,0:T(8,128)(2,1)}) custom-call(s32[3,16]{1,0:T(4,128)} %bitcast.21, s32[3,16]{1,0:T(4,128)} %bitcast.22, s32[16]{0:T(128)} %count.1, bf16[3,4096]{1,0:T(4,128)(2,1)} %bitcast.18, bf16[3,4096]{1,0:T(4,128)(2,1)} %bitcast.19), custom_call_target="tpu_custom_call" | custom-call | tf_op jit(solution)/shard_map/prep/pallas_call | solution.py:300
  11.0 4.7 %collective-permute-start = (bf16[192,128]{1,0:T(8,128)(2,1)}, bf16[192,128]{1,0:T(8,128)(2,1)S(1)}, u32[]{:S(2)}, u32[]{:S(2)}) collective-permute-start(bf16[192,128]{1,0:T(8,128)(2,1)} %get-tuple-element.12), channel_id=1, source_target_pairs={{0,6},{1,7},{2,2},{3,3},{4,0},{5,1},{6,4},{7,5},{8,8},{9,9},{10,12... | collective-permute-start | bytes 147464 | tf_op jit(solution)/shard_map/ppermute | solution.py:313
  15.8 1.9 %collective-permute-start.1 = (bf16[128,128]{1,0:T(8,128)(2,1)}, bf16[128,128]{1,0:T(8,128)(2,1)S(1)}, u32[]{:S(2)}, u32[]{:S(2)}) collective-permute-start(bf16[128,128]{1,0:T(8,128)(2,1)} %get-tuple-element.13), channel_id=1, source_target_pairs={{0,11},{1,2},{2,7},{3,0},{4,3},{5,4},{6,1},{7,8},{8,5},{9,12},{10,... | collective-permute-start | bytes 98312 | tf_op jit(solution)/shard_map/ppermute | solution.py:312
  17.6 1.9 %collective-permute-done.1.gchip = bf16[128,128]{1,0:T(8,128)(2,1)S(1)} collective-permute-done((bf16[128,128]{1,0:T(8,128)(2,1)}, bf16[128,128]{1,0:T(8,128)(2,1)S(1)}, u32[]{:S(2)}, u32[]{:S(2)}) %collective-permute-start.1) | collective-permute-done | bytes 32800 | tf_op jit(solution)/shard_map/ppermute | solution.py:312
  19.6 0.0 collective-permute-done.gown
  19.6 2.4 %all-to-all-done.sown = bf16[16,96,128]{2,1,0:T(8,128)(2,1)S(1)} async-done(((bf16[16,96,128]{2,1,0:T(8,128)(2,1)}), bf16[16,96,128]{2,1,0:T(8,128)(2,1)S(1)}, u32[]{:S(2)}, u32[]{:S(2)}) %all-to-all-start) | async-done | bytes 393248 | tf_op jit(solution)/shard_map/all_to_all | solution.py:314
  22.0 0.1 fusion
  22.1 0.2 collective-permute-start.2
  22.2 0.0 collective-permute-start.3
  22.2 0.5 %collective-permute-start.4 = (bf16[128,128]{1,0:T(8,128)(2,1)S(1)}, bf16[128,128]{1,0:T(8,128)(2,1)S(1)}, u32[]{:S(2)}, u32[]{:S(2)}) collective-permute-start(bf16[128,128]{1,0:T(8,128)(2,1)S(1)} %slice.11), channel_id=1, source_target_pairs={{6,7},{7,6},{2,3},{3,2},{0,1},{1,0},{4,5},{5,4},{8,9},{9,8},{12,13... | collective-permute-start | bytes 98312 | tf_op jit(solution)/shard_map/ppermute | solution.py:322
  22.7 1.0 %early.1 = (f32[16,16]{1,0:T(8,128)S(1)}, bf16[3,64,1024]{2,1,0:T(8,128)(2,1)S(1)}) custom-call(bf16[16,96,128]{2,1,0:T(8,128)(2,1)S(1)} %all-to-all-done.sown, bf16[192,128]{1,0:T(8,128)(2,1)S(1)} %collective-permute-done.gown), custom_call_target="tpu_custom_call" | custom-call | tf_op jit(solution)/shard_map/early/pallas_call | solution.py:323
  23.8 0.0 collective-permute-done.4.gcore
  23.8 4.1 %collective-permute-done.2.schip = bf16[1024,128]{1,0:T(8,128)(2,1)S(1)} collective-permute-done((bf16[1024,128]{1,0:T(8,128)(2,1)S(1)}, bf16[1024,128]{1,0:T(8,128)(2,1)S(1)}, u32[]{:S(2)}, u32[]{:S(2)}) %collective-permute-start.2) | collective-permute-done | bytes 262176 | tf_op jit(solution)/shard_map/ppermute | solution.py:320
  27.9 0.0 collective-permute-done.3.score
  27.9 1.3 %products.1 = f32[16,16]{1,0:T(8,128)S(1)} custom-call(f32[16,16]{1,0:T(8,128)S(1)} %get-tuple-element.16.part_ref, bf16[3,64,1024]{2,1,0:T(8,128)(2,1)S(1)} %get-tuple-element.17.sides_ref, bf16[1024,128]{1,0:T(8,128)(2,1)S(1)} %collective-permute-done.2.schip, bf16[128,128]{1,0:T(8,128)(2,1)S(1)} %collective-permute-done.1.gchip, ...), custom_call_target="tpu_custom_call" | custom-call | tf_op jit(solution)/shard_map/products/pallas_call | solution.py:339
  29.2 9.5 %all_to_all.14 = f32[16,1,16]{2,1,0:T(1,128)S(1)} all-to-all(f32[16,1,16]{2,1,0:T(1,128)S(1)} %bitcast.14), channel_id=1, replica_groups=mesh['grp'=2,'blk'=16] {'blk'}, dimensions={0} | all-to-all | bytes 2048 | tf_op jit(solution)/shard_map/all_to_all | solution.py:352
  38.7 0.5 %reduce_sum.9 = f32[16]{0:T(128)} reduce(f32[16,1,16]{2,1,0:T(1,128)S(1)} %all_to_all.14, f32[]{:T(128)} %constant.0.clone.1), dimensions={0,1}, to_apply=%region_0.0 | reduce | flops 240 | bytes 1092 | tf_op jit(solution)/shard_map/reduce_sum | solution.py:353
  (1 shorter events, 0.0 us)
Async XLA Ops:
  1.9 20.1 %all-to-all-start = ((bf16[16,96,128]{2,1,0:T(8,128)(2,1)}), bf16[16,96,128]{2,1,0:T(8,128)(2,1)S(1)}, u32[]{:S(2)}, u32[]{:S(2)}) async-start(bf16[16,96,128]{2,1,0:T(8,128)(2,1)} %pack.1), calls=%async_computation | async-start | bytes 786432 | tf_op jit(solution)/shard_map/all_to_all | solution.py:314
  11.0 8.5 %collective-permute-start = (bf16[192,128]{1,0:T(8,128)(2,1)}, bf16[192,128]{1,0:T(8,128)(2,1)S(1)}, u32[]{:S(2)}, u32[]{:S(2)}) collective-permute-start(bf16[192,128]{1,0:T(8,128)(2,1)} %get-tuple-element.12), channel_id=1, source_target_pairs={{0,6},{1,7},{2,2},{3,3},{4,0},{5,1},{6,4},{7,5},{8,8},{9,9},{10,12... | collective-permute-start | bytes 147464 | tf_op jit(solution)/shard_map/ppermute | solution.py:313
  15.8 3.8 %collective-permute-start.1 = (bf16[128,128]{1,0:T(8,128)(2,1)}, bf16[128,128]{1,0:T(8,128)(2,1)S(1)}, u32[]{:S(2)}, u32[]{:S(2)}) collective-permute-start(bf16[128,128]{1,0:T(8,128)(2,1)} %get-tuple-element.13), channel_id=1, source_target_pairs={{0,11},{1,2},{2,7},{3,0},{4,3},{5,4},{6,1},{7,8},{8,5},{9,12},{10,... | collective-permute-start | bytes 98312 | tf_op jit(solution)/shard_map/ppermute | solution.py:312
  22.1 5.9 %collective-permute-start.2 = (bf16[1024,128]{1,0:T(8,128)(2,1)S(1)}, bf16[1024,128]{1,0:T(8,128)(2,1)S(1)}, u32[]{:S(2)}, u32[]{:S(2)}) collective-permute-start(bf16[1024,128]{1,0:T(8,128)(2,1)S(1)} %bitcast.17), channel_id=1, source_target_pairs={{6,11},{7,2},{2,7},{3,0},{0,3},{1,4},{4,1},{5,8},{8,5},{9,12},{12,... | collective-permute-start | bytes 786440 | tf_op jit(solution)/shard_map/ppermute | solution.py:320
  22.2 5.7 %collective-permute-start.3 = (bf16[1024,128]{1,0:T(8,128)(2,1)S(1)}, bf16[1024,128]{1,0:T(8,128)(2,1)S(1)}, u32[]{:S(2)}, u32[]{:S(2)}) collective-permute-start(bf16[1024,128]{1,0:T(8,128)(2,1)S(1)} %bitcast.16), channel_id=1, source_target_pairs={{6,7},{7,6},{2,3},{3,2},{0,1},{1,0},{4,5},{5,4},{8,9},{9,8},{12,13... | collective-permute-start | bytes 786440 | tf_op jit(solution)/shard_map/ppermute | solution.py:321
  22.2 1.6 %collective-permute-start.4 = (bf16[128,128]{1,0:T(8,128)(2,1)S(1)}, bf16[128,128]{1,0:T(8,128)(2,1)S(1)}, u32[]{:S(2)}, u32[]{:S(2)}) collective-permute-start(bf16[128,128]{1,0:T(8,128)(2,1)S(1)} %slice.11), channel_id=1, source_target_pairs={{6,7},{7,6},{2,3},{3,2},{0,1},{1,0},{4,5},{5,4},{8,9},{9,8},{12,13... | collective-permute-start | bytes 98312 | tf_op jit(solution)/shard_map/ppermute | solution.py:322

commit v17 on v15

--- a/solution.py
+++ b/solution.py
@@ -26,11 +26,21 @@
 
 def pack_kernel(works_on, x_hbm, imask_hbm, out_hbm, x_ref, imask_ref, rows_ref, out_ref, sems):
     blocks = x_ref.shape[1]
-    copies = [pltpu.make_async_copy(x_hbm.at[a], x_ref.at[a], sems.at[a]) for a in range(3)]
+    cut = HALF // 2 * LANES
+    copies = [
+        [
+            pltpu.make_async_copy(
+                x_hbm.at[a, :, pl.ds(k * cut, cut)], x_ref.at[a, :, pl.ds(k * cut, cut)], sems.at[7 + 2 * a + k]
+            )
+            for k in range(2)
+        ]
+        for a in range(3)
+    ]
     masks = pltpu.make_async_copy(imask_hbm, imask_ref, sems.at[3])
     masks.start()
-    for copy in copies:
-        copy.start()
+    for a in (1, 0, 2):
+        for copy in copies[a]:
+            copy.start()
     diagonal = lax.broadcasted_iota(jnp.int32, (blocks, blocks), 0) == lax.broadcasted_iota(
         jnp.int32, (blocks, blocks), 1
     )
@@ -39,8 +49,9 @@
     for a in (1, 0, 2):
         mask = jnp.where(diagonal, imask_ref[pl.ds(a, 1), :].astype(jnp.float32), 0.0)
         mask = jnp.broadcast_to(jnp.sum(mask, axis=1, keepdims=True), (blocks, LANES))
-        copies[a].wait()
         for c in range(HALF):
+            if c % (HALF // 2) == 0:
+                copies[a][c // (HALF // 2)].wait()
             rows_ref[a, pl.ds(c, blocks, stride=PITCH), :] = (
                 x_ref[a, :, c * LANES : (c + 1) * LANES].astype(jnp.float32) * mask
             )
@@ -291,7 +302,7 @@
             pltpu.VMEM((3, total), jnp.int32),
             pltpu.VMEM((3, total * PITCH, LANES), jnp.float32),
             pltpu.VMEM((members, 3 * HALF, LANES), jnp.bfloat16),
-            pltpu.SemaphoreType.DMA((7,)),
+            pltpu.SemaphoreType.DMA((13,)),
         ],
         compiler_params=pltpu.CompilerParams(vmem_limit_bytes=63 * 1024 * 1024),
         name="pack",

time: 39.7 us -> 39.7 us (level)
  no operation moved by 1% of the time
where the time goes in v17:
time: 39.7 us; the launch traced here: 39.3 us
  starting transfers between devices  14.7 us (37%)
  blocking collectives  9.49 us (24%)
  waiting for transfers between devices  8.48 us (21%)
  Pallas kernels  6.02 us (15%)
  other arithmetic  0.54 us (1%)
    all_to_all x1, blocking collectives, body(): mine = lax.all_to_all(part, 'blk', split_axis=0, concat_axis=0, tiled=True)  9.49 us
    all_to_all x1, starting transfers between devices, body(): own = lax.all_to_all(rows, 'blk', split_axis=0, concat_axis=0, tiled=True)  7.4 us
    ppermute x1, starting transfers between devices, body(): greens = lax.ppermute(greens, 'blk', list(enumerate(order)))  4.72 us
    ppermute x1, waiting for transfers between devices, body(): schip = lax.ppermute(to_chip, 'blk', chip_pairs)  4.12 us
    all_to_all x1, waiting for transfers between devices, body(): own = lax.all_to_all(rows, 'blk', split_axis=0, concat_axis=0, tiled=True)  2.42 us
    pallas_call x1, Pallas kernels, body(): pl.pallas_call(functools.partial(pack_kernel, works_on), out_shape=jax.Sh...  1.99 us
    ppermute x1, waiting for transfers between devices, body(): gchip = lax.ppermute(gchip, 'blk', list(enumerate(chip_next)))  1.91 us
    ppermute x1, starting transfers between devices, body(): gchip = lax.ppermute(gchip, 'blk', list(enumerate(chip_next)))  1.9 us
  transfers between devices with their start and end apart: 6, of which 3 were waited for; matrix products, arithmetic and copies ran while one was open for 0% of the time, Pallas kernels for 7%

profile of v17, /device:TPU:0, one launch (start us, length us, event | category | flops | bytes accessed | tf_op | source)
XLA Modules:
  0.0 39.3 jit_solution(12396703543968254893)
XLA Ops:
  0.0 2.0 %pack.1 = bf16[16,96,128]{2,1,0:T(8,128)(2,1)} custom-call(bf16[3,16,4096]{2,1,0:T(8,128)(2,1)} %bitcast.15, s32[3,16]{1,0:T(4,128)} %bitcast.20), custom_call_target="tpu_custom_call" | custom-call | tf_op jit(solution)/shard_map/pack/pallas_call | solution.py:295
  2.0 7.4 %all-to-all-start = ((bf16[16,96,128]{2,1,0:T(8,128)(2,1)}), bf16[16,96,128]{2,1,0:T(8,128)(2,1)S(1)}, u32[]{:S(2)}, u32[]{:S(2)}) async-start(bf16[16,96,128]{2,1,0:T(8,128)(2,1)} %pack.1), calls=%async_computation | async-start | bytes 786432 | tf_op jit(solution)/shard_map/all_to_all | solution.py:324
  9.4 1.7 %prep.1 = (bf16[192,128]{1,0:T(8,128)(2,1)}, bf16[128,128]{1,0:T(8,128)(2,1)}) custom-call(s32[3,16]{1,0:T(4,128)} %bitcast.21, s32[3,16]{1,0:T(4,128)} %bitcast.22, s32[16]{0:T(128)} %count.1, bf16[3,4096]{1,0:T(4,128)(2,1)} %bitcast.18, bf16[3,4096]{1,0:T(4,128)(2,1)} %bitcast.19), custom_call_target="tpu_custom_call" | custom-call | tf_op jit(solution)/shard_map/prep/pallas_call | solution.py:310
  11.1 4.7 %collective-permute-start = (bf16[192,128]{1,0:T(8,128)(2,1)}, bf16[192,128]{1,0:T(8,128)(2,1)S(1)}, u32[]{:S(2)}, u32[]{:S(2)}) collective-permute-start(bf16[192,128]{1,0:T(8,128)(2,1)} %get-tuple-element.12), channel_id=1, source_target_pairs={{0,6},{1,7},{2,2},{3,3},{4,0},{5,1},{6,4},{7,5},{8,8},{9,9},{10,12... | collective-permute-start | bytes 147464 | tf_op jit(solution)/shard_map/ppermute | solution.py:323
  15.8 1.9 %collective-permute-start.1 = (bf16[128,128]{1,0:T(8,128)(2,1)}, bf16[128,128]{1,0:T(8,128)(2,1)S(1)}, u32[]{:S(2)}, u32[]{:S(2)}) collective-permute-start(bf16[128,128]{1,0:T(8,128)(2,1)} %get-tuple-element.13), channel_id=1, source_target_pairs={{0,11},{1,2},{2,7},{3,0},{4,3},{5,4},{6,1},{7,8},{8,5},{9,12},{10,... | collective-permute-start | bytes 98312 | tf_op jit(solution)/shard_map/ppermute | solution.py:322
  17.7 1.9 %collective-permute-done.1.gchip = bf16[128,128]{1,0:T(8,128)(2,1)S(1)} collective-permute-done((bf16[128,128]{1,0:T(8,128)(2,1)}, bf16[128,128]{1,0:T(8,128)(2,1)S(1)}, u32[]{:S(2)}, u32[]{:S(2)}) %collective-permute-start.1) | collective-permute-done | bytes 32800 | tf_op jit(solution)/shard_map/ppermute | solution.py:322
  19.6 0.0 collective-permute-done.gown
  19.6 2.4 %all-to-all-done.sown = bf16[16,96,128]{2,1,0:T(8,128)(2,1)S(1)} async-done(((bf16[16,96,128]{2,1,0:T(8,128)(2,1)}), bf16[16,96,128]{2,1,0:T(8,128)(2,1)S(1)}, u32[]{:S(2)}, u32[]{:S(2)}) %all-to-all-start) | async-done | bytes 393248 | tf_op jit(solution)/shard_map/all_to_all | solution.py:324
  22.1 0.1 fusion
  22.1 0.2 collective-permute-start.2
  22.3 0.0 collective-permute-start.3
  22.3 0.5 %collective-permute-start.4 = (bf16[128,128]{1,0:T(8,128)(2,1)S(1)}, bf16[128,128]{1,0:T(8,128)(2,1)S(1)}, u32[]{:S(2)}, u32[]{:S(2)}) collective-permute-start(bf16[128,128]{1,0:T(8,128)(2,1)S(1)} %slice.11), channel_id=1, source_target_pairs={{6,7},{7,6},{2,3},{3,2},{0,1},{1,0},{4,5},{5,4},{8,9},{9,8},{12,13... | collective-permute-start | bytes 98312 | tf_op jit(solution)/shard_map/ppermute | solution.py:332
  22.8 1.1 %early.1 = (f32[16,16]{1,0:T(8,128)S(1)}, bf16[3,64,1024]{2,1,0:T(8,128)(2,1)S(1)}) custom-call(bf16[16,96,128]{2,1,0:T(8,128)(2,1)S(1)} %all-to-all-done.sown, bf16[192,128]{1,0:T(8,128)(2,1)S(1)} %collective-permute-done.gown), custom_call_target="tpu_custom_call" | custom-call | tf_op jit(solution)/shard_map/early/pallas_call | solution.py:333
  23.9 0.0 collective-permute-done.4.gcore
  23.9 4.1 %collective-permute-done.2.schip = bf16[1024,128]{1,0:T(8,128)(2,1)S(1)} collective-permute-done((bf16[1024,128]{1,0:T(8,128)(2,1)S(1)}, bf16[1024,128]{1,0:T(8,128)(2,1)S(1)}, u32[]{:S(2)}, u32[]{:S(2)}) %collective-permute-start.2) | collective-permute-done | bytes 262176 | tf_op jit(solution)/shard_map/ppermute | solution.py:330
  28.0 0.0 collective-permute-done.3.score
  28.0 1.3 %products.1 = f32[16,16]{1,0:T(8,128)S(1)} custom-call(f32[16,16]{1,0:T(8,128)S(1)} %get-tuple-element.16.part_ref, bf16[3,64,1024]{2,1,0:T(8,128)(2,1)S(1)} %get-tuple-element.17.sides_ref, bf16[1024,128]{1,0:T(8,128)(2,1)S(1)} %collective-permute-done.2.schip, bf16[128,128]{1,0:T(8,128)(2,1)S(1)} %collective-permute-done.1.gchip, ...), custom_call_target="tpu_custom_call" | custom-call | tf_op jit(solution)/shard_map/products/pallas_call | solution.py:349
  29.3 9.5 %all_to_all.14 = f32[16,1,16]{2,1,0:T(1,128)S(1)} all-to-all(f32[16,1,16]{2,1,0:T(1,128)S(1)} %bitcast.14), channel_id=1, replica_groups=mesh['grp'=2,'blk'=16] {'blk'}, dimensions={0} | all-to-all | bytes 2048 | tf_op jit(solution)/shard_map/all_to_all | solution.py:362
  38.8 0.5 %reduce_sum.9 = f32[16]{0:T(128)} reduce(f32[16,1,16]{2,1,0:T(1,128)S(1)} %all_to_all.14, f32[]{:T(128)} %constant.0.clone.1), dimensions={0,1}, to_apply=%region_0.0 | reduce | flops 240 | bytes 1092 | tf_op jit(solution)/shard_map/reduce_sum | solution.py:363
  (1 shorter events, 0.0 us)
Async XLA Ops:
  2.0 20.1 %all-to-all-start = ((bf16[16,96,128]{2,1,0:T(8,128)(2,1)}), bf16[16,96,128]{2,1,0:T(8,128)(2,1)S(1)}, u32[]{:S(2)}, u32[]{:S(2)}) async-start(bf16[16,96,128]{2,1,0:T(8,128)(2,1)} %pack.1), calls=%async_computation | async-start | bytes 786432 | tf_op jit(solution)/shard_map/all_to_all | solution.py:324
  11.1 8.5 %collective-permute-start = (bf16[192,128]{1,0:T(8,128)(2,1)}, bf16[192,128]{1,0:T(8,128)(2,1)S(1)}, u32[]{:S(2)}, u32[]{:S(2)}) collective-permute-start(bf16[192,128]{1,0:T(8,128)(2,1)} %get-tuple-element.12), channel_id=1, source_target_pairs={{0,6},{1,7},{2,2},{3,3},{4,0},{5,1},{6,4},{7,5},{8,8},{9,9},{10,12... | collective-permute-start | bytes 147464 | tf_op jit(solution)/shard_map/ppermute | solution.py:323
  15.8 3.8 %collective-permute-start.1 = (bf16[128,128]{1,0:T(8,128)(2,1)}, bf16[128,128]{1,0:T(8,128)(2,1)S(1)}, u32[]{:S(2)}, u32[]{:S(2)}) collective-permute-start(bf16[128,128]{1,0:T(8,128)(2,1)} %get-tuple-element.13), channel_id=1, source_target_pairs={{0,11},{1,2},{2,7},{3,0},{4,3},{5,4},{6,1},{7,8},{8,5},{9,12},{10,... | collective-permute-start | bytes 98312 | tf_op jit(solution)/shard_map/ppermute | solution.py:322
  22.1 5.9 %collective-permute-start.2 = (bf16[1024,128]{1,0:T(8,128)(2,1)S(1)}, bf16[1024,128]{1,0:T(8,128)(2,1)S(1)}, u32[]{:S(2)}, u32[]{:S(2)}) collective-permute-start(bf16[1024,128]{1,0:T(8,128)(2,1)S(1)} %bitcast.17), channel_id=1, source_target_pairs={{6,11},{7,2},{2,7},{3,0},{0,3},{1,4},{4,1},{5,8},{8,5},{9,12},{12,... | collective-permute-start | bytes 786440 | tf_op jit(solution)/shard_map/ppermute | solution.py:330
  22.3 5.7 %collective-permute-start.3 = (bf16[1024,128]{1,0:T(8,128)(2,1)S(1)}, bf16[1024,128]{1,0:T(8,128)(2,1)S(1)}, u32[]{:S(2)}, u32[]{:S(2)}) collective-permute-start(bf16[1024,128]{1,0:T(8,128)(2,1)S(1)} %bitcast.16), channel_id=1, source_target_pairs={{6,7},{7,6},{2,3},{3,2},{0,1},{1,0},{4,5},{5,4},{8,9},{9,8},{12,13... | collective-permute-start | bytes 786440 | tf_op jit(solution)/shard_map/ppermute | solution.py:331
  22.3 1.6 %collective-permute-start.4 = (bf16[128,128]{1,0:T(8,128)(2,1)S(1)}, bf16[128,128]{1,0:T(8,128)(2,1)S(1)}, u32[]{:S(2)}, u32[]{:S(2)}) collective-permute-start(bf16[128,128]{1,0:T(8,128)(2,1)S(1)} %slice.11), channel_id=1, source_target_pairs={{6,7},{7,6},{2,3},{3,2},{0,1},{1,0},{4,5},{5,4},{8,9},{9,8},{12,13... | collective-permute-start | bytes 98312 | tf_op jit(solution)/shard_map/ppermute | solution.py:332
